TPU v7x, 32 devices: a whole 2x2x4 slice. The times are simulated.
32 devices in a mesh: row: 8 (over y, x, core), col: 4 (over z).
Axes of the slice: x: 2, y: 2, z: 4, core: 2. Of those that a mesh axis runs over, the one named last changes fastest.
Arguments:
- item_factors: bfloat16 [16, 2048, 256], P('col', 'row'), may hold values from -1 to 1
- tile_counts: int32 [16], P('col'), may hold values from 1024 to 2048, as said below
- observed_tiles: int32 [8, 8], P('row', 'col'), may hold values from 0 to 3, as said below
- mask_words: int32 [1024, 8, 256], P('row', 'col'), may hold values from 0 to 255
- confidence: float32 [1024], P('row'), may hold values from 1 to 40
- previous: bfloat16 [1024, 256], P('row'), may hold values from -6 to 6
Outputs:
- user_factors: float32 [1024, 256], P('row')
Inputs may be any that keep to these rules, and one draw needn't show every extreme that they name: `tile_counts`: a tile's slots at and past its count are padding; some tile of the draw has all 2048 slots valid. `observed_tiles`: the 2 entries of one user block and one column group are distinct.
All inputs are finite; a program needn't handle non-finite values.
Results may differ from a plain program's by a relative error of at most 0.0013.
The roundings to bfloat16 on the way count: a program that leaves them out, or rounds other values in their place, can miss the bound.
Values may be sent and summed in bfloat16 or wider, within the bound.
No kernel may reach another device: no remote copies, remote signals or barrier semaphores. Data moves between devices by JAX's collectives and lax.ppermute only.
A program may use at most 64 MiB of HBM per device.

v0:
```python
import jax
import jax.numpy as jnp
from jax import lax
from jax.sharding import PartitionSpec as P

R = 256
OBS = 2
ITERS = 3


ridge_weight = 0.1


def unpack_bits(words):
    shifts = jnp.arange(8, dtype=jnp.int32)
    bits = jnp.right_shift(words[..., None], shifts) & 1
    return bits.reshape(words.shape[:-1] + (words.shape[-1] * 8,))


def local(item_factors, tile_counts, observed_tiles, mask_words, confidence, previous):
    tiles = lax.all_gather(item_factors, "row", axis=1, tiled=True)
    tile_len = tiles.shape[1]
    valid = jnp.arange(tile_len, dtype=jnp.int32)[None, :] < tile_counts[:, None]
    masked = jnp.where(valid[..., None], tiles, jnp.zeros_like(tiles)).reshape(-1, R)
    gram = lax.psum(
        jnp.einsum("jr,js->rs", masked, masked, preferred_element_type=jnp.float32), "col"
    )
    picked = observed_tiles[0]
    slot_tiles = tiles[picked]
    seen = (unpack_bits(mask_words) * valid[picked][None].astype(jnp.int32)).astype(jnp.bfloat16)
    seen = jnp.transpose(seen, (1, 0, 2))
    users = previous.shape[0]

    def weighted(rounded):
        total = jnp.zeros((users, R), jnp.float32)
        for slot in range(OBS):
            scores = jnp.einsum(
                "ur,jr->uj", rounded, slot_tiles[slot], preferred_element_type=jnp.float32
            )
            weights = (confidence[:, None] * seen[slot].astype(jnp.float32) * scores).astype(
                jnp.bfloat16
            )
            total = total + jnp.dot(weights, slot_tiles[slot], preferred_element_type=jnp.float32)
        return total

    rhs_part = jnp.zeros((users, R), jnp.float32)
    for slot in range(OBS):
        rhs_part = rhs_part + jnp.dot(
            seen[slot], slot_tiles[slot], preferred_element_type=jnp.float32
        )

    def local_op(vector, summed):
        return (
            jnp.dot(vector, gram, precision=lax.Precision.HIGHEST) + ridge_weight * vector + summed
        )

    def reduce_terms(parts):
        return lax.psum(parts, "col")

    solution = previous.astype(jnp.float32)
    rhs_sum, start_sum = reduce_terms((rhs_part, weighted(previous)))
    rhs = (1.0 + confidence)[:, None] * rhs_sum
    residual = rhs - local_op(solution, start_sum)
    direction = residual
    norm_now = jnp.sum(residual * residual, axis=1)
    for iteration in range(ITERS):
        image = local_op(direction, reduce_terms((weighted(direction.astype(jnp.bfloat16)),))[0])
        step_size = norm_now / jnp.sum(direction * image, axis=1)
        solution = solution + step_size[:, None] * direction
        residual = residual - step_size[:, None] * image
        norm_next = jnp.sum(residual * residual, axis=1)
        direction = residual + (norm_next / norm_now)[:, None] * direction
        norm_now = norm_next
    return solution


def solution(mesh):
    return jax.shard_map(
        local,
        mesh=mesh,
        in_specs=(
            P("col", "row", None),
            P("col"),
            P("row", "col"),
            P("row", "col", None),
            P("row"),
            P("row", None),
        ),
        out_specs=P("row", None),
        check_vma=False,
    )
```

profile of v0, /device:TPU:0, one launch (start us, length us, event | category | flops | bytes accessed | tf_op | source)
XLA Modules:
  0.0 231.7 jit_solution(6853995396478709208)
XLA Ops:
  8.0 0.7 iota_compare_fusion
  9.4 1.1 copy.10
  10.5 1.2 fusion.40
  11.8 36.9 %all-gather.2.cloned.1.call-done = bf16[4,2048,256]{2,1,0:T(8,128)(2,1)} async-done(((bf16[4,256,256]{2,1,0:T(8,128)(2,1)}), bf16[4,2048,256]{2,1,0:T(8,128)(2,1)}) %all-gather.2.cloned.1.call-update) | async-done | bytes 4194320 | tf_op jit(solution)/shard_map/all_gather | solution.py:21
  48.7 2.9 %gather_fusion.1 = bf16[2,2048,256]{2,1,0:T(8,128)(2,1)S(1)} fusion(bf16[4,2048,256]{2,1,0:T(8,128)(2,1)} %all-gather.2.cloned.1.call-done, s32[1024]{0:T(1024)S(1)} %pad_clamp_fusion), kind=kCustom, calls=%fused_computation.1 | custom fusion | bytes 4194312 | tf_op jit(solution)/shard_map/gather | solution.py:29
  52.0 1.5 fusion.17
  53.4 2.4 %fusion.38 = f32[128,256]{1,0:T(8,128)} fusion(f32[128,256]{1,0:T(8,128)} %fusion.17, bf16[128,256]{1,0:T(8,128)(2,1)S(1)} %copy-done.2, bf16[2,2048,256]{2,1,0:T(8,128)(2,1)S(1)} %gather_fusion.1, f32[128]{0:T(128)S(1)} %copy-done.4, bf16[2,128,2048]{1,2,0:T(8,128)(2,1)S(1)} %fusion.40), kind=kOutput, calls=%fused_computation.51 | convolution fusion | flops 269516800 | bytes 2949632 | tf_op jit(solution)/shard_map/dot_general | solution.py:43
  55.8 1.0 convolution_add_fusion.3
  56.8 7.2 %fusion.25 = f32[256,256]{1,0:T(8,128)} fusion(bf16[4,2048,256]{2,1,0:T(8,128)(2,1)} %all-gather.2.cloned.1.call-done, pred[4,2048]{1,0:T(4,128)(4,1)S(1)} %iota_compare_fusion), kind=kOutput, calls=%fused_computation.36 | convolution fusion | flops 1075838976 | bytes 4464640 | tf_op jit(solution)/shard_map/jr,js->rs/dot_general | solution.py:26
  64.1 38.9 %all-reduce.12.cloned.1.call-done = (f32[128,256]{1,0:T(8,128)}, f32[256,256]{1,0:T(8,128)}, f32[128,256]{1,0:T(8,128)}) async-done(((f32[128,256]{1,0:T(8,128)}, f32[256,256]{1,0:T(8,128)}, f32[128,256]{1,0:T(8,128)}), (f32[128,256]{1,0:T(8,128)}, f32[256,256]{1,0:T(8,128)}, f32[128,256]{1,0:T(8,128)})) %all-reduce.12.cloned.1.call-update) | async-done | bytes 524304 | tf_op jit(solution)/shard_map/psum | solution.py:58
  103.0 1.3 fusion.34
  104.3 1.5 fusion.23
  105.8 2.4 %fusion.35 = f32[128,256]{1,0:T(8,128)} fusion(f32[128,256]{1,0:T(8,128)} %fusion.23, bf16[2,2048,256]{2,1,0:T(8,128)(2,1)S(1)} %gather_fusion.1, f32[128]{0:T(128)S(1)} %copy-done.4, bf16[2,128,2048]{1,2,0:T(8,128)(2,1)S(1)} %fusion.40, f32[128,256]{1,0:T(8,128)S(1)} %fusion.34), kind=kOutput, calls=%fused_computation.48 | convolution fusion | flops 269549568 | bytes 3015168 | tf_op jit(solution)/shard_map/dot_general | solution.py:43
  108.3 34.2 %all-reduce.6.cloned.1.call-done = f32[128,256]{1,0:T(8,128)} async-done(((f32[128,256]{1,0:T(8,128)}), f32[128,256]{1,0:T(8,128)}) %all-reduce.6.cloned.1.call-update) | async-done | bytes 131088 | tf_op jit(solution)/shard_map/psum | solution.py:58
  142.5 1.3 multiply_reduce_fusion.3
  144.1 1.9 fusion.21
  145.9 2.5 %fusion.36 = f32[128,256]{1,0:T(8,128)} fusion(f32[128,256]{1,0:T(8,128)S(1)} %fusion.21, bf16[2,2048,256]{2,1,0:T(8,128)(2,1)S(1)} %gather_fusion.1, f32[128]{0:T(128)S(1)} %copy-done.4, bf16[2,128,2048]{1,2,0:T(8,128)(2,1)} %copy-done.1, f32[128,256]{1,0:T(8,128)S(1)} %multiply_add_fusion.1), kind=kOutput, calls=%fused_computation.49 | convolution fusion | flops 269549568 | bytes 3015168 | tf_op jit(solution)/shard_map/dot_general | solution.py:43
  148.5 34.3 %all-reduce.8.cloned.1.call-done = f32[128,256]{1,0:T(8,128)} async-done(((f32[128,256]{1,0:T(8,128)}), f32[128,256]{1,0:T(8,128)}) %all-reduce.8.cloned.1.call-update) | async-done | bytes 131088 | tf_op jit(solution)/shard_map/psum | solution.py:58
  182.8 1.3 multiply_reduce_fusion.1
  184.4 1.9 fusion.19
  186.3 2.5 %fusion.37 = f32[128,256]{1,0:T(8,128)} fusion(f32[128,256]{1,0:T(8,128)S(1)} %fusion.19, bf16[2,2048,256]{2,1,0:T(8,128)(2,1)S(1)} %gather_fusion.1, f32[128]{0:T(128)S(1)} %copy-done.4, bf16[2,128,2048]{1,2,0:T(8,128)(2,1)} %copy-done.1, f32[128,256]{1,0:T(8,128)S(1)} %multiply_add_fusion), kind=kOutput, calls=%fused_computation.50 | convolution fusion | flops 269549568 | bytes 3015168 | tf_op jit(solution)/shard_map/dot_general | solution.py:43
  188.9 34.2 %all-reduce.10.cloned.1.call-done = f32[128,256]{1,0:T(8,128)} async-done(((f32[128,256]{1,0:T(8,128)}), f32[128,256]{1,0:T(8,128)}) %all-reduce.10.cloned.1.call-update) | async-done | bytes 131088 | tf_op jit(solution)/shard_map/psum | solution.py:58
  223.1 1.3 fusion.39
  224.4 0.8 fusion.51
  (37 shorter events, 3.3 us)
Async XLA Ops:
  6.5 42.2 %all-gather.2.cloned.1.call-start = ((), (), s32[]{:S(2)}) async-start(), calls=%async_computation | async-start | bytes 4718592 | tf_op jit(solution)/shard_map/all_gather | solution.py:21
  7.3 95.7 %all-reduce.12.cloned.1.call-start = ((), (), s32[]{:S(2)}) async-start(), calls=%async_computation.4 | async-start | bytes 1048576 | tf_op jit(solution)/shard_map/psum | solution.py:58
  11.8 94.0 %copy-start.1 = (bf16[2,128,2048]{1,2,0:T(8,128)(2,1)}, bf16[2,128,2048]{1,2,0:T(8,128)(2,1)S(1)}, u32[]{:S(2)}) copy-start(bf16[2,128,2048]{1,2,0:T(8,128)(2,1)S(1)} %fusion.40) | copy-start | bytes 3145732
  11.8 40.2 %copy-start.2 = (bf16[128,256]{1,0:T(8,128)(2,1)S(1)}, bf16[128,256]{1,0:T(8,128)(2,1)}, u32[]{:S(2)}) copy-start(bf16[128,256]{1,0:T(8,128)(2,1)} %param.11) | copy-start | bytes 196612
  11.8 40.2 %copy-start.4 = (f32[128]{0:T(128)S(1)}, f32[128]{0:T(128)}, u32[]{:S(2)}) copy-start(f32[128]{0:T(128)} %param.10) | copy-start | bytes 1540
  64.1 78.4 %all-reduce.6.cloned.1.call-start = ((), (), s32[]{:S(2)}) async-start(), calls=%async_computation.1 | async-start | bytes 262144 | tf_op jit(solution)/shard_map/psum | solution.py:58
  105.8 36.7 %copy-start = (f32[256,256]{1,0:T(8,128)S(1)}, f32[256,256]{1,0:T(8,128)}, u32[]{:S(2)}) copy-start(f32[256,256]{1,0:T(8,128)} %get-tuple-element.8) | copy-start | bytes 786436
  108.2 74.6 %all-reduce.8.cloned.1.call-start = ((), (), s32[]{:S(2)}) async-start(), calls=%async_computation.2 | async-start | bytes 262144 | tf_op jit(solution)/shard_map/psum | solution.py:58
  148.5 74.6 %all-reduce.10.cloned.1.call-start = ((), (), s32[]{:S(2)}) async-start(), calls=%async_computation.3 | async-start | bytes 262144 | tf_op jit(solution)/shard_map/psum | solution.py:58
  186.3 38.1 %copy-start.3 = (bf16[128,256]{1,0:T(8,128)(2,1)S(1)}, bf16[128,256]{1,0:T(8,128)(2,1)}, u32[]{:S(2)}) copy-start(bf16[128,256]{1,0:T(8,128)(2,1)} %param.11) | copy-start | bytes 196612
Sparse Core Ops, SparseCore 0:
  9.3 39.4 all-gather.1
  64.2 38.7 all-reduce.11
  108.3 34.1 all-reduce.5
  148.6 34.1 all-reduce.7
  189.0 34.0 all-reduce.9
where the time goes:
time: 232 us
  waiting for transfers between devices  179 us (77%)
  matrix products  30.2 us (13%)
  between operations  13.3 us (6%)
  local copies, waits for them, and re-layouts  4.66 us (2%)
  other arithmetic  4.04 us (2%)
    psum x4, waiting for transfers between devices, reduce_terms(): return lax.psum(parts, 'col')  142 us
    all_gather x1, waiting for transfers between devices, local(): tiles = lax.all_gather(item_factors, 'row', axis=1, tiled=True)  36.9 us
    dot_general x8, matrix products, weighted(): jnp.dot(weights, slot_tiles[slot], preferred_element_type=jnp.float32)  16.5 us
    dot_general x1, matrix products, local(): jnp.einsum('jr,js->rs', masked, masked, preferred_element_type=jnp.float32)  7.22 us
    dot_general x4, matrix products, local_op(): jnp.dot(vector, gram, precision=lax.Precision.HIGHEST)  5.09 us
  transfers between devices with their start and end apart: 5, of which 5 were waited for; matrix products, arithmetic and copies ran while one was open for 2% of the time, Pallas kernels for 0%

commit v1 on v0

v1 whole, which is shorter than its diff:
```python
import functools

import jax
import jax.numpy as jnp
from jax import lax
from jax.experimental import pallas as pl
from jax.experimental.pallas import tpu as pltpu
from jax.sharding import PartitionSpec as P

ITERS = 3
BLOCK = 256
PAD = 16
ridge_weight = 0.1

SMEM = pl.BlockSpec(memory_space=pltpu.SMEM)
VMEM = pl.BlockSpec(memory_space=pltpu.VMEM)
F32 = jnp.float32
BF16 = jnp.bfloat16


def call(body, outs, args, n_smem, flops, name):
    return pl.pallas_call(
        body,
        out_shape=[pltpu.VMEM(o.shape, o.dtype) for o in outs],
        in_specs=[SMEM] * n_smem + [VMEM] * (len(args) - n_smem),
        out_specs=[VMEM] * len(outs),
        compiler_params=pltpu.CompilerParams(vmem_limit_bytes=24 * 1024 * 1024),
        cost_estimate=pl.CostEstimate(flops=flops, bytes_accessed=1 << 20, transcendentals=0),
        name=name,
    )(*args)


def column_of(row_values, lanes):
    return jnp.broadcast_to(row_values, (lanes, row_values.shape[1])).T


def row_of(column, rows):
    return jnp.broadcast_to(column, (column.shape[0], 128)).T[:rows]


def pack(values, out_ref):
    users, rank = values.shape
    top = jnp.max(jnp.abs(values), axis=1, keepdims=True)
    power = jnp.ceil(jnp.log2(jnp.maximum(top, 1e-30)))
    scaled = jnp.clip(jnp.round(values * jnp.exp2(15.0 - power)), -32767.0, 32767.0)
    out_ref[:users, :] = scaled.astype(jnp.int32).astype(jnp.int16)
    exponents = row_of(power, PAD).astype(jnp.int32).astype(jnp.int16)
    for at in range(0, rank, users):
        out_ref[users:, at : at + users] = exponents


def unpack(ref):
    users = ref.shape[0] - PAD
    rank = ref.shape[1]
    exponents = ref[users:, :users].astype(jnp.int32).astype(F32)[:1]
    scale = jnp.exp2(column_of(exponents, 128) - 15.0)
    whole = ref[:users, :].astype(jnp.int32).astype(F32)
    return jnp.concatenate([whole[:, at : at + 128] * scale for at in range(0, rank, 128)], axis=1)


def tree_sum(parts):
    while len(parts) > 1:
        parts = [parts[i] + parts[i + 1] for i in range(0, len(parts), 2)]
    return parts[0]


def masks_kernel(pieces, rows, me_ref, picks_ref, counts_ref, words_ref, conf_ref, out_ref):
    me = me_ref[0]
    obs, _, width = words_ref.shape
    lane = lax.broadcasted_iota(jnp.int32, (1, BLOCK), 1)
    word_index = lax.broadcasted_iota(jnp.int32, (width, BLOCK), 0)
    for at in range(0, out_ref.shape[2], BLOCK):
        slot = jnp.zeros((1, BLOCK), jnp.int32)
        for place, shard, offset, length in pieces:
            if at <= place < at + BLOCK:
                start = (me ^ shard) * rows + offset - (place - at)
                slot = jnp.where(lane >= place - at, lane + start, slot)
        spread = (word_index == jnp.right_shift(slot, 3)).astype(BF16)
        for p in range(obs):
            count = counts_ref[picks_ref[p]]
            word = jnp.dot(words_ref[p], spread, preferred_element_type=F32).astype(jnp.int32)
            bits = jnp.right_shift(word, slot & 7) & 1
            bits = jnp.where(slot < count, bits, 0).astype(F32)
            out_ref[p, :, at : at + BLOCK] = bits * conf_ref[...]


def gather_kernel(pieces, rows, place, first, last, *refs):
    me_ref, picks_ref, counts_ref, alpha_ref, conf_ref, prev_ref = refs[:6]
    at = 6
    shards = refs[at : at + len(pieces)]
    at += len(pieces)
    if not first:
        sums_in, gram_in = refs[at : at + 2]
        at += 2
    if last:
        picked_ref, gram_ref, msg_ref = refs[at:]
    else:
        picked_ref, gram_ref, sums_ref = refs[at:]
    me = me_ref[0]
    users, rank = prev_ref.shape
    obs = alpha_ref.shape[0]
    tiles = shards[0].shape[0]
    for p in range(obs):
        tile = picks_ref[p]
        for (spot, _, _, length), ref in zip(pieces, shards):
            picked_ref[p, spot - place : spot - place + length, :] = ref[tile]
    gram = jnp.zeros((rank, rank), F32) if first else gram_in[...]
    for (_, shard, offset, length), ref in zip(pieces, shards):
        slot = lax.broadcasted_iota(jnp.int32, (length, rank), 0) + ((me ^ shard) * rows + offset)
        for t in range(tiles):
            tile_rows = ref[t]
            masked = jnp.where(slot < counts_ref[t], tile_rows, jnp.zeros_like(tile_rows))
            gram = gram + lax.dot_general(
                masked, tile_rows, (((0,), (0,)), ((), ())), preferred_element_type=F32
            )
    gram_ref[...] = gram
    prev = prev_ref[...]
    rhs = jnp.zeros((users, rank), F32) if first else sums_in[0]
    image = jnp.zeros((users, rank), F32) if first else sums_in[1]
    for p in range(obs):
        for start in range(0, picked_ref.shape[1], BLOCK):
            items = picked_ref[p, start : start + BLOCK, :]
            alpha = alpha_ref[p, :, place + start : place + start + BLOCK]
            scores = lax.dot_general(
                prev, items, (((1,), (1,)), ((), ())), preferred_element_type=F32
            )
            weights = (alpha * scores).astype(BF16)
            seen = jnp.where(alpha > 0.0, 1.0, 0.0).astype(BF16)
            rhs = rhs + jnp.dot(seen, items, preferred_element_type=F32)
            image = image + jnp.dot(weights, items, preferred_element_type=F32)
    if last:
        image = image + jnp.dot(prev.astype(F32), gram, precision=lax.Precision.HIGHEST)
        pack((1.0 + conf_ref[...]) * rhs - image, msg_ref)
    else:
        sums_ref[0] = rhs
        sums_ref[1] = image


def round_kernel(step_index, n_msgs, spots, *refs):
    msgs = refs[:n_msgs]
    refs = refs[n_msgs:]
    n_in = 2 if step_index == 0 else 4
    prev_ref, alpha_ref, gram_ref = refs[:3]
    refs = refs[3:]
    picked = refs[: len(spots)]
    refs = refs[len(spots) :]
    summed = tree_sum([unpack(m) for m in msgs])
    if step_index == 0:
        (r_ref, msg_ref) = refs
        residual = summed - ridge_weight * prev_ref[...].astype(F32)
        direction = residual
        r_ref[...] = residual
    else:
        n_state = 1 if step_index == 1 else 3
        state = refs[:n_state]
        refs = refs[n_state:]
        if step_index == 1:
            residual = direction = state[0][...]
            solution = prev_ref[...].astype(F32)
        else:
            residual, direction, solution = (s[...] for s in state)
        image = summed + ridge_weight * direction
        norm_now = jnp.sum(residual * residual, axis=1, keepdims=True)
        step_size = norm_now / jnp.sum(direction * image, axis=1, keepdims=True)
        solution = solution + step_size * direction
        residual = residual - step_size * image
        norm_next = jnp.sum(residual * residual, axis=1, keepdims=True)
        direction = residual + (norm_next / norm_now) * direction
        if step_index < ITERS - 1:
            r_ref, d_ref, x_ref, msg_ref = refs
            r_ref[...] = residual
        else:
            n_ref, d_ref, x_ref, msg_ref = refs
            n_ref[...] = jnp.broadcast_to(norm_next, n_ref.shape)
        d_ref[...] = direction
        x_ref[...] = solution
    last = step_index == ITERS - 1
    rounded = direction.astype(BF16)
    image = jnp.dot(direction, gram_ref[...], precision=lax.Precision.HIGHEST)
    if last:
        total = jnp.sum(image * direction, axis=1, keepdims=True)
        squares = jnp.zeros((direction.shape[0], BLOCK), F32)
    for (place, size), ref in zip(spots, picked):
        for p in range(alpha_ref.shape[0]):
            for start in range(0, size, BLOCK):
                items = ref[p, start : start + BLOCK, :]
                alpha = alpha_ref[p, :, place + start : place + start + BLOCK]
                scores = lax.dot_general(
                    rounded, items, (((1,), (1,)), ((), ())), preferred_element_type=F32
                )
                weights = (alpha * scores).astype(BF16)
                if last:
                    squares = squares + weights.astype(F32) * scores
                else:
                    image = image + jnp.dot(weights, items, preferred_element_type=F32)
    if last:
        total = total + jnp.sum(squares, axis=1, keepdims=True)
        msg_ref[...] = row_of(total, msg_ref.shape[0])
    else:
        pack(image, msg_ref)


def final_kernel(n_msgs, *refs):
    msgs = refs[:n_msgs]
    n_ref, d_ref, x_ref, out_ref = refs[n_msgs:]
    direction = d_ref[...]
    total = column_of(tree_sum([m[...] for m in msgs])[:1], 128)
    squares = jnp.sum(direction * direction, axis=1, keepdims=True)
    step_size = n_ref[...] / (total + ridge_weight * squares)
    for at in range(0, direction.shape[1], 128):
        out_ref[:, at : at + 128] = x_ref[:, at : at + 128] + step_size * direction[:, at : at + 128]


def shifted(array, axis, size, bits):
    return lax.ppermute(array, axis, [(i, i ^ bits) for i in range(size)])


def gather_plan(own, size):
    send = functools.partial(shifted, axis="row", size=size)
    held = {0: own}
    bit = 8
    while bit < size:
        held.update({s ^ bit: send(a, bits=bit) for s, a in held.items()})
        bit *= 2
    if size < 8:
        bit = 1
        while bit < size:
            held.update({s ^ bit: send(a, bits=bit) for s, a in held.items()})
            bit *= 2
        return [[(s, 0, a) for s, a in held.items()]]
    stages = [[], [], []]
    half = own.shape[1] // 2
    for s, a in held.items():
        x, y = send(a, bits=2), send(a, bits=4)
        upper, lower = send(x[:, :half], bits=4), send(y[:, half:], bits=2)
        stages[0] += [(s, 0, a), (s ^ 1, 0, send(a, bits=1))]
        stages[1] += [(s ^ 2, 0, x), (s ^ 3, 0, send(x, bits=1)), (s ^ 4, 0, y), (s ^ 5, 0, send(y, bits=1))]
        stages[2] += [(s ^ 6, 0, upper), (s ^ 7, 0, send(upper, bits=1))]
        stages[2] += [(s ^ 6, half, lower), (s ^ 7, half, send(lower, bits=1))]
    return stages


def local(mesh, item_factors, tile_counts, observed_tiles, mask_words, confidence, previous):
    n_row, n_col = mesh.shape["row"], mesh.shape["col"]
    tiles, rows, rank = item_factors.shape
    users, obs, width = mask_words.shape
    slots = rows * n_row
    me = lax.axis_index("row").astype(jnp.int32).reshape(1)
    picks = observed_tiles[0]
    conf = confidence[:, None]
    words = jnp.transpose(mask_words, (1, 0, 2)).astype(BF16)
    shape = jax.ShapeDtypeStruct

    stages, pieces, place = [], [], 0
    for stage in gather_plan(item_factors, n_row):
        here, start = [], place
        for shard, offset, array in stage:
            here.append((place, shard, offset, array.shape[1]))
            place += array.shape[1]
        stages.append((start, here, [array for _, _, array in stage]))
        pieces += here

    (alpha,) = call(
        functools.partial(masks_kernel, pieces, rows),
        [shape((obs, users, slots), F32)],
        (me, picks, tile_counts, words, conf),
        3,
        2 * obs * users * slots * width,
        "masks",
    )

    message = shape((users + PAD, rank), jnp.int16)
    sums = shape((2, users, rank), F32)
    gram_shape = shape((rank, rank), F32)
    spots, picked, carry = [], [], []
    for index, (start, here, arrays) in enumerate(stages):
        first, last = index == 0, index == len(stages) - 1
        size = sum(length for _, _, _, length in here)
        kept, gram, carried = call(
            functools.partial(gather_kernel, here, rows, start, first, last),
            [shape((obs, size, rank), BF16), gram_shape, message if last else sums],
            (me, picks, tile_counts, alpha, conf, previous, *arrays, *carry),
            3,
            2 * size * rank * (tiles * rank + 3 * obs * users),
            f"stage{index}",
        )
        carry = [carried, gram]
        spots.append((start, size))
        picked.append(kept)
    msg, gram = carry

    def to_all(own):
        return [own] + [shifted(own, "col", n_col, bits) for bits in range(1, n_col)]

    vec = shape((users, rank), F32)
    state = []
    for index in range(ITERS):
        last = index == ITERS - 1
        msgs = to_all(msg)
        outs = [vec] if index == 0 else [vec, vec, vec]
        if last:
            outs = [shape((users, 128), F32), vec, vec]
        outs.append(shape((8, users), F32) if last else message)
        *state, msg = call(
            functools.partial(round_kernel, index, n_col, spots),
            outs,
            (*msgs, previous, alpha, gram, *picked, *state),
            0,
            4 * obs * users * slots * rank,
            f"round{index}",
        )
    msgs = to_all(msg)
    (out,) = pl.pallas_call(
        functools.partial(final_kernel, n_col),
        out_shape=[vec],
        in_specs=[VMEM] * (n_col + 3),
        out_specs=[VMEM],
        name="final",
    )(*msgs, *state)
    return out


def solution(mesh):
    return jax.shard_map(
        functools.partial(local, mesh),
        mesh=mesh,
        in_specs=(
            P("col", "row", None),
            P("col"),
            P("row", "col"),
            P("row", "col", None),
            P("row"),
            P("row", None),
        ),
        out_specs=P("row", None),
        check_vma=False,
    )
```

time: 232 us -> 83.8 us (0.36)
  waiting for transfers between devices: 179 us -> 37.1 us
  matrix products: 30.2 us -> 0 us
  starting transfers between devices: 0.17 us -> 25.8 us
  Pallas kernels: 0 us -> 15.1 us
  between operations: 13.3 us -> 0.13 us
  other arithmetic: 4.04 us -> 0.97 us
    psum x4 -> x0, waiting for transfers between devices: 142 us -> none  [reduce_terms(): return lax.psum(parts, 'col')]
    ppermute x0 -> x21, waiting for transfers between devices: none -> 37.1 us  [shifted(): return lax.ppermute(array, axis, [(i, i ^ bits) for i in range(size)])]
    all_gather x1 -> x0, waiting for transfers between devices: 36.9 us -> none  [local(): tiles = lax.all_gather(item_factors, 'row', axis=1, tiled=True)]
    dot_general x15 -> x0, matrix products: 30.2 us -> none  [the longest x8 16.5 us: weighted(): jnp.dot(weights, slot_tiles[slot], preferred_element_type=jnp.float32)]
    ppermute x0 -> x21, starting transfers between devices: none -> 25.8 us  [shifted(): return lax.ppermute(array, axis, [(i, i ^ bits) for i in range(size)])]
    pallas_call x0 -> x8, Pallas kernels: none -> 15.1 us  [the longest x7 13.2 us: call(): pl.pallas_call(body, out_shape=[pltpu.VMEM(o.shape, o.dtype) for o in out...]
    gather x2 -> x0, local copies, waits for them, and re-layouts: 3.44 us -> none  [the longest x1 2.87 us: local(): slot_tiles = tiles[picked]]
    unnamed x11 -> x22, local copies, waits for them, and re-layouts: 1.1 us -> 3.82 us
  transfers between devices with their start and end apart: 5 -> 21, of which waited for: 5 -> 12; matrix products, arithmetic and copies ran while one was open for 2% -> 2% of each run, Pallas kernels for 0% -> 6%
where the time goes in v1:
time: 83.8 us; the launch traced here: 83.6 us
  waiting for transfers between devices  37.1 us (44%)
  starting transfers between devices  25.8 us (31%)
  Pallas kernels  15.1 us (18%)
  local copies, waits for them, and re-layouts  4.62 us (6%)
  other arithmetic  0.97 us (1%)
    ppermute x21, waiting for transfers between devices, shifted(): return lax.ppermute(array, axis, [(i, i ^ bits) for i in range(size)])  37.1 us
    ppermute x21, starting transfers between devices, shifted(): return lax.ppermute(array, axis, [(i, i ^ bits) for i in range(size)])  25.8 us
    pallas_call x7, Pallas kernels, call(): pl.pallas_call(body, out_shape=[pltpu.VMEM(o.shape, o.dtype) for o in out...  13.2 us
    unnamed x22, local copies, waits for them, and re-layouts  3.82 us
    pallas_call x1, Pallas kernels, local(): pl.pallas_call(functools.partial(final_kernel, n_col), out_shape=[vec], i...  1.82 us
  transfers between devices with their start and end apart: 21, of which 12 were waited for; matrix products, arithmetic and copies ran while one was open for 2% of the time, Pallas kernels for 6%

profile of v1, /device:TPU:0, one launch (start us, length us, event | category | flops | bytes accessed | tf_op | source)
XLA Modules:
  0.0 83.6 jit_solution(11798232419274517402)
XLA Ops:
  0.0 2.9 %collective-permute-start = (bf16[4,256,256]{2,1,0:T(8,128)(2,1)}, bf16[4,256,256]{2,1,0:T(8,128)(2,1)S(1)}, u32[]{:S(2)}, u32[]{:S(2)}) collective-permute-start(bf16[4,256,256]{2,1,0:T(8,128)(2,1)} %refs_6_.1), channel_id=1, source_target_pairs={{0,8},{4,12},{8,0},{12,4},{16,24},{20,28},{24,16},{28,20},{1,9},{5... | collective-permute-start | bytes 1572872 | tf_op jit(solution)/shard_map/ppermute | solution.py:215
  2.9 1.5 %collective-permute-start.3 = (bf16[4,256,256]{2,1,0:T(8,128)(2,1)}, bf16[4,256,256]{2,1,0:T(8,128)(2,1)S(1)}, u32[]{:S(2)}, u32[]{:S(2)}) collective-permute-start(bf16[4,256,256]{2,1,0:T(8,128)(2,1)} %refs_6_.1), channel_id=1, source_target_pairs={{0,16},{4,20},{8,24},{12,28},{16,0},{20,4},{24,8},{28,12},{1,17},{... | collective-permute-start | bytes 1572872 | tf_op jit(solution)/shard_map/ppermute | solution.py:215
  4.5 10.7 %collective-permute-done.refs_6_ = bf16[4,256,256]{2,1,0:T(8,128)(2,1)S(1)} collective-permute-done((bf16[4,256,256]{2,1,0:T(8,128)(2,1)}, bf16[4,256,256]{2,1,0:T(8,128)(2,1)S(1)}, u32[]{:S(2)}, u32[]{:S(2)}) %collective-permute-start) | collective-permute-done | bytes 524320 | tf_op jit(solution)/shard_map/ppermute | solution.py:215
  15.2 1.8 %collective-permute-start.1 = (bf16[4,128,256]{2,1,0:T(8,128)(2,1)S(1)}, bf16[4,128,256]{2,1,0:T(8,128)(2,1)}, u32[]{:S(2)}, u32[]{:S(2)}) collective-permute-start(bf16[4,128,256]{2,1,0:T(8,128)(2,1)S(1)} %slice.8), channel_id=1, source_target_pairs={{0,16},{4,20},{8,24},{12,28},{16,0},{20,4},{24,8},{28,12},{1,17},{... | collective-permute-start | bytes 786440 | tf_op jit(solution)/shard_map/ppermute | solution.py:215
  17.0 1.6 %collective-permute-start.4 = (bf16[4,128,256]{2,1,0:T(8,128)(2,1)S(1)}, bf16[4,128,256]{2,1,0:T(8,128)(2,1)}, u32[]{:S(2)}, u32[]{:S(2)}) collective-permute-start(bf16[4,128,256]{2,1,0:T(8,128)(2,1)S(1)} %slice.9), channel_id=1, source_target_pairs={{0,8},{4,12},{8,0},{12,4},{16,24},{20,28},{24,16},{28,20},{1,9},{5... | collective-permute-start | bytes 786440 | tf_op jit(solution)/shard_map/ppermute | solution.py:215
  19.0 3.8 %collective-permute-done.1.refs_6_ = bf16[4,128,256]{2,1,0:T(8,128)(2,1)} collective-permute-done((bf16[4,128,256]{2,1,0:T(8,128)(2,1)S(1)}, bf16[4,128,256]{2,1,0:T(8,128)(2,1)}, u32[]{:S(2)}, u32[]{:S(2)}) %collective-permute-start.1) | collective-permute-done | bytes 262176 | tf_op jit(solution)/shard_map/ppermute | solution.py:215
  28.5 1.4 %stage0.1 = (bf16[2,512,256]{2,1,0:T(8,128)(2,1)S(1)}, f32[256,256]{1,0:T(8,128)S(1)}, f32[2,128,256]{2,1,0:T(8,128)S(1)}) custom-call(s32[1]{0:T(128)} %bitcast.me_ref.refs_0_, s32[2]{0:T(128)S(1)} %bitcast.6, s32[4]{0:T(128)S(1)} %copy-done.6, f32[2,128,2048]{2,1,0:T(8,128)S(1)} %masks.1.refs_3_.refs_5_, f32[128,1]{1,0:T(8,128)S(1)} %copy.8.conf_ref.refs_4_, ...), custom_call_target="tpu_custom_call" | custom-call | flops 469762048 | bytes 1048576 | tf_op jit(solution)/shard_map/stage0/pallas_call | solution.py:22
  29.9 2.3 %stage1.1 = (bf16[2,1024,256]{2,1,0:T(8,128)(2,1)S(1)}, f32[256,256]{1,0:T(8,128)S(1)}, f32[2,128,256]{2,1,0:T(8,128)S(1)}) custom-call(s32[1]{0:T(128)} %bitcast.me_ref.refs_0_, s32[2]{0:T(128)S(1)} %bitcast.7, s32[4]{0:T(128)S(1)} %copy-done.6, f32[2,128,2048]{2,1,0:T(8,128)S(1)} %masks.1.refs_3_.refs_5_, f32[128,1]{1,0:T(8,128)S(1)} %copy.8.conf_ref.refs_4_, ...), custom_call_target="tpu_custom_call" | custom-call | flops 939524096 | bytes 1048576 | tf_op jit(solution)/shard_map/stage1/pallas_call | solution.py:22
  32.2 2.8 %stage2.1 = (bf16[2,512,256]{2,1,0:T(8,128)(2,1)S(1)}, f32[256,256]{1,0:T(8,128)S(1)}, s16[144,256]{1,0:T(8,128)(2,1)S(1)}) custom-call(s32[1]{0:T(128)} %bitcast.me_ref.refs_0_, s32[2]{0:T(128)S(1)} %bitcast.8, s32[4]{0:T(128)S(1)} %copy-done.6, f32[2,128,2048]{2,1,0:T(8,128)S(1)} %masks.1.refs_3_.refs_5_, f32[128,1]{1,0:T(8,128)S(1)} %copy.8.conf_ref.refs_4_, ...), custom_call_target="tpu_custom_call" | custom-call | flops 469762048 | bytes 1048576 | tf_op jit(solution)/shard_map/stage2/pallas_call | solution.py:22
  35.0 2.6 %collective-permute-start.10 = (s16[144,256]{1,0:T(8,128)(2,1)S(1)}, s16[144,256]{1,0:T(8,128)(2,1)S(1)}, u32[]{:S(2)}, u32[]{:S(2)}) collective-permute-start(s16[144,256]{1,0:T(8,128)(2,1)S(1)} %get-tuple-element.28.refs_0_), channel_id=1, source_target_pairs={{0,2},{1,3},{2,0},{3,1},{4,6},{5,7},{6,4},{7,5},{8,10},{9,11},{10,... | collective-permute-start | bytes 221192 | tf_op jit(solution)/shard_map/ppermute | solution.py:215
  39.2 4.6 %collective-permute-done.10.refs_2_ = s16[144,256]{1,0:T(8,128)(2,1)S(1)} collective-permute-done((s16[144,256]{1,0:T(8,128)(2,1)S(1)}, s16[144,256]{1,0:T(8,128)(2,1)S(1)}, u32[]{:S(2)}, u32[]{:S(2)}) %collective-permute-start.10) | collective-permute-done | bytes 73760 | tf_op jit(solution)/shard_map/ppermute | solution.py:215
  45.2 1.9 %round0.1 = (f32[128,256]{1,0:T(8,128)S(1)}, s16[144,256]{1,0:T(8,128)(2,1)S(1)}) custom-call(s16[144,256]{1,0:T(8,128)(2,1)S(1)} %get-tuple-element.28.refs_0_, s16[144,256]{1,0:T(8,128)(2,1)S(1)} %collective-permute-done.9.refs_1_, s16[144,256]{1,0:T(8,128)(2,1)S(1)} %collective-permute-done.10.refs_2_, ...), custom_call_target="tpu_custom_call" | custom-call | flops 536870912 | bytes 1048576 | tf_op jit(solution)/shard_map/round0/pallas_call | solution.py:22
  48.1 3.0 %collective-permute-start.13 = (s16[144,256]{1,0:T(8,128)(2,1)S(1)}, s16[144,256]{1,0:T(8,128)(2,1)S(1)}, u32[]{:S(2)}, u32[]{:S(2)}) collective-permute-start(s16[144,256]{1,0:T(8,128)(2,1)S(1)} %get-tuple-element.33.refs_0_), channel_id=1, source_target_pairs={{0,2},{1,3},{2,0},{3,1},{4,6},{5,7},{6,4},{7,5},{8,10},{9,11},{10,... | collective-permute-start | bytes 221192 | tf_op jit(solution)/shard_map/ppermute | solution.py:215
  52.3 3.8 %collective-permute-done.13.refs_2_ = s16[144,256]{1,0:T(8,128)(2,1)S(1)} collective-permute-done((s16[144,256]{1,0:T(8,128)(2,1)S(1)}, s16[144,256]{1,0:T(8,128)(2,1)S(1)}, u32[]{:S(2)}, u32[]{:S(2)}) %collective-permute-start.13) | collective-permute-done | bytes 73760 | tf_op jit(solution)/shard_map/ppermute | solution.py:215
  57.3 2.1 %round1.1 = (f32[128,256]{1,0:T(8,128)S(1)}, f32[128,256]{1,0:T(8,128)S(1)}, f32[128,256]{1,0:T(8,128)S(1)}, s16[144,256]{1,0:T(8,128)(2,1)S(1)}) custom-call(s16[144,256]{1,0:T(8,128)(2,1)S(1)} %get-tuple-element.33.refs_0_, s16[144,256]{1,0:T(8,128)(2,1)S(1)} %collective-permute-done.12.refs_1_, s16[144,256]{1,0:T(8,128)(2,1)S(1)} %collective-permute-done.13.refs_2_, ...), custom_call_target="tpu_custom_call" | custom-call | flops 536870912 | bytes 1048576 | tf_op jit(solution)/shard_map/round1/pallas_call | solution.py:22
  59.4 1.5 %collective-permute-start.15 = (s16[144,256]{1,0:T(8,128)(2,1)S(1)}, s16[144,256]{1,0:T(8,128)(2,1)S(1)}, u32[]{:S(2)}, u32[]{:S(2)}) collective-permute-start(s16[144,256]{1,0:T(8,128)(2,1)S(1)} %get-tuple-element.35.refs_0_), channel_id=1, source_target_pairs={{0,1},{1,0},{2,3},{3,2},{4,5},{5,4},{6,7},{7,6},{8,9},{9,8},{10,11... | collective-permute-start | bytes 221192 | tf_op jit(solution)/shard_map/ppermute | solution.py:215
  60.9 1.6 %collective-permute-start.16 = (s16[144,256]{1,0:T(8,128)(2,1)S(1)}, s16[144,256]{1,0:T(8,128)(2,1)S(1)}, u32[]{:S(2)}, u32[]{:S(2)}) collective-permute-start(s16[144,256]{1,0:T(8,128)(2,1)S(1)} %get-tuple-element.35.refs_0_), channel_id=1, source_target_pairs={{0,2},{1,3},{2,0},{3,1},{4,6},{5,7},{6,4},{7,5},{8,10},{9,11},{10,... | collective-permute-start | bytes 221192 | tf_op jit(solution)/shard_map/ppermute | solution.py:215
  63.9 5.7 %collective-permute-done.16.refs_2_ = s16[144,256]{1,0:T(8,128)(2,1)S(1)} collective-permute-done((s16[144,256]{1,0:T(8,128)(2,1)S(1)}, s16[144,256]{1,0:T(8,128)(2,1)S(1)}, u32[]{:S(2)}, u32[]{:S(2)}) %collective-permute-start.16) | collective-permute-done | bytes 73760 | tf_op jit(solution)/shard_map/ppermute | solution.py:215
  72.9 1.5 %collective-permute-start.18 = (f32[8,128]{1,0:T(8,128)S(1)}, f32[8,128]{1,0:T(8,128)S(1)}, u32[]{:S(2)}, u32[]{:S(2)}) collective-permute-start(f32[8,128]{1,0:T(8,128)S(1)} %get-tuple-element.39.refs_0_), channel_id=1, source_target_pairs={{0,1},{1,0},{2,3},{3,2},{4,5},{5,4},{6,7},{7,6},{8,9},{9,8},{10,11... | collective-permute-start | bytes 12296 | tf_op jit(solution)/shard_map/ppermute | solution.py:215
  74.3 1.5 %collective-permute-start.19 = (f32[8,128]{1,0:T(8,128)S(1)}, f32[8,128]{1,0:T(8,128)S(1)}, u32[]{:S(2)}, u32[]{:S(2)}) collective-permute-start(f32[8,128]{1,0:T(8,128)S(1)} %get-tuple-element.39.refs_0_), channel_id=1, source_target_pairs={{0,2},{1,3},{2,0},{3,1},{4,6},{5,7},{6,4},{7,5},{8,10},{9,11},{10,... | collective-permute-start | bytes 12296 | tf_op jit(solution)/shard_map/ppermute | solution.py:215
  75.8 1.4 %collective-permute-start.20 = (f32[8,128]{1,0:T(8,128)S(1)}, f32[8,128]{1,0:T(8,128)S(1)}, u32[]{:S(2)}, u32[]{:S(2)}) collective-permute-start(f32[8,128]{1,0:T(8,128)S(1)} %get-tuple-element.39.refs_0_), channel_id=1, source_target_pairs={{0,3},{1,2},{2,1},{3,0},{4,7},{5,6},{6,5},{7,4},{8,11},{9,10},{10,... | collective-permute-start | bytes 12296 | tf_op jit(solution)/shard_map/ppermute | solution.py:215
  77.3 1.6 %collective-permute-done.19.refs_2_ = f32[8,128]{1,0:T(8,128)S(1)} collective-permute-done((f32[8,128]{1,0:T(8,128)S(1)}, f32[8,128]{1,0:T(8,128)S(1)}, u32[]{:S(2)}, u32[]{:S(2)}) %collective-permute-start.19) | collective-permute-done | bytes 4128 | tf_op jit(solution)/shard_map/ppermute | solution.py:215
  78.9 2.3 %collective-permute-done.20.refs_3_ = f32[8,128]{1,0:T(8,128)S(1)} collective-permute-done((f32[8,128]{1,0:T(8,128)S(1)}, f32[8,128]{1,0:T(8,128)S(1)}, u32[]{:S(2)}, u32[]{:S(2)}) %collective-permute-start.20) | collective-permute-done | bytes 4128 | tf_op jit(solution)/shard_map/ppermute | solution.py:215
  81.8 1.8 %final.1 = f32[128,256]{1,0:T(8,128)} custom-call(f32[8,128]{1,0:T(8,128)} %copy-done.7, f32[8,128]{1,0:T(8,128)} %copy-done.8, f32[8,128]{1,0:T(8,128)} %copy-done.9, f32[8,128]{1,0:T(8,128)} %copy-done.10, f32[128,128]{1,0:T(8,128)} %copy-done.4, f32[128,256]{1,0:T(8,128)} %copy-done.2, f32[128,256]{1,0:T(8,128)} %copy-done.3), custom_call_target="tpu_custom_call" | custom-call | tf_op jit(solution)/shard_map/final/pallas_call | solution.py:313
  (52 shorter events, 17.7 us)
Async XLA Ops:
  0.0 28.4 %copy-start.1 = (bf16[4,256,256]{2,1,0:T(8,128)(2,1)S(1)}, bf16[4,256,256]{2,1,0:T(8,128)(2,1)}, u32[]{:S(2)}) copy-start(bf16[4,256,256]{2,1,0:T(8,128)(2,1)} %refs_6_.1) | copy-start | bytes 1572868
  0.0 28.5 %copy-start = (bf16[128,256]{1,0:T(8,128)(2,1)S(1)}, bf16[128,256]{1,0:T(8,128)(2,1)}, u32[]{:S(2)}) copy-start(bf16[128,256]{1,0:T(8,128)(2,1)} %refs_4_.5) | copy-start | bytes 196612
  0.0 15.1 %collective-permute-start = (bf16[4,256,256]{2,1,0:T(8,128)(2,1)}, bf16[4,256,256]{2,1,0:T(8,128)(2,1)S(1)}, u32[]{:S(2)}, u32[]{:S(2)}) collective-permute-start(bf16[4,256,256]{2,1,0:T(8,128)(2,1)} %refs_6_.1), channel_id=1, source_target_pairs={{0,8},{4,12},{8,0},{12,4},{16,24},{20,28},{24,16},{28,20},{1,9},{5... | collective-permute-start | bytes 1572872 | tf_op jit(solution)/shard_map/ppermute | solution.py:215
  2.9 14.0 %collective-permute-start.3 = (bf16[4,256,256]{2,1,0:T(8,128)(2,1)}, bf16[4,256,256]{2,1,0:T(8,128)(2,1)S(1)}, u32[]{:S(2)}, u32[]{:S(2)}) collective-permute-start(bf16[4,256,256]{2,1,0:T(8,128)(2,1)} %refs_6_.1), channel_id=1, source_target_pairs={{0,16},{4,20},{8,24},{12,28},{16,0},{20,4},{24,8},{28,12},{1,17},{... | collective-permute-start | bytes 1572872 | tf_op jit(solution)/shard_map/ppermute | solution.py:215
  4.5 24.0 %collective-permute-start.8 = (bf16[4,256,256]{2,1,0:T(8,128)(2,1)}, bf16[4,256,256]{2,1,0:T(8,128)(2,1)S(1)}, u32[]{:S(2)}, u32[]{:S(2)}) collective-permute-start(bf16[4,256,256]{2,1,0:T(8,128)(2,1)} %refs_6_.1), channel_id=1, source_target_pairs={{0,4},{4,0},{8,12},{12,8},{16,20},{20,16},{24,28},{28,24},{1,5},{5... | collective-permute-start | bytes 1572872 | tf_op jit(solution)/shard_map/ppermute | solution.py:215
  15.2 7.7 %collective-permute-start.1 = (bf16[4,128,256]{2,1,0:T(8,128)(2,1)S(1)}, bf16[4,128,256]{2,1,0:T(8,128)(2,1)}, u32[]{:S(2)}, u32[]{:S(2)}) collective-permute-start(bf16[4,128,256]{2,1,0:T(8,128)(2,1)S(1)} %slice.8), channel_id=1, source_target_pairs={{0,16},{4,20},{8,24},{12,28},{16,0},{20,4},{24,8},{28,12},{1,17},{... | collective-permute-start | bytes 786440 | tf_op jit(solution)/shard_map/ppermute | solution.py:215
  17.0 7.1 %collective-permute-start.4 = (bf16[4,128,256]{2,1,0:T(8,128)(2,1)S(1)}, bf16[4,128,256]{2,1,0:T(8,128)(2,1)}, u32[]{:S(2)}, u32[]{:S(2)}) collective-permute-start(bf16[4,128,256]{2,1,0:T(8,128)(2,1)S(1)} %slice.9), channel_id=1, source_target_pairs={{0,8},{4,12},{8,0},{12,4},{16,24},{20,28},{24,16},{28,20},{1,9},{5... | collective-permute-start | bytes 786440 | tf_op jit(solution)/shard_map/ppermute | solution.py:215
  18.5 11.4 %collective-permute-start.6 = (bf16[4,256,256]{2,1,0:T(8,128)(2,1)S(1)}, bf16[4,256,256]{2,1,0:T(8,128)(2,1)S(1)}, u32[]{:S(2)}, u32[]{:S(2)}) collective-permute-start(bf16[4,256,256]{2,1,0:T(8,128)(2,1)S(1)} %collective-permute-done.refs_6_), channel_id=1, source_target_pairs={{0,4},{4,0},{8,12},{12,8},{16,20},{20,16},{24,28},{28,24},{1,5},{5... | collective-permute-start | bytes 1572872 | tf_op jit(solution)/shard_map/ppermute | solution.py:215
  18.5 11.4 %collective-permute-start.7 = (bf16[4,256,256]{2,1,0:T(8,128)(2,1)S(1)}, bf16[4,256,256]{2,1,0:T(8,128)(2,1)S(1)}, u32[]{:S(2)}, u32[]{:S(2)}) collective-permute-start(bf16[4,256,256]{2,1,0:T(8,128)(2,1)S(1)} %collective-permute-done.3.refs_8_), channel_id=1, source_target_pairs={{0,4},{4,0},{8,12},{12,8},{16,20},{20,16},{24,28},{28,24},{1,5},{5... | collective-permute-start | bytes 1572872 | tf_op jit(solution)/shard_map/ppermute | solution.py:215
  22.8 9.4 %collective-permute-start.2 = (bf16[4,128,256]{2,1,0:T(8,128)(2,1)}, bf16[4,128,256]{2,1,0:T(8,128)(2,1)}, u32[]{:S(2)}, u32[]{:S(2)}) collective-permute-start(bf16[4,128,256]{2,1,0:T(8,128)(2,1)} %collective-permute-done.1.refs_6_), channel_id=1, source_target_pairs={{0,4},{4,0},{8,12},{12,8},{16,20},{20,16},{24,28},{28,24},{1,5},{5... | collective-permute-start | bytes 786440 | tf_op jit(solution)/shard_map/ppermute | solution.py:215
  24.0 8.2 %collective-permute-start.5 = (bf16[4,128,256]{2,1,0:T(8,128)(2,1)}, bf16[4,128,256]{2,1,0:T(8,128)(2,1)}, u32[]{:S(2)}, u32[]{:S(2)}) collective-permute-start(bf16[4,128,256]{2,1,0:T(8,128)(2,1)} %collective-permute-done.4.refs_8_), channel_id=1, source_target_pairs={{0,4},{4,0},{8,12},{12,8},{16,20},{20,16},{24,28},{28,24},{1,5},{5... | collective-permute-start | bytes 786440 | tf_op jit(solution)/shard_map/ppermute | solution.py:215
  35.0 8.8 %collective-permute-start.10 = (s16[144,256]{1,0:T(8,128)(2,1)S(1)}, s16[144,256]{1,0:T(8,128)(2,1)S(1)}, u32[]{:S(2)}, u32[]{:S(2)}) collective-permute-start(s16[144,256]{1,0:T(8,128)(2,1)S(1)} %get-tuple-element.28.refs_0_), channel_id=1, source_target_pairs={{0,2},{1,3},{2,0},{3,1},{4,6},{5,7},{6,4},{7,5},{8,10},{9,11},{10,... | collective-permute-start | bytes 221192 | tf_op jit(solution)/shard_map/ppermute | solution.py:215
  37.6 6.9 %collective-permute-start.11 = (s16[144,256]{1,0:T(8,128)(2,1)S(1)}, s16[144,256]{1,0:T(8,128)(2,1)S(1)}, u32[]{:S(2)}, u32[]{:S(2)}) collective-permute-start(s16[144,256]{1,0:T(8,128)(2,1)S(1)} %get-tuple-element.28.refs_0_), channel_id=1, source_target_pairs={{0,3},{1,2},{2,1},{3,0},{4,7},{5,6},{6,5},{7,4},{8,11},{9,10},{10,... | collective-permute-start | bytes 221192 | tf_op jit(solution)/shard_map/ppermute | solution.py:215
  39.0 6.2 %collective-permute-start.9 = (s16[144,256]{1,0:T(8,128)(2,1)S(1)}, s16[144,256]{1,0:T(8,128)(2,1)S(1)}, u32[]{:S(2)}, u32[]{:S(2)}) collective-permute-start(s16[144,256]{1,0:T(8,128)(2,1)S(1)} %get-tuple-element.28.refs_0_), channel_id=1, source_target_pairs={{0,1},{1,0},{2,3},{3,2},{4,5},{5,4},{6,7},{7,6},{8,9},{9,8},{10,11... | collective-permute-start | bytes 221192 | tf_op jit(solution)/shard_map/ppermute | solution.py:215
  47.1 5.2 %collective-permute-start.12 = (s16[144,256]{1,0:T(8,128)(2,1)S(1)}, s16[144,256]{1,0:T(8,128)(2,1)S(1)}, u32[]{:S(2)}, u32[]{:S(2)}) collective-permute-start(s16[144,256]{1,0:T(8,128)(2,1)S(1)} %get-tuple-element.33.refs_0_), channel_id=1, source_target_pairs={{0,1},{1,0},{2,3},{3,2},{4,5},{5,4},{6,7},{7,6},{8,9},{9,8},{10,11... | collective-permute-start | bytes 221192 | tf_op jit(solution)/shard_map/ppermute | solution.py:215
  48.1 8.0 %collective-permute-start.13 = (s16[144,256]{1,0:T(8,128)(2,1)S(1)}, s16[144,256]{1,0:T(8,128)(2,1)S(1)}, u32[]{:S(2)}, u32[]{:S(2)}) collective-permute-start(s16[144,256]{1,0:T(8,128)(2,1)S(1)} %get-tuple-element.33.refs_0_), channel_id=1, source_target_pairs={{0,2},{1,3},{2,0},{3,1},{4,6},{5,7},{6,4},{7,5},{8,10},{9,11},{10,... | collective-permute-start | bytes 221192 | tf_op jit(solution)/shard_map/ppermute | solution.py:215
  51.1 6.2 %collective-permute-start.14 = (s16[144,256]{1,0:T(8,128)(2,1)S(1)}, s16[144,256]{1,0:T(8,128)(2,1)S(1)}, u32[]{:S(2)}, u32[]{:S(2)}) collective-permute-start(s16[144,256]{1,0:T(8,128)(2,1)S(1)} %get-tuple-element.33.refs_0_), channel_id=1, source_target_pairs={{0,3},{1,2},{2,1},{3,0},{4,7},{5,6},{6,5},{7,4},{8,11},{9,10},{10,... | collective-permute-start | bytes 221192 | tf_op jit(solution)/shard_map/ppermute | solution.py:215
  59.4 4.4 %collective-permute-start.15 = (s16[144,256]{1,0:T(8,128)(2,1)S(1)}, s16[144,256]{1,0:T(8,128)(2,1)S(1)}, u32[]{:S(2)}, u32[]{:S(2)}) collective-permute-start(s16[144,256]{1,0:T(8,128)(2,1)S(1)} %get-tuple-element.35.refs_0_), channel_id=1, source_target_pairs={{0,1},{1,0},{2,3},{3,2},{4,5},{5,4},{6,7},{7,6},{8,9},{9,8},{10,11... | collective-permute-start | bytes 221192 | tf_op jit(solution)/shard_map/ppermute | solution.py:215
  60.9 8.7 %collective-permute-start.16 = (s16[144,256]{1,0:T(8,128)(2,1)S(1)}, s16[144,256]{1,0:T(8,128)(2,1)S(1)}, u32[]{:S(2)}, u32[]{:S(2)}) collective-permute-start(s16[144,256]{1,0:T(8,128)(2,1)S(1)} %get-tuple-element.35.refs_0_), channel_id=1, source_target_pairs={{0,2},{1,3},{2,0},{3,1},{4,6},{5,7},{6,4},{7,5},{8,10},{9,11},{10,... | collective-permute-start | bytes 221192 | tf_op jit(solution)/shard_map/ppermute | solution.py:215
  62.5 7.1 %collective-permute-start.17 = (s16[144,256]{1,0:T(8,128)(2,1)S(1)}, s16[144,256]{1,0:T(8,128)(2,1)S(1)}, u32[]{:S(2)}, u32[]{:S(2)}) collective-permute-start(s16[144,256]{1,0:T(8,128)(2,1)S(1)} %get-tuple-element.35.refs_0_), channel_id=1, source_target_pairs={{0,3},{1,2},{2,1},{3,0},{4,7},{5,6},{6,5},{7,4},{8,11},{9,10},{10,... | collective-permute-start | bytes 221192 | tf_op jit(solution)/shard_map/ppermute | solution.py:215
  72.9 8.4 %copy-start.7 = (f32[8,128]{1,0:T(8,128)}, f32[8,128]{1,0:T(8,128)S(1)}, u32[]{:S(2)}) copy-start(f32[8,128]{1,0:T(8,128)S(1)} %get-tuple-element.39.refs_0_) | copy-start | bytes 12292
  72.9 4.4 %collective-permute-start.18 = (f32[8,128]{1,0:T(8,128)S(1)}, f32[8,128]{1,0:T(8,128)S(1)}, u32[]{:S(2)}, u32[]{:S(2)}) collective-permute-start(f32[8,128]{1,0:T(8,128)S(1)} %get-tuple-element.39.refs_0_), channel_id=1, source_target_pairs={{0,1},{1,0},{2,3},{3,2},{4,5},{5,4},{6,7},{7,6},{8,9},{9,8},{10,11... | collective-permute-start | bytes 12296 | tf_op jit(solution)/shard_map/ppermute | solution.py:215
  74.3 4.5 %collective-permute-start.19 = (f32[8,128]{1,0:T(8,128)S(1)}, f32[8,128]{1,0:T(8,128)S(1)}, u32[]{:S(2)}, u32[]{:S(2)}) collective-permute-start(f32[8,128]{1,0:T(8,128)S(1)} %get-tuple-element.39.refs_0_), channel_id=1, source_target_pairs={{0,2},{1,3},{2,0},{3,1},{4,6},{5,7},{6,4},{7,5},{8,10},{9,11},{10,... | collective-permute-start | bytes 12296 | tf_op jit(solution)/shard_map/ppermute | solution.py:215
  75.8 5.4 %collective-permute-start.20 = (f32[8,128]{1,0:T(8,128)S(1)}, f32[8,128]{1,0:T(8,128)S(1)}, u32[]{:S(2)}, u32[]{:S(2)}) collective-permute-start(f32[8,128]{1,0:T(8,128)S(1)} %get-tuple-element.39.refs_0_), channel_id=1, source_target_pairs={{0,3},{1,2},{2,1},{3,0},{4,7},{5,6},{6,5},{7,4},{8,11},{9,10},{10,... | collective-permute-start | bytes 12296 | tf_op jit(solution)/shard_map/ppermute | solution.py:215
  (8 other events, 10.1 us)

commit v2 on v1

v2 whole, which is shorter than its diff:
```python
import functools

import jax
import jax.numpy as jnp
from jax import lax
from jax.experimental import pallas as pl
from jax.experimental.pallas import tpu as pltpu
from jax.sharding import PartitionSpec as P

ITERS = 3
BLOCK = 256
ridge_weight = 0.1

SMEM = pl.BlockSpec(memory_space=pltpu.SMEM)
VMEM = pl.BlockSpec(memory_space=pltpu.VMEM)
F32 = jnp.float32
BF16 = jnp.bfloat16


def call(body, outs, args, n_smem, flops, name):
    return pl.pallas_call(
        body,
        out_shape=[pltpu.VMEM(o.shape, o.dtype) for o in outs],
        in_specs=[SMEM] * n_smem + [VMEM] * (len(args) - n_smem),
        out_specs=[VMEM] * len(outs),
        compiler_params=pltpu.CompilerParams(vmem_limit_bytes=24 * 1024 * 1024),
        cost_estimate=pl.CostEstimate(flops=flops, bytes_accessed=1 << 20, transcendentals=0),
        name=name,
    )(*args)


def column_of(row_values, lanes):
    return jnp.broadcast_to(row_values, (lanes, row_values.shape[1])).T


def row_of(column, rows):
    return jnp.broadcast_to(column, (column.shape[0], 128)).T[:rows]


def low_lanes(users):
    lane = lax.broadcasted_iota(jnp.int32, (users, 128), 1)
    return lane, lane < 8


def pack(values, out_ref):
    users, rank = values.shape
    top = jnp.max(jnp.abs(values), axis=1, keepdims=True)
    power = jnp.clip(jnp.ceil(jnp.log2(jnp.maximum(top, 1e-30))), -100.0, 127.0)
    scaled = jnp.round(values * jnp.exp2(15.0 - power))
    scaled = jnp.clip(scaled, -32767.0, 32767.0).astype(jnp.int32)
    lane, low = low_lanes(users)
    bit = jnp.right_shift(jnp.broadcast_to((power + 128.0).astype(jnp.int32), lane.shape), lane & 7) & 1
    head = scaled[:, :128]
    out_ref[:, :128] = jnp.where(low, (head & -2) | bit, head).astype(jnp.int16)
    out_ref[:, 128:] = scaled[:, 128:].astype(jnp.int16)


def unpack(ref):
    users = ref.shape[0]
    whole = ref[...].astype(jnp.int32)
    head = whole[:, :128]
    lane, low = low_lanes(users)
    bit = jnp.where(low, head & 1, 0)
    power = jnp.sum(jnp.left_shift(bit, lane & 7).astype(F32), axis=1, keepdims=True) - 128.0
    whole = jnp.concatenate([head - bit, whole[:, 128:]], axis=1)
    return whole.astype(F32) * jnp.exp2(power - 15.0)


def tree_sum(parts):
    while len(parts) > 1:
        parts = [parts[i] + parts[i + 1] for i in range(0, len(parts), 2)]
    return parts[0]


def shard_index(me, shards):
    even, odd = shards
    return me ^ (even + (me & 1) * (odd - even))


def masks_kernel(stages, rows, me_ref, picks_ref, counts_ref, words_ref, conf_ref, *out_refs):
    me = me_ref[0]
    obs, _, width = words_ref.shape
    lane = lax.broadcasted_iota(jnp.int32, (1, BLOCK), 1)
    word_index = lax.broadcasted_iota(jnp.int32, (width, BLOCK), 0)
    for pieces, out_ref in zip(stages, out_refs):
        for at in range(0, out_ref.shape[2], BLOCK):
            slot = jnp.zeros((1, BLOCK), jnp.int32)
            for spot, pair, offset, _ in pieces:
                if at <= spot < at + BLOCK:
                    start = shard_index(me, pair) * rows + offset - (spot - at)
                    slot = jnp.where(lane >= spot - at, lane + start, slot)
            spread = (word_index == jnp.right_shift(slot, 3)).astype(BF16)
            for p in range(obs):
                count = counts_ref[picks_ref[p]]
                word = jnp.dot(words_ref[p], spread, preferred_element_type=F32).astype(jnp.int32)
                bits = jnp.right_shift(word, slot & 7) & 1
                bits = jnp.where(slot < count, bits, 0).astype(F32)
                out_ref[p, :, at : at + BLOCK] = bits * conf_ref[...]


def gather_kernel(pieces, rows, first, last, *refs):
    me_ref, picks_ref, counts_ref, alpha_ref, conf_ref, prev_ref = refs[:6]
    at = 6
    arrays = refs[at : at + len(pieces)]
    at += len(pieces)
    if not first:
        gram_in, sums_in = refs[at : at + 2]
        at += 2
    picked_ref, turned_ref = refs[at : at + 2]
    at += 2
    if last:
        high_ref, low_ref, msg_ref = refs[at:]
    else:
        gram_ref, sums_ref = refs[at:]
    me = me_ref[0]
    users, rank = prev_ref.shape
    obs = alpha_ref.shape[0]
    tiles = arrays[0].shape[0]
    for p in range(obs):
        tile = picks_ref[p]
        for (spot, _, _, length), ref in zip(pieces, arrays):
            picked_ref[p, spot : spot + length, :] = ref[tile]
    gram = jnp.zeros((rank, rank), F32) if first else gram_in[...]
    for (_, pair, offset, length), ref in zip(pieces, arrays):
        slot = lax.broadcasted_iota(jnp.int32, (length, rank), 0)
        slot = slot + (shard_index(me, pair) * rows + offset)
        for t in range(tiles):
            tile_rows = ref[t]
            masked = jnp.where(slot < counts_ref[t], tile_rows, jnp.zeros_like(tile_rows))
            gram = gram + lax.dot_general(
                masked, tile_rows, (((0,), (0,)), ((), ())), preferred_element_type=F32
            )
    if last:
        high = gram.astype(BF16)
        low = (gram - high.astype(F32)).astype(BF16)
        high_ref[...] = high
        low_ref[...] = low
    else:
        gram_ref[...] = gram
    prev = prev_ref[...]
    rhs = jnp.zeros((users, rank), F32) if first else sums_in[0]
    image = jnp.zeros((users, rank), F32) if first else sums_in[1]
    for p in range(obs):
        for start in range(0, picked_ref.shape[1], BLOCK):
            items = picked_ref[p, start : start + BLOCK, :]
            turned = items.T
            turned_ref[p, :, start : start + BLOCK] = turned
            alpha = alpha_ref[p, :, start : start + BLOCK]
            scores = jnp.dot(prev, turned, preferred_element_type=F32)
            weights = (alpha * scores).astype(BF16)
            seen = jnp.where(alpha > 0.0, 1.0, 0.0).astype(BF16)
            rhs = rhs + jnp.dot(seen, items, preferred_element_type=F32)
            image = image + jnp.dot(weights, items, preferred_element_type=F32)
    if last:
        image = image + jnp.dot(prev, high, preferred_element_type=F32)
        image = image + jnp.dot(prev, low, preferred_element_type=F32)
        pack((1.0 + conf_ref[...]) * rhs - image, msg_ref)
    else:
        sums_ref[0] = rhs
        sums_ref[1] = image


def round_kernel(step_index, n_msgs, n_stages, *refs):
    msgs = refs[:n_msgs]
    refs = refs[n_msgs:]
    prev_ref, high_ref, low_ref = refs[:3]
    alphas, picked, turned = (refs[3 + n * n_stages : 3 + (n + 1) * n_stages] for n in range(3))
    refs = refs[3 + 3 * n_stages :]
    summed = tree_sum([unpack(m) for m in msgs])
    if step_index == 0:
        (r_ref, msg_ref) = refs
        residual = summed - ridge_weight * prev_ref[...].astype(F32)
        direction = residual
        r_ref[...] = residual
    else:
        n_state = 1 if step_index == 1 else 3
        state = refs[:n_state]
        refs = refs[n_state:]
        if step_index == 1:
            residual = direction = state[0][...]
            solution = prev_ref[...].astype(F32)
        else:
            residual, direction, solution = (s[...] for s in state)
        image = summed + ridge_weight * direction
        norm_now = jnp.sum(residual * residual, axis=1, keepdims=True)
        step_size = norm_now / jnp.sum(direction * image, axis=1, keepdims=True)
        solution = solution + step_size * direction
        residual = residual - step_size * image
        norm_next = jnp.sum(residual * residual, axis=1, keepdims=True)
        direction = residual + (norm_next / norm_now) * direction
        if step_index < ITERS - 1:
            r_ref, d_ref, x_ref, msg_ref = refs
            r_ref[...] = residual
        else:
            n_ref, d_ref, x_ref, msg_ref = refs
            n_ref[...] = jnp.broadcast_to(norm_next, n_ref.shape)
        d_ref[...] = direction
        x_ref[...] = solution
    last = step_index == ITERS - 1
    rounded = direction.astype(BF16)
    users = direction.shape[0]
    both = jnp.concatenate([rounded, (direction - rounded.astype(F32)).astype(BF16)], axis=0)
    both = jnp.dot(both, high_ref[...], preferred_element_type=F32)
    image = both[:users] + both[users:] + jnp.dot(rounded, low_ref[...], preferred_element_type=F32)
    if last:
        total = jnp.sum(image * direction, axis=1, keepdims=True)
        squares = jnp.zeros((direction.shape[0], BLOCK), F32)
    for alpha_ref, ref, turned_ref in zip(alphas, picked, turned):
        for p in range(ref.shape[0]):
            for start in range(0, ref.shape[1], BLOCK):
                items = ref[p, start : start + BLOCK, :]
                alpha = alpha_ref[p, :, start : start + BLOCK]
                scores = jnp.dot(
                    rounded, turned_ref[p, :, start : start + BLOCK], preferred_element_type=F32
                )
                weights = (alpha * scores).astype(BF16)
                if last:
                    squares = squares + weights.astype(F32) * scores
                else:
                    image = image + jnp.dot(weights, items, preferred_element_type=F32)
    if last:
        total = total + jnp.sum(squares, axis=1, keepdims=True)
        msg_ref[...] = row_of(total, msg_ref.shape[0])
    else:
        pack(image, msg_ref)


def final_kernel(n_msgs, *refs):
    msgs = refs[:n_msgs]
    n_ref, d_ref, x_ref, out_ref = refs[n_msgs:]
    direction = d_ref[...]
    total = column_of(tree_sum([m[...] for m in msgs])[:1], 128)
    squares = jnp.sum(direction * direction, axis=1, keepdims=True)
    step_size = n_ref[...] / (total + ridge_weight * squares)
    for at in range(0, direction.shape[1], 128):
        out_ref[:, at : at + 128] = x_ref[:, at : at + 128] + step_size * direction[:, at : at + 128]


def permuted(array, axis, size, target):
    return lax.ppermute(array, axis, [(i, target(i)) for i in range(size)])


def tied(array, token):
    return lax.optimization_barrier((array, token))[0]


def gather_stages(own, size, plan, work):
    send = functools.partial(permuted, axis="row", size=size)
    held = {0: own}
    bit = 8 if size >= 8 else 1
    while bit < size:
        held.update({s ^ bit: send(a, target=lambda i: i ^ bit) for s, a in held.items()})
        bit *= 2
    rows = own.shape[1]
    if size < 8:
        plan([[((s, s), 0, rows) for s in held]])
        work(list(held.values()))
        return

    def twin(array):
        return send(array, target=lambda i: i ^ 1)

    def first_way(array):
        return send(array, target=lambda i: i ^ (2 + 2 * (i & 1)))

    def second_way(array):
        return send(array, target=lambda i: i ^ (4 - 2 * (i & 1)))

    half = rows // 2
    whole, upper, lower = (0, rows), (0, half), (half, half)
    kinds = [
        [((0, 0), *whole), ((1, 1), *whole)],
        [((2, 4), *whole), ((5, 3), *whole), ((4, 2), *whole), ((3, 5), *upper), ((3, 5), *lower)],
        [((6, 6), *whole), ((7, 7), *whole)],
    ]
    early = plan([[((s ^ e, s ^ o), at, n) for s in held for (e, o), at, n in kind] for kind in kinds])

    one = [first_way(a) for a in held.values()]
    two = [second_way(tied(a, early)) for a in held.values()]
    token = work([x for a in held.values() for x in (a, twin(a))])
    one = [tied(a, token) for a in one]
    two = [tied(a, token) for a in two]
    far = [second_way(a) for a in one]
    token = work([x for a, b in zip(one, two) for x in (a, twin(a), b, twin(b[:, :half]), twin(b[:, half:]))])
    far = [tied(a, token) for a in far]
    work([x for a in far for x in (a, twin(a))])


def local(mesh, item_factors, tile_counts, observed_tiles, mask_words, confidence, previous):
    n_row, n_col = mesh.shape["row"], mesh.shape["col"]
    tiles, rows, rank = item_factors.shape
    users, obs, width = mask_words.shape
    slots = rows * n_row
    me = lax.axis_index("row").astype(jnp.int32).reshape(1)
    picks = observed_tiles[0]
    conf = confidence[:, None]
    words = jnp.transpose(mask_words, (1, 0, 2)).astype(BF16)
    shape = jax.ShapeDtypeStruct

    message = shape((users, rank), jnp.int16)
    sums = shape((2, users, rank), F32)
    gram_shape = shape((rank, rank), F32)
    stages, picked, turned, alphas, carry = [], [], [], [], []

    def masks_of(plan):
        for stage in plan:
            spot, pieces = 0, []
            for pair, offset, length in stage:
                pieces.append((spot, pair, offset, length))
                spot += length
            stages.append(pieces)
        sizes = [sum(length for _, _, _, length in pieces) for pieces in stages]
        alphas.extend(
            call(
                functools.partial(masks_kernel, stages, rows),
                [shape((obs, users, size), F32) for size in sizes],
                (me, picks, tile_counts, words, conf),
                3,
                2 * obs * users * sum(sizes) * width,
                "masks",
            )
        )
        return alphas

    def work(arrays):
        index = len(picked)
        first, last = index == 0, index == len(stages) - 1
        pieces, alpha = stages[index], alphas[index]
        size = alpha.shape[2]
        split = shape((rank, rank), BF16)
        kept, kept_turned, *carried = call(
            functools.partial(gather_kernel, pieces, rows, first, last),
            [shape((obs, size, rank), BF16), shape((obs, rank, size), BF16)]
            + ([split, split, message] if last else [gram_shape, sums]),
            (me, picks, tile_counts, alpha, conf, previous, *arrays, *carry),
            3,
            2 * size * rank * (tiles * rank + 3 * obs * users),
            "stage",
        )
        carry[:] = carried
        picked.append(kept)
        turned.append(kept_turned)
        return carried, alphas

    gather_stages(item_factors, n_row, masks_of, work)
    high, low, msg = carry

    def to_all(own):
        return [own] + [permuted(own, "col", n_col, lambda i: i ^ bits) for bits in range(1, n_col)]

    vec = shape((users, rank), F32)
    state = []
    for index in range(ITERS):
        last = index == ITERS - 1
        msgs = to_all(msg)
        outs = [vec] if index == 0 else [vec, vec, vec]
        if last:
            outs = [shape((users, 128), F32), vec, vec]
        outs.append(shape((8, users), F32) if last else message)
        *state, msg = call(
            functools.partial(round_kernel, index, n_col, len(picked)),
            outs,
            (*msgs, previous, high, low, *alphas, *picked, *turned, *state),
            0,
            4 * obs * users * slots * rank,
            f"round{index}",
        )
    msgs = to_all(msg)
    (out,) = pl.pallas_call(
        functools.partial(final_kernel, n_col),
        out_shape=[vec],
        in_specs=[VMEM] * (n_col + 3),
        out_specs=[VMEM],
        compiler_params=pltpu.CompilerParams(vmem_limit_bytes=4 * 1024 * 1024),
        name="final",
    )(*msgs, *state)
    return out


def solution(mesh):
    return jax.shard_map(
        functools.partial(local, mesh),
        mesh=mesh,
        in_specs=(
            P("col", "row", None),
            P("col"),
            P("row", "col"),
            P("row", "col", None),
            P("row"),
            P("row", None),
        ),
        out_specs=P("row", None),
        check_vma=False,
    )
```

time: 83.8 us -> 63.3 us (0.76)
  waiting for transfers between devices: 37.1 us -> 23 us
  Pallas kernels: 15.1 us -> 11.1 us
  local copies, waits for them, and re-layouts: 4.62 us -> 1.45 us
    ppermute x21 -> x20, waiting for transfers between devices: 37.1 us -> 23 us  [permuted(): return lax.ppermute(array, axis, [(i, target(i)) for i in range(size)])]
    pallas_call x7, Pallas kernels: 13.2 us -> 10.3 us  [call(): pl.pallas_call(body, out_shape=[pltpu.VMEM(o.shape, o.dtype) for o in out...]
    unnamed x22 -> x10, local copies, waits for them, and re-layouts: 3.82 us -> 1.31 us
    pallas_call x1, Pallas kernels: 1.82 us -> 0.81 us  [local(): pl.pallas_call(functools.partial(final_kernel, n_col), out_shape=[vec], i...]
    ppermute x21 -> x20, starting transfers between devices: 25.8 us -> 26.5 us  [permuted(): return lax.ppermute(array, axis, [(i, target(i)) for i in range(size)])]
  transfers between devices with their start and end apart: 21 -> 20, of which waited for: 12 -> 14; matrix products, arithmetic and copies ran while one was open for 2% -> 2% of each run, Pallas kernels for 6% -> 8%
where the time goes in v2:
time: 63.3 us; the launch traced here: 63.1 us
  starting transfers between devices  26.5 us (42%)
  waiting for transfers between devices  23 us (36%)
  Pallas kernels  11.1 us (18%)
  local copies, waits for them, and re-layouts  1.45 us (2%)
  other arithmetic  0.97 us (2%)
    ppermute x20, starting transfers between devices, permuted(): return lax.ppermute(array, axis, [(i, target(i)) for i in range(size)])  26.5 us
    ppermute x20, waiting for transfers between devices, permuted(): return lax.ppermute(array, axis, [(i, target(i)) for i in range(size)])  23 us
    pallas_call x7, Pallas kernels, call(): pl.pallas_call(body, out_shape=[pltpu.VMEM(o.shape, o.dtype) for o in out...  10.3 us
    unnamed x10, local copies, waits for them, and re-layouts  1.31 us
  transfers between devices with their start and end apart: 20, of which 14 were waited for; matrix products, arithmetic and copies ran while one was open for 2% of the time, Pallas kernels for 8%

profile of v2, /device:TPU:0, one launch (start us, length us, event | category | flops | bytes accessed | tf_op | source)
XLA Modules:
  0.0 63.1 jit_solution(18365458984760749149)
XLA Ops:
  0.5 2.5 %collective-permute-start = (bf16[4,256,256]{2,1,0:T(8,128)(2,1)}, bf16[4,256,256]{2,1,0:T(8,128)(2,1)S(1)}, u32[]{:S(2)}, u32[]{:S(2)}) collective-permute-start(bf16[4,256,256]{2,1,0:T(8,128)(2,1)} %refs_6_.1), channel_id=1, source_target_pairs={{0,8},{4,20},{8,0},{12,28},{16,24},{20,4},{24,16},{28,12},{1,9},{5... | collective-permute-start | bytes 1572872 | tf_op jit(solution)/shard_map/ppermute | solution.py:240
  5.4 1.3 %masks.1 = (f32[2,128,512]{2,1,0:T(8,128)S(1)}, f32[2,128,1024]{2,1,0:T(8,128)S(1)}, f32[2,128,512]{2,1,0:T(8,128)S(1)}) custom-call(s32[1]{0:T(128)} %bitcast.me_ref.refs_0_, s32[2]{0:T(128)S(1)} %bitcast.5, s32[4]{0:T(128)S(1)} %copy-done.2, bf16[2,128,256]{2,1,0:T(8,128)(2,1)S(1)} %fusion.words_ref, f32[128,1]{1,0:T(8,128)S(1)} %copy.8.conf_ref.refs_4_), custom_call_target="tpu_custom_call" | custom-call | flops 268435456 | bytes 1048576 | tf_op jit(solution)/shard_map/masks/pallas_call | solution.py:21
  6.7 1.6 %collective-permute-start.4 = (bf16[4,256,256]{2,1,0:T(8,128)(2,1)S(1)}, bf16[4,256,256]{2,1,0:T(8,128)(2,1)S(1)}, u32[]{:S(2)}, u32[]{:S(2)}) collective-permute-start(bf16[4,256,256]{2,1,0:T(8,128)(2,1)S(1)} %copy-done.3), channel_id=1, source_target_pairs={{0,16},{4,12},{8,24},{12,4},{16,0},{20,28},{24,8},{28,20},{1,17},{... | collective-permute-start | bytes 1572872 | tf_op jit(solution)/shard_map/ppermute | solution.py:240
  8.3 1.4 %stage.3 = (bf16[2,512,256]{2,1,0:T(8,128)(2,1)S(1)}, bf16[2,256,512]{2,1,0:T(8,128)(2,1)S(1)}, f32[256,256]{1,0:T(8,128)S(1)}, f32[2,128,256]{2,1,0:T(8,128)S(1)}) custom-call(s32[1]{0:T(128)} %bitcast.me_ref.refs_0_, s32[2]{0:T(128)S(1)} %bitcast.6, s32[4]{0:T(128)S(1)} %copy-done.2, f32[2,128,512]{2,1,0:T(8,128)S(1)} %get-tuple-element.36.refs_3_.refs_7_, ...), custom_call_target="tpu_custom_call" | custom-call | flops 469762048 | bytes 1048576 | tf_op jit(solution)/shard_map/stage/pallas_call | solution.py:21
  9.7 1.3 %collective-permute-done.refs_6_ = bf16[4,256,256]{2,1,0:T(8,128)(2,1)S(1)} collective-permute-done((bf16[4,256,256]{2,1,0:T(8,128)(2,1)}, bf16[4,256,256]{2,1,0:T(8,128)(2,1)S(1)}, u32[]{:S(2)}, u32[]{:S(2)}) %collective-permute-start) | collective-permute-done | bytes 524320 | tf_op jit(solution)/shard_map/ppermute | solution.py:240
  11.1 3.6 %collective-permute-start.2 = (bf16[4,256,256]{2,1,0:T(8,128)(2,1)S(1)}, bf16[4,256,256]{2,1,0:T(8,128)(2,1)S(1)}, u32[]{:S(2)}, u32[]{:S(2)}) collective-permute-start(bf16[4,256,256]{2,1,0:T(8,128)(2,1)S(1)} %collective-permute-done.refs_6_), channel_id=1, source_target_pairs={{0,16},{4,12},{8,24},{12,4},{16,0},{20,28},{24,8},{28,20},{1,17},{... | collective-permute-start | bytes 1572872 | tf_op jit(solution)/shard_map/ppermute | solution.py:240
  18.0 2.4 %stage.4 = (bf16[2,1024,256]{2,1,0:T(8,128)(2,1)S(1)}, bf16[2,256,1024]{2,1,0:T(8,128)(2,1)S(1)}, f32[256,256]{1,0:T(8,128)S(1)}, f32[2,128,256]{2,1,0:T(8,128)S(1)}) custom-call(s32[1]{0:T(128)} %bitcast.me_ref.refs_0_, s32[2]{0:T(128)S(1)} %bitcast.7, s32[4]{0:T(128)S(1)} %copy-done.2, f32[2,128,1024]{2,1,0:T(8,128)S(1)} %get-tuple-element.39.refs_3_.refs_8_, ...), custom_call_target="tpu_custom_call" | custom-call | flops 939524096 | bytes 1048576 | tf_op jit(solution)/shard_map/stage/pallas_call | solution.py:21
  20.4 1.5 %collective-permute-done.2.refs_6_ = bf16[4,256,256]{2,1,0:T(8,128)(2,1)S(1)} collective-permute-done((bf16[4,256,256]{2,1,0:T(8,128)(2,1)S(1)}, bf16[4,256,256]{2,1,0:T(8,128)(2,1)S(1)}, u32[]{:S(2)}, u32[]{:S(2)}) %collective-permute-start.2) | collective-permute-done | bytes 524320 | tf_op jit(solution)/shard_map/ppermute | solution.py:240
  21.9 1.9 %collective-permute-done.7.refs_7_ = bf16[4,256,256]{2,1,0:T(8,128)(2,1)S(1)} collective-permute-done((bf16[4,256,256]{2,1,0:T(8,128)(2,1)S(1)}, bf16[4,256,256]{2,1,0:T(8,128)(2,1)S(1)}, u32[]{:S(2)}, u32[]{:S(2)}) %collective-permute-start.7) | collective-permute-done | bytes 524320 | tf_op jit(solution)/shard_map/ppermute | solution.py:240
  23.8 1.7 %stage.5 = (bf16[2,512,256]{2,1,0:T(8,128)(2,1)S(1)}, bf16[2,256,512]{2,1,0:T(8,128)(2,1)S(1)}, bf16[256,256]{1,0:T(8,128)(2,1)S(1)}, bf16[256,256]{1,0:T(8,128)(2,1)S(1)}, s16[128,256]{1,0:T(8,128)(2,1)S(1)}) custom-call(s32[1]{0:T(128)} %bitcast.me_ref.refs_0_, s32[2]{0:T(128)S(1)} %bitcast.8, s32[4]{0:T(128)S(1)} %copy-done.2, ...), custom_call_target="tpu_custom_call" | custom-call | flops 469762048 | bytes 1048576 | tf_op jit(solution)/shard_map/stage/pallas_call | solution.py:21
  25.5 3.4 %collective-permute-start.10 = (s16[128,256]{1,0:T(8,128)(2,1)S(1)}, s16[128,256]{1,0:T(8,128)(2,1)S(1)}, u32[]{:S(2)}, u32[]{:S(2)}) collective-permute-start(s16[128,256]{1,0:T(8,128)(2,1)S(1)} %get-tuple-element.46.refs_0_), channel_id=1, source_target_pairs={{0,3},{1,2},{2,1},{3,0},{4,7},{5,6},{6,5},{7,4},{8,11},{9,10},{10,... | collective-permute-start | bytes 196616 | tf_op jit(solution)/shard_map/ppermute | solution.py:240
  29.9 2.1 %collective-permute-done.10.refs_3_ = s16[128,256]{1,0:T(8,128)(2,1)S(1)} collective-permute-done((s16[128,256]{1,0:T(8,128)(2,1)S(1)}, s16[128,256]{1,0:T(8,128)(2,1)S(1)}, u32[]{:S(2)}, u32[]{:S(2)}) %collective-permute-start.10) | collective-permute-done | bytes 65568 | tf_op jit(solution)/shard_map/ppermute | solution.py:240
  32.0 2.8 %collective-permute-done.9.refs_2_ = s16[128,256]{1,0:T(8,128)(2,1)S(1)} collective-permute-done((s16[128,256]{1,0:T(8,128)(2,1)S(1)}, s16[128,256]{1,0:T(8,128)(2,1)S(1)}, u32[]{:S(2)}, u32[]{:S(2)}) %collective-permute-start.9) | collective-permute-done | bytes 65568 | tf_op jit(solution)/shard_map/ppermute | solution.py:240
  36.0 2.5 %collective-permute-start.13 = (s16[128,256]{1,0:T(8,128)(2,1)S(1)}, s16[128,256]{1,0:T(8,128)(2,1)S(1)}, u32[]{:S(2)}, u32[]{:S(2)}) collective-permute-start(s16[128,256]{1,0:T(8,128)(2,1)S(1)} %get-tuple-element.55.refs_0_), channel_id=1, source_target_pairs={{0,3},{1,2},{2,1},{3,0},{4,7},{5,6},{6,5},{7,4},{8,11},{9,10},{10,... | collective-permute-start | bytes 196616 | tf_op jit(solution)/shard_map/ppermute | solution.py:240
  38.7 1.7 %collective-permute-start.11 = (s16[128,256]{1,0:T(8,128)(2,1)S(1)}, s16[128,256]{1,0:T(8,128)(2,1)S(1)}, u32[]{:S(2)}, u32[]{:S(2)}) collective-permute-start(s16[128,256]{1,0:T(8,128)(2,1)S(1)} %get-tuple-element.55.refs_0_), channel_id=1, source_target_pairs={{0,1},{1,0},{2,3},{3,2},{4,5},{5,4},{6,7},{7,6},{8,9},{9,8},{10,11... | collective-permute-start | bytes 196616 | tf_op jit(solution)/shard_map/ppermute | solution.py:240
  40.4 2.1 %collective-permute-done.13.refs_3_ = s16[128,256]{1,0:T(8,128)(2,1)S(1)} collective-permute-done((s16[128,256]{1,0:T(8,128)(2,1)S(1)}, s16[128,256]{1,0:T(8,128)(2,1)S(1)}, u32[]{:S(2)}, u32[]{:S(2)}) %collective-permute-start.13) | collective-permute-done | bytes 65568 | tf_op jit(solution)/shard_map/ppermute | solution.py:240
  42.5 2.6 %collective-permute-done.12.refs_2_ = s16[128,256]{1,0:T(8,128)(2,1)S(1)} collective-permute-done((s16[128,256]{1,0:T(8,128)(2,1)S(1)}, s16[128,256]{1,0:T(8,128)(2,1)S(1)}, u32[]{:S(2)}, u32[]{:S(2)}) %collective-permute-start.12) | collective-permute-done | bytes 65568 | tf_op jit(solution)/shard_map/ppermute | solution.py:240
  45.1 1.3 %round1.1 = (f32[128,256]{1,0:T(8,128)S(1)}, f32[128,256]{1,0:T(8,128)S(1)}, f32[128,256]{1,0:T(8,128)S(1)}, s16[128,256]{1,0:T(8,128)(2,1)S(1)}) custom-call(s16[128,256]{1,0:T(8,128)(2,1)S(1)} %get-tuple-element.55.refs_0_, s16[128,256]{1,0:T(8,128)(2,1)S(1)} %collective-permute-done.11.refs_1_, s16[128,256]{1,0:T(8,128)(2,1)S(1)} %collective-permute-done.12.refs_2_, ...), custom_call_target="tpu_custom_call" | custom-call | flops 536870912 | bytes 1048576 | tf_op jit(solution)/shard_map/round1/pallas_call | solution.py:21
  46.4 1.7 %collective-permute-start.16 = (s16[128,256]{1,0:T(8,128)(2,1)S(1)}, s16[128,256]{1,0:T(8,128)(2,1)S(1)}, u32[]{:S(2)}, u32[]{:S(2)}) collective-permute-start(s16[128,256]{1,0:T(8,128)(2,1)S(1)} %get-tuple-element.57.refs_0_), channel_id=1, source_target_pairs={{0,3},{1,2},{2,1},{3,0},{4,7},{5,6},{6,5},{7,4},{8,11},{9,10},{10,... | collective-permute-start | bytes 196616 | tf_op jit(solution)/shard_map/ppermute | solution.py:240
  48.2 2.7 %collective-permute-start.14 = (s16[128,256]{1,0:T(8,128)(2,1)S(1)}, s16[128,256]{1,0:T(8,128)(2,1)S(1)}, u32[]{:S(2)}, u32[]{:S(2)}) collective-permute-start(s16[128,256]{1,0:T(8,128)(2,1)S(1)} %get-tuple-element.57.refs_0_), channel_id=1, source_target_pairs={{0,1},{1,0},{2,3},{3,2},{4,5},{5,4},{6,7},{7,6},{8,9},{9,8},{10,11... | collective-permute-start | bytes 196616 | tf_op jit(solution)/shard_map/ppermute | solution.py:240
  50.9 1.8 %collective-permute-done.16.refs_3_ = s16[128,256]{1,0:T(8,128)(2,1)S(1)} collective-permute-done((s16[128,256]{1,0:T(8,128)(2,1)S(1)}, s16[128,256]{1,0:T(8,128)(2,1)S(1)}, u32[]{:S(2)}, u32[]{:S(2)}) %collective-permute-start.16) | collective-permute-done | bytes 65568 | tf_op jit(solution)/shard_map/ppermute | solution.py:240
  52.7 2.0 %collective-permute-done.15.refs_2_ = s16[128,256]{1,0:T(8,128)(2,1)S(1)} collective-permute-done((s16[128,256]{1,0:T(8,128)(2,1)S(1)}, s16[128,256]{1,0:T(8,128)(2,1)S(1)}, u32[]{:S(2)}, u32[]{:S(2)}) %collective-permute-start.15) | collective-permute-done | bytes 65568 | tf_op jit(solution)/shard_map/ppermute | solution.py:240
  55.7 2.1 %collective-permute-start.19 = (f32[8,128]{1,0:T(8,128)S(1)}, f32[8,128]{1,0:T(8,128)S(1)}, u32[]{:S(2)}, u32[]{:S(2)}) collective-permute-start(f32[8,128]{1,0:T(8,128)S(1)} %get-tuple-element.61.refs_0_), channel_id=1, source_target_pairs={{0,3},{1,2},{2,1},{3,0},{4,7},{5,6},{6,5},{7,4},{8,11},{9,10},{10,... | collective-permute-start | bytes 12296 | tf_op jit(solution)/shard_map/ppermute | solution.py:240
  57.8 2.3 %collective-permute-start.17 = (f32[8,128]{1,0:T(8,128)S(1)}, f32[8,128]{1,0:T(8,128)S(1)}, u32[]{:S(2)}, u32[]{:S(2)}) collective-permute-start(f32[8,128]{1,0:T(8,128)S(1)} %get-tuple-element.61.refs_0_), channel_id=1, source_target_pairs={{0,1},{1,0},{2,3},{3,2},{4,5},{5,4},{6,7},{7,6},{8,9},{9,8},{10,11... | collective-permute-start | bytes 12296 | tf_op jit(solution)/shard_map/ppermute | solution.py:240
  (37 shorter events, 12.5 us)
Async XLA Ops:
  0.0 8.3 %collective-permute-start.1 = (bf16[4,256,256]{2,1,0:T(8,128)(2,1)}, bf16[4,256,256]{2,1,0:T(8,128)(2,1)S(1)}, u32[]{:S(2)}, u32[]{:S(2)}) collective-permute-start(bf16[4,256,256]{2,1,0:T(8,128)(2,1)} %refs_6_.1), channel_id=1, source_target_pairs={{0,4},{4,0},{8,12},{12,8},{16,20},{20,16},{24,28},{28,24},{1,5},{5... | collective-permute-start | bytes 1572872 | tf_op jit(solution)/shard_map/ppermute | solution.py:240
  0.5 10.6 %collective-permute-start = (bf16[4,256,256]{2,1,0:T(8,128)(2,1)}, bf16[4,256,256]{2,1,0:T(8,128)(2,1)S(1)}, u32[]{:S(2)}, u32[]{:S(2)}) collective-permute-start(bf16[4,256,256]{2,1,0:T(8,128)(2,1)} %refs_6_.1), channel_id=1, source_target_pairs={{0,8},{4,20},{8,0},{12,28},{16,24},{20,4},{24,16},{28,12},{1,9},{5... | collective-permute-start | bytes 1572872 | tf_op jit(solution)/shard_map/ppermute | solution.py:240
  3.9 0.7 %copy-start.4 = (f32[128]{0:T(128)S(1)}, f32[128]{0:T(128)}, u32[]{:S(2)}) copy-start(f32[128]{0:T(128)} %param.10) | copy-start | bytes 1540
  4.7 0.7 %copy-start.2 = (s32[4]{0:T(128)S(1)}, s32[4]{0:T(128)}, u32[]{:S(2)}) copy-start(s32[4]{0:T(128)} %refs_2_.5) | copy-start | bytes 52
  4.7 2.0 %copy-start.3 = (bf16[4,256,256]{2,1,0:T(8,128)(2,1)S(1)}, bf16[4,256,256]{2,1,0:T(8,128)(2,1)}, u32[]{:S(2)}) copy-start(bf16[4,256,256]{2,1,0:T(8,128)(2,1)} %refs_6_.1) | copy-start | bytes 1572868
  5.4 3.0 %copy-start = (bf16[128,256]{1,0:T(8,128)(2,1)S(1)}, bf16[128,256]{1,0:T(8,128)(2,1)}, u32[]{:S(2)}) copy-start(bf16[128,256]{1,0:T(8,128)(2,1)} %refs_4_.5) | copy-start | bytes 196612
  6.7 9.2 %collective-permute-start.4 = (bf16[4,256,256]{2,1,0:T(8,128)(2,1)S(1)}, bf16[4,256,256]{2,1,0:T(8,128)(2,1)S(1)}, u32[]{:S(2)}, u32[]{:S(2)}) collective-permute-start(bf16[4,256,256]{2,1,0:T(8,128)(2,1)S(1)} %copy-done.3), channel_id=1, source_target_pairs={{0,16},{4,12},{8,24},{12,4},{16,0},{20,28},{24,8},{28,20},{1,17},{... | collective-permute-start | bytes 1572872 | tf_op jit(solution)/shard_map/ppermute | solution.py:240
  11.1 6.9 %collective-permute-start.3 = (bf16[4,256,256]{2,1,0:T(8,128)(2,1)S(1)}, bf16[4,256,256]{2,1,0:T(8,128)(2,1)S(1)}, u32[]{:S(2)}, u32[]{:S(2)}) collective-permute-start(bf16[4,256,256]{2,1,0:T(8,128)(2,1)S(1)} %collective-permute-done.refs_6_), channel_id=1, source_target_pairs={{0,4},{4,0},{8,12},{12,8},{16,20},{20,16},{24,28},{28,24},{1,5},{5... | collective-permute-start | bytes 1572872 | tf_op jit(solution)/shard_map/ppermute | solution.py:240
  11.1 10.8 %collective-permute-start.2 = (bf16[4,256,256]{2,1,0:T(8,128)(2,1)S(1)}, bf16[4,256,256]{2,1,0:T(8,128)(2,1)S(1)}, u32[]{:S(2)}, u32[]{:S(2)}) collective-permute-start(bf16[4,256,256]{2,1,0:T(8,128)(2,1)S(1)} %collective-permute-done.refs_6_), channel_id=1, source_target_pairs={{0,16},{4,12},{8,24},{12,4},{16,0},{20,28},{24,8},{28,20},{1,17},{... | collective-permute-start | bytes 1572872 | tf_op jit(solution)/shard_map/ppermute | solution.py:240
  16.0 1.6 %collective-permute-start.6 = (bf16[4,128,256]{2,1,0:T(8,128)(2,1)S(1)}, bf16[4,128,256]{2,1,0:T(8,128)(2,1)S(1)}, u32[]{:S(2)}, u32[]{:S(2)}) collective-permute-start(bf16[4,128,256]{2,1,0:T(8,128)(2,1)S(1)} %get-tuple-element.65), channel_id=1, source_target_pairs={{0,4},{4,0},{8,12},{12,8},{16,20},{20,16},{24,28},{28,24},{1,5},{5... | collective-permute-start | bytes 786440 | tf_op jit(solution)/shard_map/ppermute | solution.py:240
  16.1 1.8 %collective-permute-start.5 = (bf16[4,128,256]{2,1,0:T(8,128)(2,1)S(1)}, bf16[4,128,256]{2,1,0:T(8,128)(2,1)S(1)}, u32[]{:S(2)}, u32[]{:S(2)}) collective-permute-start(bf16[4,128,256]{2,1,0:T(8,128)(2,1)S(1)} %get-tuple-element.66), channel_id=1, source_target_pairs={{0,4},{4,0},{8,12},{12,8},{16,20},{20,16},{24,28},{28,24},{1,5},{5... | collective-permute-start | bytes 786440 | tf_op jit(solution)/shard_map/ppermute | solution.py:240
  21.9 1.9 %collective-permute-start.7 = (bf16[4,256,256]{2,1,0:T(8,128)(2,1)S(1)}, bf16[4,256,256]{2,1,0:T(8,128)(2,1)S(1)}, u32[]{:S(2)}, u32[]{:S(2)}) collective-permute-start(bf16[4,256,256]{2,1,0:T(8,128)(2,1)S(1)} %collective-permute-done.2.refs_6_), channel_id=1, source_target_pairs={{0,4},{4,0},{8,12},{12,8},{16,20},{20,16},{24,28},{28,24},{1,5},{5... | collective-permute-start | bytes 1572872 | tf_op jit(solution)/shard_map/ppermute | solution.py:240
  25.5 6.5 %collective-permute-start.10 = (s16[128,256]{1,0:T(8,128)(2,1)S(1)}, s16[128,256]{1,0:T(8,128)(2,1)S(1)}, u32[]{:S(2)}, u32[]{:S(2)}) collective-permute-start(s16[128,256]{1,0:T(8,128)(2,1)S(1)} %get-tuple-element.46.refs_0_), channel_id=1, source_target_pairs={{0,3},{1,2},{2,1},{3,0},{4,7},{5,6},{6,5},{7,4},{8,11},{9,10},{10,... | collective-permute-start | bytes 196616 | tf_op jit(solution)/shard_map/ppermute | solution.py:240
  28.9 5.9 %collective-permute-start.9 = (s16[128,256]{1,0:T(8,128)(2,1)S(1)}, s16[128,256]{1,0:T(8,128)(2,1)S(1)}, u32[]{:S(2)}, u32[]{:S(2)}) collective-permute-start(s16[128,256]{1,0:T(8,128)(2,1)S(1)} %get-tuple-element.46.refs_0_), channel_id=1, source_target_pairs={{0,2},{1,3},{2,0},{3,1},{4,6},{5,7},{6,4},{7,5},{8,10},{9,11},{10,... | collective-permute-start | bytes 196616 | tf_op jit(solution)/shard_map/ppermute | solution.py:240
  28.9 5.9 %collective-permute-start.8 = (s16[128,256]{1,0:T(8,128)(2,1)S(1)}, s16[128,256]{1,0:T(8,128)(2,1)S(1)}, u32[]{:S(2)}, u32[]{:S(2)}) collective-permute-start(s16[128,256]{1,0:T(8,128)(2,1)S(1)} %get-tuple-element.46.refs_0_), channel_id=1, source_target_pairs={{0,1},{1,0},{2,3},{3,2},{4,5},{5,4},{6,7},{7,6},{8,9},{9,8},{10,11... | collective-permute-start | bytes 196616 | tf_op jit(solution)/shard_map/ppermute | solution.py:240
  36.0 6.6 %collective-permute-start.13 = (s16[128,256]{1,0:T(8,128)(2,1)S(1)}, s16[128,256]{1,0:T(8,128)(2,1)S(1)}, u32[]{:S(2)}, u32[]{:S(2)}) collective-permute-start(s16[128,256]{1,0:T(8,128)(2,1)S(1)} %get-tuple-element.55.refs_0_), channel_id=1, source_target_pairs={{0,3},{1,2},{2,1},{3,0},{4,7},{5,6},{6,5},{7,4},{8,11},{9,10},{10,... | collective-permute-start | bytes 196616 | tf_op jit(solution)/shard_map/ppermute | solution.py:240
  38.5 6.6 %collective-permute-start.12 = (s16[128,256]{1,0:T(8,128)(2,1)S(1)}, s16[128,256]{1,0:T(8,128)(2,1)S(1)}, u32[]{:S(2)}, u32[]{:S(2)}) collective-permute-start(s16[128,256]{1,0:T(8,128)(2,1)S(1)} %get-tuple-element.55.refs_0_), channel_id=1, source_target_pairs={{0,2},{1,3},{2,0},{3,1},{4,6},{5,7},{6,4},{7,5},{8,10},{9,11},{10,... | collective-permute-start | bytes 196616 | tf_op jit(solution)/shard_map/ppermute | solution.py:240
  38.7 6.5 %collective-permute-start.11 = (s16[128,256]{1,0:T(8,128)(2,1)S(1)}, s16[128,256]{1,0:T(8,128)(2,1)S(1)}, u32[]{:S(2)}, u32[]{:S(2)}) collective-permute-start(s16[128,256]{1,0:T(8,128)(2,1)S(1)} %get-tuple-element.55.refs_0_), channel_id=1, source_target_pairs={{0,1},{1,0},{2,3},{3,2},{4,5},{5,4},{6,7},{7,6},{8,9},{9,8},{10,11... | collective-permute-start | bytes 196616 | tf_op jit(solution)/shard_map/ppermute | solution.py:240
  46.4 6.3 %collective-permute-start.16 = (s16[128,256]{1,0:T(8,128)(2,1)S(1)}, s16[128,256]{1,0:T(8,128)(2,1)S(1)}, u32[]{:S(2)}, u32[]{:S(2)}) collective-permute-start(s16[128,256]{1,0:T(8,128)(2,1)S(1)} %get-tuple-element.57.refs_0_), channel_id=1, source_target_pairs={{0,3},{1,2},{2,1},{3,0},{4,7},{5,6},{6,5},{7,4},{8,11},{9,10},{10,... | collective-permute-start | bytes 196616 | tf_op jit(solution)/shard_map/ppermute | solution.py:240
  48.2 6.5 %collective-permute-start.15 = (s16[128,256]{1,0:T(8,128)(2,1)S(1)}, s16[128,256]{1,0:T(8,128)(2,1)S(1)}, u32[]{:S(2)}, u32[]{:S(2)}) collective-permute-start(s16[128,256]{1,0:T(8,128)(2,1)S(1)} %get-tuple-element.57.refs_0_), channel_id=1, source_target_pairs={{0,2},{1,3},{2,0},{3,1},{4,6},{5,7},{6,4},{7,5},{8,10},{9,11},{10,... | collective-permute-start | bytes 196616 | tf_op jit(solution)/shard_map/ppermute | solution.py:240
  48.2 6.5 %collective-permute-start.14 = (s16[128,256]{1,0:T(8,128)(2,1)S(1)}, s16[128,256]{1,0:T(8,128)(2,1)S(1)}, u32[]{:S(2)}, u32[]{:S(2)}) collective-permute-start(s16[128,256]{1,0:T(8,128)(2,1)S(1)} %get-tuple-element.57.refs_0_), channel_id=1, source_target_pairs={{0,1},{1,0},{2,3},{3,2},{4,5},{5,4},{6,7},{7,6},{8,9},{9,8},{10,11... | collective-permute-start | bytes 196616 | tf_op jit(solution)/shard_map/ppermute | solution.py:240
  55.7 5.4 %collective-permute-start.19 = (f32[8,128]{1,0:T(8,128)S(1)}, f32[8,128]{1,0:T(8,128)S(1)}, u32[]{:S(2)}, u32[]{:S(2)}) collective-permute-start(f32[8,128]{1,0:T(8,128)S(1)} %get-tuple-element.61.refs_0_), channel_id=1, source_target_pairs={{0,3},{1,2},{2,1},{3,0},{4,7},{5,6},{6,5},{7,4},{8,11},{9,10},{10,... | collective-permute-start | bytes 12296 | tf_op jit(solution)/shard_map/ppermute | solution.py:240
  57.8 4.5 %collective-permute-start.18 = (f32[8,128]{1,0:T(8,128)S(1)}, f32[8,128]{1,0:T(8,128)S(1)}, u32[]{:S(2)}, u32[]{:S(2)}) collective-permute-start(f32[8,128]{1,0:T(8,128)S(1)} %get-tuple-element.61.refs_0_), channel_id=1, source_target_pairs={{0,2},{1,3},{2,0},{3,1},{4,6},{5,7},{6,4},{7,5},{8,10},{9,11},{10,... | collective-permute-start | bytes 12296 | tf_op jit(solution)/shard_map/ppermute | solution.py:240
  57.8 4.5 %collective-permute-start.17 = (f32[8,128]{1,0:T(8,128)S(1)}, f32[8,128]{1,0:T(8,128)S(1)}, u32[]{:S(2)}, u32[]{:S(2)}) collective-permute-start(f32[8,128]{1,0:T(8,128)S(1)} %get-tuple-element.61.refs_0_), channel_id=1, source_target_pairs={{0,1},{1,0},{2,3},{3,2},{4,5},{5,4},{6,7},{7,6},{8,9},{9,8},{10,11... | collective-permute-start | bytes 12296 | tf_op jit(solution)/shard_map/ppermute | solution.py:240
  (1 other events, 0.7 us)

commit v3 on v2

--- a/solution.py
+++ b/solution.py
@@ -17,16 +17,17 @@
 BF16 = jnp.bfloat16
 
 
-def call(body, outs, args, n_smem, flops, name):
+def call(body, outs, args, n_smem, flops, name, scalars=()):
+    kept = [pltpu.with_memory_space_constraint(a, pltpu.SMEM) for a in args[:n_smem]]
     return pl.pallas_call(
         body,
-        out_shape=[pltpu.VMEM(o.shape, o.dtype) for o in outs],
+        out_shape=[pltpu.VMEM(o.shape, o.dtype) for o in outs] + [pltpu.SMEM(o.shape, o.dtype) for o in scalars],
         in_specs=[SMEM] * n_smem + [VMEM] * (len(args) - n_smem),
-        out_specs=[VMEM] * len(outs),
+        out_specs=[VMEM] * len(outs) + [SMEM] * len(scalars),
         compiler_params=pltpu.CompilerParams(vmem_limit_bytes=24 * 1024 * 1024),
         cost_estimate=pl.CostEstimate(flops=flops, bytes_accessed=1 << 20, transcendentals=0),
         name=name,
-    )(*args)
+    )(*kept, *args[n_smem:])
 
 
 def column_of(row_values, lanes):
@@ -77,8 +78,11 @@
     return me ^ (even + (me & 1) * (odd - even))
 
 
-def masks_kernel(stages, rows, me_ref, picks_ref, counts_ref, words_ref, conf_ref, *out_refs):
-    me = me_ref[0]
+def masks_kernel(stages, rows, info_ref, words_ref, conf_ref, *out_refs):
+    *out_refs, kept_ref = out_refs
+    for index in range(info_ref.shape[0]):
+        kept_ref[index] = info_ref[index]
+    me = info_ref[0]
     obs, _, width = words_ref.shape
     lane = lax.broadcasted_iota(jnp.int32, (1, BLOCK), 1)
     word_index = lax.broadcasted_iota(jnp.int32, (width, BLOCK), 0)
@@ -91,7 +95,7 @@
                     slot = jnp.where(lane >= spot - at, lane + start, slot)
             spread = (word_index == jnp.right_shift(slot, 3)).astype(BF16)
             for p in range(obs):
-                count = counts_ref[picks_ref[p]]
+                count = info_ref[1 + obs + info_ref[1 + p]]
                 word = jnp.dot(words_ref[p], spread, preferred_element_type=F32).astype(jnp.int32)
                 bits = jnp.right_shift(word, slot & 7) & 1
                 bits = jnp.where(slot < count, bits, 0).astype(F32)
@@ -99,8 +103,8 @@
 
 
 def gather_kernel(pieces, rows, first, last, *refs):
-    me_ref, picks_ref, counts_ref, alpha_ref, conf_ref, prev_ref = refs[:6]
-    at = 6
+    info_ref, alpha_ref, conf_ref, prev_ref = refs[:4]
+    at = 4
     arrays = refs[at : at + len(pieces)]
     at += len(pieces)
     if not first:
@@ -112,12 +116,12 @@
         high_ref, low_ref, msg_ref = refs[at:]
     else:
         gram_ref, sums_ref = refs[at:]
-    me = me_ref[0]
+    me = info_ref[0]
     users, rank = prev_ref.shape
     obs = alpha_ref.shape[0]
     tiles = arrays[0].shape[0]
     for p in range(obs):
-        tile = picks_ref[p]
+        tile = info_ref[1 + p]
         for (spot, _, _, length), ref in zip(pieces, arrays):
             picked_ref[p, spot : spot + length, :] = ref[tile]
     gram = jnp.zeros((rank, rank), F32) if first else gram_in[...]
@@ -126,7 +130,7 @@
         slot = slot + (shard_index(me, pair) * rows + offset)
         for t in range(tiles):
             tile_rows = ref[t]
-            masked = jnp.where(slot < counts_ref[t], tile_rows, jnp.zeros_like(tile_rows))
+            masked = jnp.where(slot < info_ref[1 + obs + t], tile_rows, jnp.zeros_like(tile_rows))
             gram = gram + lax.dot_general(
                 masked, tile_rows, (((0,), (0,)), ((), ())), preferred_element_type=F32
             )
@@ -160,9 +164,13 @@
         sums_ref[1] = image
 
 
-def round_kernel(step_index, n_msgs, n_stages, *refs):
-    msgs = refs[:n_msgs]
-    refs = refs[n_msgs:]
+def in_order(refs, order):
+    return [refs[order.index(bits)] for bits in range(len(order))]
+
+
+def round_kernel(step_index, order, n_stages, *refs):
+    msgs = in_order(refs, order)
+    refs = refs[len(order) :]
     prev_ref, high_ref, low_ref = refs[:3]
     alphas, picked, turned = (refs[3 + n * n_stages : 3 + (n + 1) * n_stages] for n in range(3))
     refs = refs[3 + 3 * n_stages :]
@@ -225,9 +233,9 @@
         pack(image, msg_ref)
 
 
-def final_kernel(n_msgs, *refs):
-    msgs = refs[:n_msgs]
-    n_ref, d_ref, x_ref, out_ref = refs[n_msgs:]
+def final_kernel(order, *refs):
+    msgs = in_order(refs, order)
+    n_ref, d_ref, x_ref, out_ref = refs[len(order) :]
     direction = d_ref[...]
     total = column_of(tree_sum([m[...] for m in msgs])[:1], 128)
     squares = jnp.sum(direction * direction, axis=1, keepdims=True)
@@ -270,8 +278,9 @@
     whole, upper, lower = (0, rows), (0, half), (half, half)
     kinds = [
         [((0, 0), *whole), ((1, 1), *whole)],
-        [((2, 4), *whole), ((5, 3), *whole), ((4, 2), *whole), ((3, 5), *upper), ((3, 5), *lower)],
-        [((6, 6), *whole), ((7, 7), *whole)],
+        [((2, 4), *whole), ((5, 3), *upper), ((5, 3), *lower), ((4, 2), *whole), ((3, 5), *upper), ((3, 5), *lower)],
+        [((6, 6), *whole)],
+        [((7, 7), *whole)],
     ]
     early = plan([[((s ^ e, s ^ o), at, n) for s in held for (e, o), at, n in kind] for kind in kinds])
 
@@ -281,9 +290,10 @@
     one = [tied(a, token) for a in one]
     two = [tied(a, token) for a in two]
     far = [second_way(a) for a in one]
-    token = work([x for a, b in zip(one, two) for x in (a, twin(a), b, twin(b[:, :half]), twin(b[:, half:]))])
+    token = work([x for a, b in zip(one, two) for x in (a, twin(a[:, :half]), twin(a[:, half:]), b, twin(b[:, :half]), twin(b[:, half:]))])
     far = [tied(a, token) for a in far]
-    work([x for a in far for x in (a, twin(a))])
+    work(far)
+    work([twin(a) for a in far])
 
 
 def local(mesh, item_factors, tile_counts, observed_tiles, mask_words, confidence, previous):
@@ -292,7 +302,7 @@
     users, obs, width = mask_words.shape
     slots = rows * n_row
     me = lax.axis_index("row").astype(jnp.int32).reshape(1)
-    picks = observed_tiles[0]
+    info = jnp.concatenate([me, observed_tiles[0], tile_counts])
     conf = confidence[:, None]
     words = jnp.transpose(mask_words, (1, 0, 2)).astype(BF16)
     shape = jax.ShapeDtypeStruct
@@ -300,7 +310,7 @@
     message = shape((users, rank), jnp.int16)
     sums = shape((2, users, rank), F32)
     gram_shape = shape((rank, rank), F32)
-    stages, picked, turned, alphas, carry = [], [], [], [], []
+    stages, picked, turned, alphas, carry, scalars = [], [], [], [], [], []
 
     def masks_of(plan):
         for stage in plan:
@@ -310,16 +320,19 @@
                 spot += length
             stages.append(pieces)
         sizes = [sum(length for _, _, _, length in pieces) for pieces in stages]
-        alphas.extend(
+        *masks, kept_info = (
             call(
                 functools.partial(masks_kernel, stages, rows),
                 [shape((obs, users, size), F32) for size in sizes],
-                (me, picks, tile_counts, words, conf),
-                3,
+                (info, words, conf),
+                1,
                 2 * obs * users * sum(sizes) * width,
                 "masks",
+                [shape(info.shape, info.dtype)],
             )
         )
+        alphas.extend(masks)
+        scalars.append(kept_info)
         return alphas
 
     def work(arrays):
@@ -332,8 +345,8 @@
             functools.partial(gather_kernel, pieces, rows, first, last),
             [shape((obs, size, rank), BF16), shape((obs, rank, size), BF16)]
             + ([split, split, message] if last else [gram_shape, sums]),
-            (me, picks, tile_counts, alpha, conf, previous, *arrays, *carry),
-            3,
+            (*scalars, alpha, conf, previous, *arrays, *carry),
+            1,
             2 * size * rank * (tiles * rank + 3 * obs * users),
             "stage",
         )
@@ -345,8 +358,10 @@
     gather_stages(item_factors, n_row, masks_of, work)
     high, low, msg = carry
 
+    order = [0, *range(2, n_col, 2), *range(1, n_col, 2)]
+
     def to_all(own):
-        return [own] + [permuted(own, "col", n_col, lambda i: i ^ bits) for bits in range(1, n_col)]
+        return [own] + [permuted(own, "col", n_col, lambda i: i ^ bits) for bits in order[1:]]
 
     vec = shape((users, rank), F32)
     state = []
@@ -358,7 +373,7 @@
             outs = [shape((users, 128), F32), vec, vec]
         outs.append(shape((8, users), F32) if last else message)
         *state, msg = call(
-            functools.partial(round_kernel, index, n_col, len(picked)),
+            functools.partial(round_kernel, index, order, len(picked)),
             outs,
             (*msgs, previous, high, low, *alphas, *picked, *turned, *state),
             0,
@@ -367,7 +382,7 @@
         )
     msgs = to_all(msg)
     (out,) = pl.pallas_call(
-        functools.partial(final_kernel, n_col),
+        functools.partial(final_kernel, order),
         out_shape=[vec],
         in_specs=[VMEM] * (n_col + 3),
         out_specs=[VMEM],

time: 63.3 us -> 61.8 us (0.976)
  Pallas kernels: 11.1 us -> 9.77 us
  waiting for transfers between devices: 23 us -> 22.2 us
    pallas_call x7 -> x8, Pallas kernels: 10.3 us -> 8.97 us  [call(): pl.pallas_call(body, out_shape=[pltpu.VMEM(o.shape, o.dtype) for o in out...]
    ppermute x20 -> x21, waiting for transfers between devices: 23 us -> 22.2 us  [permuted(): return lax.ppermute(array, axis, [(i, target(i)) for i in range(size)])]
    ppermute x20 -> x21, starting transfers between devices: 26.5 us -> 27 us  [permuted(): return lax.ppermute(array, axis, [(i, target(i)) for i in range(size)])]
  transfers between devices with their start and end apart: 20 -> 21, of which waited for: 14 -> 19; matrix products, arithmetic and copies ran while one was open for 2% -> 2% of each run, Pallas kernels for 8% -> 8%
where the time goes in v3:
time: 61.8 us; the launch traced here: 61.7 us
  starting transfers between devices  27 us (44%)
  waiting for transfers between devices  22.2 us (36%)
  Pallas kernels  9.77 us (16%)
  local copies, waits for them, and re-layouts  1.52 us (2%)
  other arithmetic  1.04 us (2%)
    ppermute x21, starting transfers between devices, permuted(): return lax.ppermute(array, axis, [(i, target(i)) for i in range(size)])  27 us
    ppermute x21, waiting for transfers between devices, permuted(): return lax.ppermute(array, axis, [(i, target(i)) for i in range(size)])  22.2 us
    pallas_call x8, Pallas kernels, call(): pl.pallas_call(body, out_shape=[pltpu.VMEM(o.shape, o.dtype) for o in out...  8.97 us
    unnamed x10, local copies, waits for them, and re-layouts  1.34 us
  transfers between devices with their start and end apart: 21, of which 19 were waited for; matrix products, arithmetic and copies ran while one was open for 2% of the time, Pallas kernels for 8%

profile of v3, /device:TPU:0, one launch (start us, length us, event | category | flops | bytes accessed | tf_op | source)
XLA Modules:
  0.0 61.7 jit_solution(11532419783712962946)
XLA Ops:
  0.5 2.5 %collective-permute-start = (bf16[4,256,256]{2,1,0:T(8,128)(2,1)}, bf16[4,256,256]{2,1,0:T(8,128)(2,1)S(1)}, u32[]{:S(2)}, u32[]{:S(2)}) collective-permute-start(bf16[4,256,256]{2,1,0:T(8,128)(2,1)} %refs_4_.4), channel_id=1, source_target_pairs={{0,8},{4,20},{8,0},{12,28},{16,24},{20,4},{24,16},{28,12},{1,9},{5... | collective-permute-start | bytes 1572872 | tf_op jit(solution)/shard_map/ppermute | solution.py:248
  5.5 1.4 %masks.1 = (f32[2,128,512]{2,1,0:T(8,128)S(1)}, f32[2,128,1024]{2,1,0:T(8,128)S(1)}, f32[2,128,256]{2,1,0:T(8,128)S(1)}, f32[2,128,256]{2,1,0:T(8,128)S(1)}, s32[7]{0:T(128)S(4)}) custom-call(s32[7]{0:T(128)S(1)} %pad_add_fusion.info_ref, bf16[2,128,256]{2,1,0:T(8,128)(2,1)S(1)} %fusion.words_ref, f32[128,1]{1,0:T(8,128)S(1)} %copy.8.conf_ref.refs_2_), custom_call_target="tpu_custom_call" | custom-call | flops 268435456 | bytes 1048576 | tf_op jit(solution)/shard_map/masks/pallas_call | solution.py:22
  6.8 1.6 %collective-permute-start.5 = (bf16[4,256,256]{2,1,0:T(8,128)(2,1)S(1)}, bf16[4,256,256]{2,1,0:T(8,128)(2,1)S(1)}, u32[]{:S(2)}, u32[]{:S(2)}) collective-permute-start(bf16[4,256,256]{2,1,0:T(8,128)(2,1)S(1)} %copy-done.1), channel_id=1, source_target_pairs={{0,16},{4,12},{8,24},{12,4},{16,0},{20,28},{24,8},{28,20},{1,17},{... | collective-permute-start | bytes 1572872 | tf_op jit(solution)/shard_map/ppermute | solution.py:248
  9.3 1.7 %collective-permute-done.refs_4_ = bf16[4,256,256]{2,1,0:T(8,128)(2,1)S(1)} collective-permute-done((bf16[4,256,256]{2,1,0:T(8,128)(2,1)}, bf16[4,256,256]{2,1,0:T(8,128)(2,1)S(1)}, u32[]{:S(2)}, u32[]{:S(2)}) %collective-permute-start) | collective-permute-done | bytes 524320 | tf_op jit(solution)/shard_map/ppermute | solution.py:248
  11.0 3.6 %collective-permute-start.2 = (bf16[4,256,256]{2,1,0:T(8,128)(2,1)S(1)}, bf16[4,256,256]{2,1,0:T(8,128)(2,1)S(1)}, u32[]{:S(2)}, u32[]{:S(2)}) collective-permute-start(bf16[4,256,256]{2,1,0:T(8,128)(2,1)S(1)} %collective-permute-done.refs_4_), channel_id=1, source_target_pairs={{0,16},{4,12},{8,24},{12,4},{16,0},{20,28},{24,8},{28,20},{1,17},{... | collective-permute-start | bytes 1572872 | tf_op jit(solution)/shard_map/ppermute | solution.py:248
  14.7 1.4 %collective-permute-done.5.refs_7_ = bf16[4,256,256]{2,1,0:T(8,128)(2,1)S(1)} collective-permute-done((bf16[4,256,256]{2,1,0:T(8,128)(2,1)S(1)}, bf16[4,256,256]{2,1,0:T(8,128)(2,1)S(1)}, u32[]{:S(2)}, u32[]{:S(2)}) %collective-permute-start.5) | collective-permute-done | bytes 524320 | tf_op jit(solution)/shard_map/ppermute | solution.py:248
  18.7 1.9 %stage.5 = (bf16[2,1024,256]{2,1,0:T(8,128)(2,1)S(1)}, bf16[2,256,1024]{2,1,0:T(8,128)(2,1)S(1)}, f32[256,256]{1,0:T(8,128)S(1)}, f32[2,128,256]{2,1,0:T(8,128)S(1)}) custom-call(s32[7]{0:T(128)S(4)} %get-tuple-element.41.refs_0_, f32[2,128,1024]{2,1,0:T(8,128)S(1)} %get-tuple-element.46.refs_1_.refs_8_, f32[128,1]{1,0:T(8,128)S(1)} %copy.8.conf_ref.refs_2_, ...), custom_call_target="tpu_custom_call" | custom-call | flops 939524096 | bytes 1048576 | tf_op jit(solution)/shard_map/stage/pallas_call | solution.py:22
  20.6 1.2 %collective-permute-done.2.refs_4_ = bf16[4,256,256]{2,1,0:T(8,128)(2,1)S(1)} collective-permute-done((bf16[4,256,256]{2,1,0:T(8,128)(2,1)S(1)}, bf16[4,256,256]{2,1,0:T(8,128)(2,1)S(1)}, u32[]{:S(2)}, u32[]{:S(2)}) %collective-permute-start.2) | collective-permute-done | bytes 524320 | tf_op jit(solution)/shard_map/ppermute | solution.py:248
  22.4 1.3 %collective-permute-done.8.refs_4_ = bf16[4,256,256]{2,1,0:T(8,128)(2,1)S(1)} collective-permute-done((bf16[4,256,256]{2,1,0:T(8,128)(2,1)S(1)}, bf16[4,256,256]{2,1,0:T(8,128)(2,1)S(1)}, u32[]{:S(2)}, u32[]{:S(2)}) %collective-permute-start.8) | collective-permute-done | bytes 524320 | tf_op jit(solution)/shard_map/ppermute | solution.py:248
  24.5 3.6 %collective-permute-start.11 = (s16[128,256]{1,0:T(8,128)(2,1)S(1)}, s16[128,256]{1,0:T(8,128)(2,1)S(1)}, u32[]{:S(2)}, u32[]{:S(2)}) collective-permute-start(s16[128,256]{1,0:T(8,128)(2,1)S(1)} %get-tuple-element.56.refs_0_), channel_id=1, source_target_pairs={{0,3},{1,2},{2,1},{3,0},{4,7},{5,6},{6,5},{7,4},{8,11},{9,10},{10,... | collective-permute-start | bytes 196616 | tf_op jit(solution)/shard_map/ppermute | solution.py:248
  28.9 2.3 %collective-permute-done.11.refs_3_ = s16[128,256]{1,0:T(8,128)(2,1)S(1)} collective-permute-done((s16[128,256]{1,0:T(8,128)(2,1)S(1)}, s16[128,256]{1,0:T(8,128)(2,1)S(1)}, u32[]{:S(2)}, u32[]{:S(2)}) %collective-permute-start.11) | collective-permute-done | bytes 65568 | tf_op jit(solution)/shard_map/ppermute | solution.py:248
  31.3 2.0 %collective-permute-done.10.refs_2_ = s16[128,256]{1,0:T(8,128)(2,1)S(1)} collective-permute-done((s16[128,256]{1,0:T(8,128)(2,1)S(1)}, s16[128,256]{1,0:T(8,128)(2,1)S(1)}, u32[]{:S(2)}, u32[]{:S(2)}) %collective-permute-start.10) | collective-permute-done | bytes 65568 | tf_op jit(solution)/shard_map/ppermute | solution.py:248
  33.9 1.2 %round0.1 = (f32[128,256]{1,0:T(8,128)S(1)}, s16[128,256]{1,0:T(8,128)(2,1)S(1)}) custom-call(s16[128,256]{1,0:T(8,128)(2,1)S(1)} %get-tuple-element.56.refs_0_, s16[128,256]{1,0:T(8,128)(2,1)S(1)} %collective-permute-done.9.refs_1_, s16[128,256]{1,0:T(8,128)(2,1)S(1)} %collective-permute-done.10.refs_2_, ...), custom_call_target="tpu_custom_call" | custom-call | flops 536870912 | bytes 1048576 | tf_op jit(solution)/shard_map/round0/pallas_call | solution.py:22
  35.1 2.3 %collective-permute-start.14 = (s16[128,256]{1,0:T(8,128)(2,1)S(1)}, s16[128,256]{1,0:T(8,128)(2,1)S(1)}, u32[]{:S(2)}, u32[]{:S(2)}) collective-permute-start(s16[128,256]{1,0:T(8,128)(2,1)S(1)} %get-tuple-element.67.refs_0_), channel_id=1, source_target_pairs={{0,3},{1,2},{2,1},{3,0},{4,7},{5,6},{6,5},{7,4},{8,11},{9,10},{10,... | collective-permute-start | bytes 196616 | tf_op jit(solution)/shard_map/ppermute | solution.py:248
  37.8 1.8 %collective-permute-start.12 = (s16[128,256]{1,0:T(8,128)(2,1)S(1)}, s16[128,256]{1,0:T(8,128)(2,1)S(1)}, u32[]{:S(2)}, u32[]{:S(2)}) collective-permute-start(s16[128,256]{1,0:T(8,128)(2,1)S(1)} %get-tuple-element.67.refs_0_), channel_id=1, source_target_pairs={{0,2},{1,3},{2,0},{3,1},{4,6},{5,7},{6,4},{7,5},{8,10},{9,11},{10,... | collective-permute-start | bytes 196616 | tf_op jit(solution)/shard_map/ppermute | solution.py:248
  39.5 1.8 %collective-permute-done.14.refs_3_ = s16[128,256]{1,0:T(8,128)(2,1)S(1)} collective-permute-done((s16[128,256]{1,0:T(8,128)(2,1)S(1)}, s16[128,256]{1,0:T(8,128)(2,1)S(1)}, u32[]{:S(2)}, u32[]{:S(2)}) %collective-permute-start.14) | collective-permute-done | bytes 65568 | tf_op jit(solution)/shard_map/ppermute | solution.py:248
  43.1 1.3 %round1.1 = (f32[128,256]{1,0:T(8,128)S(1)}, f32[128,256]{1,0:T(8,128)S(1)}, f32[128,256]{1,0:T(8,128)S(1)}, s16[128,256]{1,0:T(8,128)(2,1)S(1)}) custom-call(s16[128,256]{1,0:T(8,128)(2,1)S(1)} %get-tuple-element.67.refs_0_, s16[128,256]{1,0:T(8,128)(2,1)S(1)} %collective-permute-done.12.refs_1_, s16[128,256]{1,0:T(8,128)(2,1)S(1)} %collective-permute-done.13.refs_2_, ...), custom_call_target="tpu_custom_call" | custom-call | flops 536870912 | bytes 1048576 | tf_op jit(solution)/shard_map/round1/pallas_call | solution.py:22
  44.5 3.1 %collective-permute-start.17 = (s16[128,256]{1,0:T(8,128)(2,1)S(1)}, s16[128,256]{1,0:T(8,128)(2,1)S(1)}, u32[]{:S(2)}, u32[]{:S(2)}) collective-permute-start(s16[128,256]{1,0:T(8,128)(2,1)S(1)} %get-tuple-element.69.refs_0_), channel_id=1, source_target_pairs={{0,3},{1,2},{2,1},{3,0},{4,7},{5,6},{6,5},{7,4},{8,11},{9,10},{10,... | collective-permute-start | bytes 196616 | tf_op jit(solution)/shard_map/ppermute | solution.py:248
  47.6 1.3 %collective-permute-start.15 = (s16[128,256]{1,0:T(8,128)(2,1)S(1)}, s16[128,256]{1,0:T(8,128)(2,1)S(1)}, u32[]{:S(2)}, u32[]{:S(2)}) collective-permute-start(s16[128,256]{1,0:T(8,128)(2,1)S(1)} %get-tuple-element.69.refs_0_), channel_id=1, source_target_pairs={{0,2},{1,3},{2,0},{3,1},{4,6},{5,7},{6,4},{7,5},{8,10},{9,11},{10,... | collective-permute-start | bytes 196616 | tf_op jit(solution)/shard_map/ppermute | solution.py:248
  48.9 2.0 %collective-permute-done.17.refs_3_ = s16[128,256]{1,0:T(8,128)(2,1)S(1)} collective-permute-done((s16[128,256]{1,0:T(8,128)(2,1)S(1)}, s16[128,256]{1,0:T(8,128)(2,1)S(1)}, u32[]{:S(2)}, u32[]{:S(2)}) %collective-permute-start.17) | collective-permute-done | bytes 65568 | tf_op jit(solution)/shard_map/ppermute | solution.py:248
  51.0 1.9 %collective-permute-done.16.refs_2_ = s16[128,256]{1,0:T(8,128)(2,1)S(1)} collective-permute-done((s16[128,256]{1,0:T(8,128)(2,1)S(1)}, s16[128,256]{1,0:T(8,128)(2,1)S(1)}, u32[]{:S(2)}, u32[]{:S(2)}) %collective-permute-start.16) | collective-permute-done | bytes 65568 | tf_op jit(solution)/shard_map/ppermute | solution.py:248
  53.8 2.5 %collective-permute-start.20 = (f32[8,128]{1,0:T(8,128)S(1)}, f32[8,128]{1,0:T(8,128)S(1)}, u32[]{:S(2)}, u32[]{:S(2)}) collective-permute-start(f32[8,128]{1,0:T(8,128)S(1)} %get-tuple-element.73.refs_0_), channel_id=1, source_target_pairs={{0,3},{1,2},{2,1},{3,0},{4,7},{5,6},{6,5},{7,4},{8,11},{9,10},{10,... | collective-permute-start | bytes 12296 | tf_op jit(solution)/shard_map/ppermute | solution.py:248
  56.3 1.9 %collective-permute-start.18 = (f32[8,128]{1,0:T(8,128)S(1)}, f32[8,128]{1,0:T(8,128)S(1)}, u32[]{:S(2)}, u32[]{:S(2)}) collective-permute-start(f32[8,128]{1,0:T(8,128)S(1)} %get-tuple-element.73.refs_0_), channel_id=1, source_target_pairs={{0,2},{1,3},{2,0},{3,1},{4,6},{5,7},{6,4},{7,5},{8,10},{9,11},{10,... | collective-permute-start | bytes 12296 | tf_op jit(solution)/shard_map/ppermute | solution.py:248
  58.3 1.0 %collective-permute-done.20.refs_3_ = f32[8,128]{1,0:T(8,128)S(1)} collective-permute-done((f32[8,128]{1,0:T(8,128)S(1)}, f32[8,128]{1,0:T(8,128)S(1)}, u32[]{:S(2)}, u32[]{:S(2)}) %collective-permute-start.20) | collective-permute-done | bytes 4128 | tf_op jit(solution)/shard_map/ppermute | solution.py:248
  (42 shorter events, 14.9 us)
Async XLA Ops:
  0.0 8.4 %collective-permute-start.1 = (bf16[4,256,256]{2,1,0:T(8,128)(2,1)}, bf16[4,256,256]{2,1,0:T(8,128)(2,1)S(1)}, u32[]{:S(2)}, u32[]{:S(2)}) collective-permute-start(bf16[4,256,256]{2,1,0:T(8,128)(2,1)} %refs_4_.4), channel_id=1, source_target_pairs={{0,4},{4,0},{8,12},{12,8},{16,20},{20,16},{24,28},{28,24},{1,5},{5... | collective-permute-start | bytes 1572872 | tf_op jit(solution)/shard_map/ppermute | solution.py:248
  0.5 10.5 %collective-permute-start = (bf16[4,256,256]{2,1,0:T(8,128)(2,1)}, bf16[4,256,256]{2,1,0:T(8,128)(2,1)S(1)}, u32[]{:S(2)}, u32[]{:S(2)}) collective-permute-start(bf16[4,256,256]{2,1,0:T(8,128)(2,1)} %refs_4_.4), channel_id=1, source_target_pairs={{0,8},{4,20},{8,0},{12,28},{16,24},{20,4},{24,16},{28,12},{1,9},{5... | collective-permute-start | bytes 1572872 | tf_op jit(solution)/shard_map/ppermute | solution.py:248
  2.9 0.7 %copy-start.4 = (s32[1,2]{1,0:T(1,128)S(1)}, s32[1,2]{1,0:T(1,128)}, u32[]{:S(2)}) copy-start(s32[1,2]{1,0:T(1,128)} %param.8) | copy-start | bytes 28
  5.4 1.4 %copy-start.1 = (bf16[4,256,256]{2,1,0:T(8,128)(2,1)S(1)}, bf16[4,256,256]{2,1,0:T(8,128)(2,1)}, u32[]{:S(2)}) copy-start(bf16[4,256,256]{2,1,0:T(8,128)(2,1)} %refs_4_.4) | copy-start | bytes 1572868
  5.4 3.0 %copy-start = (bf16[128,256]{1,0:T(8,128)(2,1)S(1)}, bf16[128,256]{1,0:T(8,128)(2,1)}, u32[]{:S(2)}) copy-start(bf16[128,256]{1,0:T(8,128)(2,1)} %refs_4_.7) | copy-start | bytes 196612
  6.8 9.2 %collective-permute-start.5 = (bf16[4,256,256]{2,1,0:T(8,128)(2,1)S(1)}, bf16[4,256,256]{2,1,0:T(8,128)(2,1)S(1)}, u32[]{:S(2)}, u32[]{:S(2)}) collective-permute-start(bf16[4,256,256]{2,1,0:T(8,128)(2,1)S(1)} %copy-done.1), channel_id=1, source_target_pairs={{0,16},{4,12},{8,24},{12,4},{16,0},{20,28},{24,8},{28,20},{1,17},{... | collective-permute-start | bytes 1572872 | tf_op jit(solution)/shard_map/ppermute | solution.py:248
  11.0 10.8 %collective-permute-start.2 = (bf16[4,256,256]{2,1,0:T(8,128)(2,1)S(1)}, bf16[4,256,256]{2,1,0:T(8,128)(2,1)S(1)}, u32[]{:S(2)}, u32[]{:S(2)}) collective-permute-start(bf16[4,256,256]{2,1,0:T(8,128)(2,1)S(1)} %collective-permute-done.refs_4_), channel_id=1, source_target_pairs={{0,16},{4,12},{8,24},{12,4},{16,0},{20,28},{24,8},{28,20},{1,17},{... | collective-permute-start | bytes 1572872 | tf_op jit(solution)/shard_map/ppermute | solution.py:248
  16.1 1.5 %collective-permute-start.4 = (bf16[4,128,256]{2,1,0:T(8,128)(2,1)S(1)}, bf16[4,128,256]{2,1,0:T(8,128)(2,1)S(1)}, u32[]{:S(2)}, u32[]{:S(2)}) collective-permute-start(bf16[4,128,256]{2,1,0:T(8,128)(2,1)S(1)} %get-tuple-element.79), channel_id=1, source_target_pairs={{0,4},{4,0},{8,12},{12,8},{16,20},{20,16},{24,28},{28,24},{1,5},{5... | collective-permute-start | bytes 786440 | tf_op jit(solution)/shard_map/ppermute | solution.py:248
  16.1 1.9 %collective-permute-start.3 = (bf16[4,128,256]{2,1,0:T(8,128)(2,1)S(1)}, bf16[4,128,256]{2,1,0:T(8,128)(2,1)S(1)}, u32[]{:S(2)}, u32[]{:S(2)}) collective-permute-start(bf16[4,128,256]{2,1,0:T(8,128)(2,1)S(1)} %get-tuple-element.80), channel_id=1, source_target_pairs={{0,4},{4,0},{8,12},{12,8},{16,20},{20,16},{24,28},{28,24},{1,5},{5... | collective-permute-start | bytes 786440 | tf_op jit(solution)/shard_map/ppermute | solution.py:248
  16.6 1.7 %collective-permute-start.7 = (bf16[4,128,256]{2,1,0:T(8,128)(2,1)S(1)}, bf16[4,128,256]{2,1,0:T(8,128)(2,1)S(1)}, u32[]{:S(2)}, u32[]{:S(2)}) collective-permute-start(bf16[4,128,256]{2,1,0:T(8,128)(2,1)S(1)} %get-tuple-element.77), channel_id=1, source_target_pairs={{0,4},{4,0},{8,12},{12,8},{16,20},{20,16},{24,28},{28,24},{1,5},{5... | collective-permute-start | bytes 786440 | tf_op jit(solution)/shard_map/ppermute | solution.py:248
  16.7 2.0 %collective-permute-start.6 = (bf16[4,128,256]{2,1,0:T(8,128)(2,1)S(1)}, bf16[4,128,256]{2,1,0:T(8,128)(2,1)S(1)}, u32[]{:S(2)}, u32[]{:S(2)}) collective-permute-start(bf16[4,128,256]{2,1,0:T(8,128)(2,1)S(1)} %get-tuple-element.78), channel_id=1, source_target_pairs={{0,4},{4,0},{8,12},{12,8},{16,20},{20,16},{24,28},{28,24},{1,5},{5... | collective-permute-start | bytes 786440 | tf_op jit(solution)/shard_map/ppermute | solution.py:248
  21.8 1.9 %collective-permute-start.8 = (bf16[4,256,256]{2,1,0:T(8,128)(2,1)S(1)}, bf16[4,256,256]{2,1,0:T(8,128)(2,1)S(1)}, u32[]{:S(2)}, u32[]{:S(2)}) collective-permute-start(bf16[4,256,256]{2,1,0:T(8,128)(2,1)S(1)} %collective-permute-done.2.refs_4_), channel_id=1, source_target_pairs={{0,4},{4,0},{8,12},{12,8},{16,20},{20,16},{24,28},{28,24},{1,5},{5... | collective-permute-start | bytes 1572872 | tf_op jit(solution)/shard_map/ppermute | solution.py:248
  24.5 6.8 %collective-permute-start.11 = (s16[128,256]{1,0:T(8,128)(2,1)S(1)}, s16[128,256]{1,0:T(8,128)(2,1)S(1)}, u32[]{:S(2)}, u32[]{:S(2)}) collective-permute-start(s16[128,256]{1,0:T(8,128)(2,1)S(1)} %get-tuple-element.56.refs_0_), channel_id=1, source_target_pairs={{0,3},{1,2},{2,1},{3,0},{4,7},{5,6},{6,5},{7,4},{8,11},{9,10},{10,... | collective-permute-start | bytes 196616 | tf_op jit(solution)/shard_map/ppermute | solution.py:248
  28.1 5.2 %collective-permute-start.10 = (s16[128,256]{1,0:T(8,128)(2,1)S(1)}, s16[128,256]{1,0:T(8,128)(2,1)S(1)}, u32[]{:S(2)}, u32[]{:S(2)}) collective-permute-start(s16[128,256]{1,0:T(8,128)(2,1)S(1)} %get-tuple-element.56.refs_0_), channel_id=1, source_target_pairs={{0,1},{1,0},{2,3},{3,2},{4,5},{5,4},{6,7},{7,6},{8,9},{9,8},{10,11... | collective-permute-start | bytes 196616 | tf_op jit(solution)/shard_map/ppermute | solution.py:248
  28.1 5.9 %collective-permute-start.9 = (s16[128,256]{1,0:T(8,128)(2,1)S(1)}, s16[128,256]{1,0:T(8,128)(2,1)S(1)}, u32[]{:S(2)}, u32[]{:S(2)}) collective-permute-start(s16[128,256]{1,0:T(8,128)(2,1)S(1)} %get-tuple-element.56.refs_0_), channel_id=1, source_target_pairs={{0,2},{1,3},{2,0},{3,1},{4,6},{5,7},{6,4},{7,5},{8,10},{9,11},{10,... | collective-permute-start | bytes 196616 | tf_op jit(solution)/shard_map/ppermute | solution.py:248
  35.1 6.3 %collective-permute-start.14 = (s16[128,256]{1,0:T(8,128)(2,1)S(1)}, s16[128,256]{1,0:T(8,128)(2,1)S(1)}, u32[]{:S(2)}, u32[]{:S(2)}) collective-permute-start(s16[128,256]{1,0:T(8,128)(2,1)S(1)} %get-tuple-element.67.refs_0_), channel_id=1, source_target_pairs={{0,3},{1,2},{2,1},{3,0},{4,7},{5,6},{6,5},{7,4},{8,11},{9,10},{10,... | collective-permute-start | bytes 196616 | tf_op jit(solution)/shard_map/ppermute | solution.py:248
  37.4 4.9 %collective-permute-start.13 = (s16[128,256]{1,0:T(8,128)(2,1)S(1)}, s16[128,256]{1,0:T(8,128)(2,1)S(1)}, u32[]{:S(2)}, u32[]{:S(2)}) collective-permute-start(s16[128,256]{1,0:T(8,128)(2,1)S(1)} %get-tuple-element.67.refs_0_), channel_id=1, source_target_pairs={{0,1},{1,0},{2,3},{3,2},{4,5},{5,4},{6,7},{7,6},{8,9},{9,8},{10,11... | collective-permute-start | bytes 196616 | tf_op jit(solution)/shard_map/ppermute | solution.py:248
  37.8 5.4 %collective-permute-start.12 = (s16[128,256]{1,0:T(8,128)(2,1)S(1)}, s16[128,256]{1,0:T(8,128)(2,1)S(1)}, u32[]{:S(2)}, u32[]{:S(2)}) collective-permute-start(s16[128,256]{1,0:T(8,128)(2,1)S(1)} %get-tuple-element.67.refs_0_), channel_id=1, source_target_pairs={{0,2},{1,3},{2,0},{3,1},{4,6},{5,7},{6,4},{7,5},{8,10},{9,11},{10,... | collective-permute-start | bytes 196616 | tf_op jit(solution)/shard_map/ppermute | solution.py:248
  44.5 6.5 %collective-permute-start.17 = (s16[128,256]{1,0:T(8,128)(2,1)S(1)}, s16[128,256]{1,0:T(8,128)(2,1)S(1)}, u32[]{:S(2)}, u32[]{:S(2)}) collective-permute-start(s16[128,256]{1,0:T(8,128)(2,1)S(1)} %get-tuple-element.69.refs_0_), channel_id=1, source_target_pairs={{0,3},{1,2},{2,1},{3,0},{4,7},{5,6},{6,5},{7,4},{8,11},{9,10},{10,... | collective-permute-start | bytes 196616 | tf_op jit(solution)/shard_map/ppermute | solution.py:248
  47.6 5.2 %collective-permute-start.16 = (s16[128,256]{1,0:T(8,128)(2,1)S(1)}, s16[128,256]{1,0:T(8,128)(2,1)S(1)}, u32[]{:S(2)}, u32[]{:S(2)}) collective-permute-start(s16[128,256]{1,0:T(8,128)(2,1)S(1)} %get-tuple-element.69.refs_0_), channel_id=1, source_target_pairs={{0,1},{1,0},{2,3},{3,2},{4,5},{5,4},{6,7},{7,6},{8,9},{9,8},{10,11... | collective-permute-start | bytes 196616 | tf_op jit(solution)/shard_map/ppermute | solution.py:248
  47.6 5.2 %collective-permute-start.15 = (s16[128,256]{1,0:T(8,128)(2,1)S(1)}, s16[128,256]{1,0:T(8,128)(2,1)S(1)}, u32[]{:S(2)}, u32[]{:S(2)}) collective-permute-start(s16[128,256]{1,0:T(8,128)(2,1)S(1)} %get-tuple-element.69.refs_0_), channel_id=1, source_target_pairs={{0,2},{1,3},{2,0},{3,1},{4,6},{5,7},{6,4},{7,5},{8,10},{9,11},{10,... | collective-permute-start | bytes 196616 | tf_op jit(solution)/shard_map/ppermute | solution.py:248
  53.8 5.4 %collective-permute-start.20 = (f32[8,128]{1,0:T(8,128)S(1)}, f32[8,128]{1,0:T(8,128)S(1)}, u32[]{:S(2)}, u32[]{:S(2)}) collective-permute-start(f32[8,128]{1,0:T(8,128)S(1)} %get-tuple-element.73.refs_0_), channel_id=1, source_target_pairs={{0,3},{1,2},{2,1},{3,0},{4,7},{5,6},{6,5},{7,4},{8,11},{9,10},{10,... | collective-permute-start | bytes 12296 | tf_op jit(solution)/shard_map/ppermute | solution.py:248
  56.3 3.6 %collective-permute-start.19 = (f32[8,128]{1,0:T(8,128)S(1)}, f32[8,128]{1,0:T(8,128)S(1)}, u32[]{:S(2)}, u32[]{:S(2)}) collective-permute-start(f32[8,128]{1,0:T(8,128)S(1)} %get-tuple-element.73.refs_0_), channel_id=1, source_target_pairs={{0,1},{1,0},{2,3},{3,2},{4,5},{5,4},{6,7},{7,6},{8,9},{9,8},{10,11... | collective-permute-start | bytes 12296 | tf_op jit(solution)/shard_map/ppermute | solution.py:248
  56.3 4.5 %collective-permute-start.18 = (f32[8,128]{1,0:T(8,128)S(1)}, f32[8,128]{1,0:T(8,128)S(1)}, u32[]{:S(2)}, u32[]{:S(2)}) collective-permute-start(f32[8,128]{1,0:T(8,128)S(1)} %get-tuple-element.73.refs_0_), channel_id=1, source_target_pairs={{0,2},{1,3},{2,0},{3,1},{4,6},{5,7},{6,4},{7,5},{8,10},{9,11},{10,... | collective-permute-start | bytes 12296 | tf_op jit(solution)/shard_map/ppermute | solution.py:248
  (2 other events, 1.3 us)

commit v4 on v3

--- a/solution.py
+++ b/solution.py
@@ -67,6 +67,10 @@
     return whole.astype(F32) * jnp.exp2(power - 15.0)
 
 
+def blocks(size):
+    return [slice(at, min(at + BLOCK, size)) for at in range(0, size, BLOCK)]
+
+
 def tree_sum(parts):
     while len(parts) > 1:
         parts = [parts[i] + parts[i + 1] for i in range(0, len(parts), 2)]
@@ -84,22 +88,24 @@
         kept_ref[index] = info_ref[index]
     me = info_ref[0]
     obs, _, width = words_ref.shape
-    lane = lax.broadcasted_iota(jnp.int32, (1, BLOCK), 1)
-    word_index = lax.broadcasted_iota(jnp.int32, (width, BLOCK), 0)
     for pieces, out_ref in zip(stages, out_refs):
-        for at in range(0, out_ref.shape[2], BLOCK):
-            slot = jnp.zeros((1, BLOCK), jnp.int32)
+        for block in blocks(out_ref.shape[2]):
+            size = block.stop - block.start
+            lane = lax.broadcasted_iota(jnp.int32, (1, size), 1)
+            slot = jnp.zeros((1, size), jnp.int32)
             for spot, pair, offset, _ in pieces:
-                if at <= spot < at + BLOCK:
-                    start = shard_index(me, pair) * rows + offset - (spot - at)
-                    slot = jnp.where(lane >= spot - at, lane + start, slot)
+                place = spot - block.start
+                if 0 <= place < size:
+                    start = shard_index(me, pair) * rows + offset - place
+                    slot = jnp.where(lane >= place, lane + start, slot)
+            word_index = lax.broadcasted_iota(jnp.int32, (width, size), 0)
             spread = (word_index == jnp.right_shift(slot, 3)).astype(BF16)
             for p in range(obs):
                 count = info_ref[1 + obs + info_ref[1 + p]]
                 word = jnp.dot(words_ref[p], spread, preferred_element_type=F32).astype(jnp.int32)
                 bits = jnp.right_shift(word, slot & 7) & 1
                 bits = jnp.where(slot < count, bits, 0).astype(F32)
-                out_ref[p, :, at : at + BLOCK] = bits * conf_ref[...]
+                out_ref[p, :, block] = bits * conf_ref[...]
 
 
 def gather_kernel(pieces, rows, first, last, *refs):
@@ -145,11 +151,11 @@
     rhs = jnp.zeros((users, rank), F32) if first else sums_in[0]
     image = jnp.zeros((users, rank), F32) if first else sums_in[1]
     for p in range(obs):
-        for start in range(0, picked_ref.shape[1], BLOCK):
-            items = picked_ref[p, start : start + BLOCK, :]
+        for block in blocks(picked_ref.shape[1]):
+            items = picked_ref[p, block, :]
             turned = items.T
-            turned_ref[p, :, start : start + BLOCK] = turned
-            alpha = alpha_ref[p, :, start : start + BLOCK]
+            turned_ref[p, :, block] = turned
+            alpha = alpha_ref[p, :, block]
             scores = jnp.dot(prev, turned, preferred_element_type=F32)
             weights = (alpha * scores).astype(BF16)
             seen = jnp.where(alpha > 0.0, 1.0, 0.0).astype(BF16)
@@ -212,22 +218,18 @@
     image = both[:users] + both[users:] + jnp.dot(rounded, low_ref[...], preferred_element_type=F32)
     if last:
         total = jnp.sum(image * direction, axis=1, keepdims=True)
-        squares = jnp.zeros((direction.shape[0], BLOCK), F32)
     for alpha_ref, ref, turned_ref in zip(alphas, picked, turned):
         for p in range(ref.shape[0]):
-            for start in range(0, ref.shape[1], BLOCK):
-                items = ref[p, start : start + BLOCK, :]
-                alpha = alpha_ref[p, :, start : start + BLOCK]
-                scores = jnp.dot(
-                    rounded, turned_ref[p, :, start : start + BLOCK], preferred_element_type=F32
-                )
+            for block in blocks(ref.shape[1]):
+                items = ref[p, block, :]
+                alpha = alpha_ref[p, :, block]
+                scores = jnp.dot(rounded, turned_ref[p, :, block], preferred_element_type=F32)
                 weights = (alpha * scores).astype(BF16)
                 if last:
-                    squares = squares + weights.astype(F32) * scores
+                    total = total + jnp.sum(weights.astype(F32) * scores, axis=1, keepdims=True)
                 else:
                     image = image + jnp.dot(weights, items, preferred_element_type=F32)
     if last:
-        total = total + jnp.sum(squares, axis=1, keepdims=True)
         msg_ref[...] = row_of(total, msg_ref.shape[0])
     else:
         pack(image, msg_ref)

time: 61.8 us -> 61.8 us (level)
  no operation moved by 1% of the time
where the time goes in v4:
time: 61.8 us; the launch traced here: 61.6 us
  starting transfers between devices  27 us (44%)
  waiting for transfers between devices  22.2 us (36%)
  Pallas kernels  9.73 us (16%)
  local copies, waits for them, and re-layouts  1.52 us (2%)
  other arithmetic  1.04 us (2%)
    ppermute x21, starting transfers between devices, permuted(): return lax.ppermute(array, axis, [(i, target(i)) for i in range(size)])  27 us
    ppermute x21, waiting for transfers between devices, permuted(): return lax.ppermute(array, axis, [(i, target(i)) for i in range(size)])  22.2 us
    pallas_call x8, Pallas kernels, call(): pl.pallas_call(body, out_shape=[pltpu.VMEM(o.shape, o.dtype) for o in out...  8.92 us
    unnamed x10, local copies, waits for them, and re-layouts  1.34 us
  transfers between devices with their start and end apart: 21, of which 19 were waited for; matrix products, arithmetic and copies ran while one was open for 2% of the time, Pallas kernels for 8%

profile of v4, /device:TPU:0, one launch (start us, length us, event | category | flops | bytes accessed | tf_op | source)
XLA Modules:
  0.0 61.6 jit_solution(7408333598446684281)
XLA Ops:
  0.5 2.5 %collective-permute-start = (bf16[4,256,256]{2,1,0:T(8,128)(2,1)}, bf16[4,256,256]{2,1,0:T(8,128)(2,1)S(1)}, u32[]{:S(2)}, u32[]{:S(2)}) collective-permute-start(bf16[4,256,256]{2,1,0:T(8,128)(2,1)} %refs_4_.4), channel_id=1, source_target_pairs={{0,8},{4,20},{8,0},{12,28},{16,24},{20,4},{24,16},{28,12},{1,9},{5... | collective-permute-start | bytes 1572872 | tf_op jit(solution)/shard_map/ppermute | solution.py:250
  5.5 1.4 %masks.1 = (f32[2,128,512]{2,1,0:T(8,128)S(1)}, f32[2,128,1024]{2,1,0:T(8,128)S(1)}, f32[2,128,256]{2,1,0:T(8,128)S(1)}, f32[2,128,256]{2,1,0:T(8,128)S(1)}, s32[7]{0:T(128)S(4)}) custom-call(s32[7]{0:T(128)S(1)} %pad_add_fusion.info_ref, bf16[2,128,256]{2,1,0:T(8,128)(2,1)S(1)} %fusion.words_ref, f32[128,1]{1,0:T(8,128)S(1)} %copy.8.conf_ref.refs_2_), custom_call_target="tpu_custom_call" | custom-call | flops 268435456 | bytes 1048576 | tf_op jit(solution)/shard_map/masks/pallas_call | solution.py:22
  6.8 1.6 %collective-permute-start.5 = (bf16[4,256,256]{2,1,0:T(8,128)(2,1)S(1)}, bf16[4,256,256]{2,1,0:T(8,128)(2,1)S(1)}, u32[]{:S(2)}, u32[]{:S(2)}) collective-permute-start(bf16[4,256,256]{2,1,0:T(8,128)(2,1)S(1)} %copy-done.1), channel_id=1, source_target_pairs={{0,16},{4,12},{8,24},{12,4},{16,0},{20,28},{24,8},{28,20},{1,17},{... | collective-permute-start | bytes 1572872 | tf_op jit(solution)/shard_map/ppermute | solution.py:250
  9.3 1.7 %collective-permute-done.refs_4_ = bf16[4,256,256]{2,1,0:T(8,128)(2,1)S(1)} collective-permute-done((bf16[4,256,256]{2,1,0:T(8,128)(2,1)}, bf16[4,256,256]{2,1,0:T(8,128)(2,1)S(1)}, u32[]{:S(2)}, u32[]{:S(2)}) %collective-permute-start) | collective-permute-done | bytes 524320 | tf_op jit(solution)/shard_map/ppermute | solution.py:250
  11.0 3.6 %collective-permute-start.2 = (bf16[4,256,256]{2,1,0:T(8,128)(2,1)S(1)}, bf16[4,256,256]{2,1,0:T(8,128)(2,1)S(1)}, u32[]{:S(2)}, u32[]{:S(2)}) collective-permute-start(bf16[4,256,256]{2,1,0:T(8,128)(2,1)S(1)} %collective-permute-done.refs_4_), channel_id=1, source_target_pairs={{0,16},{4,12},{8,24},{12,4},{16,0},{20,28},{24,8},{28,20},{1,17},{... | collective-permute-start | bytes 1572872 | tf_op jit(solution)/shard_map/ppermute | solution.py:250
  14.7 1.4 %collective-permute-done.5.refs_7_ = bf16[4,256,256]{2,1,0:T(8,128)(2,1)S(1)} collective-permute-done((bf16[4,256,256]{2,1,0:T(8,128)(2,1)S(1)}, bf16[4,256,256]{2,1,0:T(8,128)(2,1)S(1)}, u32[]{:S(2)}, u32[]{:S(2)}) %collective-permute-start.5) | collective-permute-done | bytes 524320 | tf_op jit(solution)/shard_map/ppermute | solution.py:250
  18.7 1.9 %stage.5 = (bf16[2,1024,256]{2,1,0:T(8,128)(2,1)S(1)}, bf16[2,256,1024]{2,1,0:T(8,128)(2,1)S(1)}, f32[256,256]{1,0:T(8,128)S(1)}, f32[2,128,256]{2,1,0:T(8,128)S(1)}) custom-call(s32[7]{0:T(128)S(4)} %get-tuple-element.41.refs_0_, f32[2,128,1024]{2,1,0:T(8,128)S(1)} %get-tuple-element.46.refs_1_.refs_8_, f32[128,1]{1,0:T(8,128)S(1)} %copy.8.conf_ref.refs_2_, ...), custom_call_target="tpu_custom_call" | custom-call | flops 939524096 | bytes 1048576 | tf_op jit(solution)/shard_map/stage/pallas_call | solution.py:22
  20.6 1.2 %collective-permute-done.2.refs_4_ = bf16[4,256,256]{2,1,0:T(8,128)(2,1)S(1)} collective-permute-done((bf16[4,256,256]{2,1,0:T(8,128)(2,1)S(1)}, bf16[4,256,256]{2,1,0:T(8,128)(2,1)S(1)}, u32[]{:S(2)}, u32[]{:S(2)}) %collective-permute-start.2) | collective-permute-done | bytes 524320 | tf_op jit(solution)/shard_map/ppermute | solution.py:250
  22.4 1.3 %collective-permute-done.8.refs_4_ = bf16[4,256,256]{2,1,0:T(8,128)(2,1)S(1)} collective-permute-done((bf16[4,256,256]{2,1,0:T(8,128)(2,1)S(1)}, bf16[4,256,256]{2,1,0:T(8,128)(2,1)S(1)}, u32[]{:S(2)}, u32[]{:S(2)}) %collective-permute-start.8) | collective-permute-done | bytes 524320 | tf_op jit(solution)/shard_map/ppermute | solution.py:250
  24.5 3.6 %collective-permute-start.11 = (s16[128,256]{1,0:T(8,128)(2,1)S(1)}, s16[128,256]{1,0:T(8,128)(2,1)S(1)}, u32[]{:S(2)}, u32[]{:S(2)}) collective-permute-start(s16[128,256]{1,0:T(8,128)(2,1)S(1)} %get-tuple-element.56.refs_0_), channel_id=1, source_target_pairs={{0,3},{1,2},{2,1},{3,0},{4,7},{5,6},{6,5},{7,4},{8,11},{9,10},{10,... | collective-permute-start | bytes 196616 | tf_op jit(solution)/shard_map/ppermute | solution.py:250
  28.9 2.3 %collective-permute-done.11.refs_3_ = s16[128,256]{1,0:T(8,128)(2,1)S(1)} collective-permute-done((s16[128,256]{1,0:T(8,128)(2,1)S(1)}, s16[128,256]{1,0:T(8,128)(2,1)S(1)}, u32[]{:S(2)}, u32[]{:S(2)}) %collective-permute-start.11) | collective-permute-done | bytes 65568 | tf_op jit(solution)/shard_map/ppermute | solution.py:250
  31.3 2.0 %collective-permute-done.10.refs_2_ = s16[128,256]{1,0:T(8,128)(2,1)S(1)} collective-permute-done((s16[128,256]{1,0:T(8,128)(2,1)S(1)}, s16[128,256]{1,0:T(8,128)(2,1)S(1)}, u32[]{:S(2)}, u32[]{:S(2)}) %collective-permute-start.10) | collective-permute-done | bytes 65568 | tf_op jit(solution)/shard_map/ppermute | solution.py:250
  33.9 1.2 %round0.1 = (f32[128,256]{1,0:T(8,128)S(1)}, s16[128,256]{1,0:T(8,128)(2,1)S(1)}) custom-call(s16[128,256]{1,0:T(8,128)(2,1)S(1)} %get-tuple-element.56.refs_0_, s16[128,256]{1,0:T(8,128)(2,1)S(1)} %collective-permute-done.9.refs_1_, s16[128,256]{1,0:T(8,128)(2,1)S(1)} %collective-permute-done.10.refs_2_, ...), custom_call_target="tpu_custom_call" | custom-call | flops 536870912 | bytes 1048576 | tf_op jit(solution)/shard_map/round0/pallas_call | solution.py:22
  35.1 2.3 %collective-permute-start.14 = (s16[128,256]{1,0:T(8,128)(2,1)S(1)}, s16[128,256]{1,0:T(8,128)(2,1)S(1)}, u32[]{:S(2)}, u32[]{:S(2)}) collective-permute-start(s16[128,256]{1,0:T(8,128)(2,1)S(1)} %get-tuple-element.67.refs_0_), channel_id=1, source_target_pairs={{0,3},{1,2},{2,1},{3,0},{4,7},{5,6},{6,5},{7,4},{8,11},{9,10},{10,... | collective-permute-start | bytes 196616 | tf_op jit(solution)/shard_map/ppermute | solution.py:250
  37.8 1.8 %collective-permute-start.12 = (s16[128,256]{1,0:T(8,128)(2,1)S(1)}, s16[128,256]{1,0:T(8,128)(2,1)S(1)}, u32[]{:S(2)}, u32[]{:S(2)}) collective-permute-start(s16[128,256]{1,0:T(8,128)(2,1)S(1)} %get-tuple-element.67.refs_0_), channel_id=1, source_target_pairs={{0,2},{1,3},{2,0},{3,1},{4,6},{5,7},{6,4},{7,5},{8,10},{9,11},{10,... | collective-permute-start | bytes 196616 | tf_op jit(solution)/shard_map/ppermute | solution.py:250
  39.5 1.8 %collective-permute-done.14.refs_3_ = s16[128,256]{1,0:T(8,128)(2,1)S(1)} collective-permute-done((s16[128,256]{1,0:T(8,128)(2,1)S(1)}, s16[128,256]{1,0:T(8,128)(2,1)S(1)}, u32[]{:S(2)}, u32[]{:S(2)}) %collective-permute-start.14) | collective-permute-done | bytes 65568 | tf_op jit(solution)/shard_map/ppermute | solution.py:250
  43.1 1.3 %round1.1 = (f32[128,256]{1,0:T(8,128)S(1)}, f32[128,256]{1,0:T(8,128)S(1)}, f32[128,256]{1,0:T(8,128)S(1)}, s16[128,256]{1,0:T(8,128)(2,1)S(1)}) custom-call(s16[128,256]{1,0:T(8,128)(2,1)S(1)} %get-tuple-element.67.refs_0_, s16[128,256]{1,0:T(8,128)(2,1)S(1)} %collective-permute-done.12.refs_1_, s16[128,256]{1,0:T(8,128)(2,1)S(1)} %collective-permute-done.13.refs_2_, ...), custom_call_target="tpu_custom_call" | custom-call | flops 536870912 | bytes 1048576 | tf_op jit(solution)/shard_map/round1/pallas_call | solution.py:22
  44.5 3.1 %collective-permute-start.17 = (s16[128,256]{1,0:T(8,128)(2,1)S(1)}, s16[128,256]{1,0:T(8,128)(2,1)S(1)}, u32[]{:S(2)}, u32[]{:S(2)}) collective-permute-start(s16[128,256]{1,0:T(8,128)(2,1)S(1)} %get-tuple-element.69.refs_0_), channel_id=1, source_target_pairs={{0,3},{1,2},{2,1},{3,0},{4,7},{5,6},{6,5},{7,4},{8,11},{9,10},{10,... | collective-permute-start | bytes 196616 | tf_op jit(solution)/shard_map/ppermute | solution.py:250
  47.6 1.3 %collective-permute-start.15 = (s16[128,256]{1,0:T(8,128)(2,1)S(1)}, s16[128,256]{1,0:T(8,128)(2,1)S(1)}, u32[]{:S(2)}, u32[]{:S(2)}) collective-permute-start(s16[128,256]{1,0:T(8,128)(2,1)S(1)} %get-tuple-element.69.refs_0_), channel_id=1, source_target_pairs={{0,2},{1,3},{2,0},{3,1},{4,6},{5,7},{6,4},{7,5},{8,10},{9,11},{10,... | collective-permute-start | bytes 196616 | tf_op jit(solution)/shard_map/ppermute | solution.py:250
  48.9 2.0 %collective-permute-done.17.refs_3_ = s16[128,256]{1,0:T(8,128)(2,1)S(1)} collective-permute-done((s16[128,256]{1,0:T(8,128)(2,1)S(1)}, s16[128,256]{1,0:T(8,128)(2,1)S(1)}, u32[]{:S(2)}, u32[]{:S(2)}) %collective-permute-start.17) | collective-permute-done | bytes 65568 | tf_op jit(solution)/shard_map/ppermute | solution.py:250
  51.0 1.9 %collective-permute-done.16.refs_2_ = s16[128,256]{1,0:T(8,128)(2,1)S(1)} collective-permute-done((s16[128,256]{1,0:T(8,128)(2,1)S(1)}, s16[128,256]{1,0:T(8,128)(2,1)S(1)}, u32[]{:S(2)}, u32[]{:S(2)}) %collective-permute-start.16) | collective-permute-done | bytes 65568 | tf_op jit(solution)/shard_map/ppermute | solution.py:250
  53.8 2.5 %collective-permute-start.20 = (f32[8,128]{1,0:T(8,128)S(1)}, f32[8,128]{1,0:T(8,128)S(1)}, u32[]{:S(2)}, u32[]{:S(2)}) collective-permute-start(f32[8,128]{1,0:T(8,128)S(1)} %get-tuple-element.73.refs_0_), channel_id=1, source_target_pairs={{0,3},{1,2},{2,1},{3,0},{4,7},{5,6},{6,5},{7,4},{8,11},{9,10},{10,... | collective-permute-start | bytes 12296 | tf_op jit(solution)/shard_map/ppermute | solution.py:250
  56.3 1.9 %collective-permute-start.18 = (f32[8,128]{1,0:T(8,128)S(1)}, f32[8,128]{1,0:T(8,128)S(1)}, u32[]{:S(2)}, u32[]{:S(2)}) collective-permute-start(f32[8,128]{1,0:T(8,128)S(1)} %get-tuple-element.73.refs_0_), channel_id=1, source_target_pairs={{0,2},{1,3},{2,0},{3,1},{4,6},{5,7},{6,4},{7,5},{8,10},{9,11},{10,... | collective-permute-start | bytes 12296 | tf_op jit(solution)/shard_map/ppermute | solution.py:250
  58.2 1.0 %collective-permute-done.20.refs_3_ = f32[8,128]{1,0:T(8,128)S(1)} collective-permute-done((f32[8,128]{1,0:T(8,128)S(1)}, f32[8,128]{1,0:T(8,128)S(1)}, u32[]{:S(2)}, u32[]{:S(2)}) %collective-permute-start.20) | collective-permute-done | bytes 4128 | tf_op jit(solution)/shard_map/ppermute | solution.py:250
  (42 shorter events, 14.9 us)
Async XLA Ops:
  0.0 8.4 %collective-permute-start.1 = (bf16[4,256,256]{2,1,0:T(8,128)(2,1)}, bf16[4,256,256]{2,1,0:T(8,128)(2,1)S(1)}, u32[]{:S(2)}, u32[]{:S(2)}) collective-permute-start(bf16[4,256,256]{2,1,0:T(8,128)(2,1)} %refs_4_.4), channel_id=1, source_target_pairs={{0,4},{4,0},{8,12},{12,8},{16,20},{20,16},{24,28},{28,24},{1,5},{5... | collective-permute-start | bytes 1572872 | tf_op jit(solution)/shard_map/ppermute | solution.py:250
  0.5 10.5 %collective-permute-start = (bf16[4,256,256]{2,1,0:T(8,128)(2,1)}, bf16[4,256,256]{2,1,0:T(8,128)(2,1)S(1)}, u32[]{:S(2)}, u32[]{:S(2)}) collective-permute-start(bf16[4,256,256]{2,1,0:T(8,128)(2,1)} %refs_4_.4), channel_id=1, source_target_pairs={{0,8},{4,20},{8,0},{12,28},{16,24},{20,4},{24,16},{28,12},{1,9},{5... | collective-permute-start | bytes 1572872 | tf_op jit(solution)/shard_map/ppermute | solution.py:250
  2.9 0.7 %copy-start.4 = (s32[1,2]{1,0:T(1,128)S(1)}, s32[1,2]{1,0:T(1,128)}, u32[]{:S(2)}) copy-start(s32[1,2]{1,0:T(1,128)} %param.8) | copy-start | bytes 28
  5.4 1.4 %copy-start.1 = (bf16[4,256,256]{2,1,0:T(8,128)(2,1)S(1)}, bf16[4,256,256]{2,1,0:T(8,128)(2,1)}, u32[]{:S(2)}) copy-start(bf16[4,256,256]{2,1,0:T(8,128)(2,1)} %refs_4_.4) | copy-start | bytes 1572868
  5.4 3.0 %copy-start = (bf16[128,256]{1,0:T(8,128)(2,1)S(1)}, bf16[128,256]{1,0:T(8,128)(2,1)}, u32[]{:S(2)}) copy-start(bf16[128,256]{1,0:T(8,128)(2,1)} %refs_4_.7) | copy-start | bytes 196612
  6.8 9.2 %collective-permute-start.5 = (bf16[4,256,256]{2,1,0:T(8,128)(2,1)S(1)}, bf16[4,256,256]{2,1,0:T(8,128)(2,1)S(1)}, u32[]{:S(2)}, u32[]{:S(2)}) collective-permute-start(bf16[4,256,256]{2,1,0:T(8,128)(2,1)S(1)} %copy-done.1), channel_id=1, source_target_pairs={{0,16},{4,12},{8,24},{12,4},{16,0},{20,28},{24,8},{28,20},{1,17},{... | collective-permute-start | bytes 1572872 | tf_op jit(solution)/shard_map/ppermute | solution.py:250
  11.0 10.8 %collective-permute-start.2 = (bf16[4,256,256]{2,1,0:T(8,128)(2,1)S(1)}, bf16[4,256,256]{2,1,0:T(8,128)(2,1)S(1)}, u32[]{:S(2)}, u32[]{:S(2)}) collective-permute-start(bf16[4,256,256]{2,1,0:T(8,128)(2,1)S(1)} %collective-permute-done.refs_4_), channel_id=1, source_target_pairs={{0,16},{4,12},{8,24},{12,4},{16,0},{20,28},{24,8},{28,20},{1,17},{... | collective-permute-start | bytes 1572872 | tf_op jit(solution)/shard_map/ppermute | solution.py:250
  16.1 1.5 %collective-permute-start.4 = (bf16[4,128,256]{2,1,0:T(8,128)(2,1)S(1)}, bf16[4,128,256]{2,1,0:T(8,128)(2,1)S(1)}, u32[]{:S(2)}, u32[]{:S(2)}) collective-permute-start(bf16[4,128,256]{2,1,0:T(8,128)(2,1)S(1)} %get-tuple-element.79), channel_id=1, source_target_pairs={{0,4},{4,0},{8,12},{12,8},{16,20},{20,16},{24,28},{28,24},{1,5},{5... | collective-permute-start | bytes 786440 | tf_op jit(solution)/shard_map/ppermute | solution.py:250
  16.1 1.9 %collective-permute-start.3 = (bf16[4,128,256]{2,1,0:T(8,128)(2,1)S(1)}, bf16[4,128,256]{2,1,0:T(8,128)(2,1)S(1)}, u32[]{:S(2)}, u32[]{:S(2)}) collective-permute-start(bf16[4,128,256]{2,1,0:T(8,128)(2,1)S(1)} %get-tuple-element.80), channel_id=1, source_target_pairs={{0,4},{4,0},{8,12},{12,8},{16,20},{20,16},{24,28},{28,24},{1,5},{5... | collective-permute-start | bytes 786440 | tf_op jit(solution)/shard_map/ppermute | solution.py:250
  16.6 1.7 %collective-permute-start.7 = (bf16[4,128,256]{2,1,0:T(8,128)(2,1)S(1)}, bf16[4,128,256]{2,1,0:T(8,128)(2,1)S(1)}, u32[]{:S(2)}, u32[]{:S(2)}) collective-permute-start(bf16[4,128,256]{2,1,0:T(8,128)(2,1)S(1)} %get-tuple-element.77), channel_id=1, source_target_pairs={{0,4},{4,0},{8,12},{12,8},{16,20},{20,16},{24,28},{28,24},{1,5},{5... | collective-permute-start | bytes 786440 | tf_op jit(solution)/shard_map/ppermute | solution.py:250
  16.7 2.0 %collective-permute-start.6 = (bf16[4,128,256]{2,1,0:T(8,128)(2,1)S(1)}, bf16[4,128,256]{2,1,0:T(8,128)(2,1)S(1)}, u32[]{:S(2)}, u32[]{:S(2)}) collective-permute-start(bf16[4,128,256]{2,1,0:T(8,128)(2,1)S(1)} %get-tuple-element.78), channel_id=1, source_target_pairs={{0,4},{4,0},{8,12},{12,8},{16,20},{20,16},{24,28},{28,24},{1,5},{5... | collective-permute-start | bytes 786440 | tf_op jit(solution)/shard_map/ppermute | solution.py:250
  21.8 1.9 %collective-permute-start.8 = (bf16[4,256,256]{2,1,0:T(8,128)(2,1)S(1)}, bf16[4,256,256]{2,1,0:T(8,128)(2,1)S(1)}, u32[]{:S(2)}, u32[]{:S(2)}) collective-permute-start(bf16[4,256,256]{2,1,0:T(8,128)(2,1)S(1)} %collective-permute-done.2.refs_4_), channel_id=1, source_target_pairs={{0,4},{4,0},{8,12},{12,8},{16,20},{20,16},{24,28},{28,24},{1,5},{5... | collective-permute-start | bytes 1572872 | tf_op jit(solution)/shard_map/ppermute | solution.py:250
  24.5 6.8 %collective-permute-start.11 = (s16[128,256]{1,0:T(8,128)(2,1)S(1)}, s16[128,256]{1,0:T(8,128)(2,1)S(1)}, u32[]{:S(2)}, u32[]{:S(2)}) collective-permute-start(s16[128,256]{1,0:T(8,128)(2,1)S(1)} %get-tuple-element.56.refs_0_), channel_id=1, source_target_pairs={{0,3},{1,2},{2,1},{3,0},{4,7},{5,6},{6,5},{7,4},{8,11},{9,10},{10,... | collective-permute-start | bytes 196616 | tf_op jit(solution)/shard_map/ppermute | solution.py:250
  28.1 5.2 %collective-permute-start.10 = (s16[128,256]{1,0:T(8,128)(2,1)S(1)}, s16[128,256]{1,0:T(8,128)(2,1)S(1)}, u32[]{:S(2)}, u32[]{:S(2)}) collective-permute-start(s16[128,256]{1,0:T(8,128)(2,1)S(1)} %get-tuple-element.56.refs_0_), channel_id=1, source_target_pairs={{0,1},{1,0},{2,3},{3,2},{4,5},{5,4},{6,7},{7,6},{8,9},{9,8},{10,11... | collective-permute-start | bytes 196616 | tf_op jit(solution)/shard_map/ppermute | solution.py:250
  28.1 5.9 %collective-permute-start.9 = (s16[128,256]{1,0:T(8,128)(2,1)S(1)}, s16[128,256]{1,0:T(8,128)(2,1)S(1)}, u32[]{:S(2)}, u32[]{:S(2)}) collective-permute-start(s16[128,256]{1,0:T(8,128)(2,1)S(1)} %get-tuple-element.56.refs_0_), channel_id=1, source_target_pairs={{0,2},{1,3},{2,0},{3,1},{4,6},{5,7},{6,4},{7,5},{8,10},{9,11},{10,... | collective-permute-start | bytes 196616 | tf_op jit(solution)/shard_map/ppermute | solution.py:250
  35.1 6.3 %collective-permute-start.14 = (s16[128,256]{1,0:T(8,128)(2,1)S(1)}, s16[128,256]{1,0:T(8,128)(2,1)S(1)}, u32[]{:S(2)}, u32[]{:S(2)}) collective-permute-start(s16[128,256]{1,0:T(8,128)(2,1)S(1)} %get-tuple-element.67.refs_0_), channel_id=1, source_target_pairs={{0,3},{1,2},{2,1},{3,0},{4,7},{5,6},{6,5},{7,4},{8,11},{9,10},{10,... | collective-permute-start | bytes 196616 | tf_op jit(solution)/shard_map/ppermute | solution.py:250
  37.4 4.9 %collective-permute-start.13 = (s16[128,256]{1,0:T(8,128)(2,1)S(1)}, s16[128,256]{1,0:T(8,128)(2,1)S(1)}, u32[]{:S(2)}, u32[]{:S(2)}) collective-permute-start(s16[128,256]{1,0:T(8,128)(2,1)S(1)} %get-tuple-element.67.refs_0_), channel_id=1, source_target_pairs={{0,1},{1,0},{2,3},{3,2},{4,5},{5,4},{6,7},{7,6},{8,9},{9,8},{10,11... | collective-permute-start | bytes 196616 | tf_op jit(solution)/shard_map/ppermute | solution.py:250
  37.8 5.4 %collective-permute-start.12 = (s16[128,256]{1,0:T(8,128)(2,1)S(1)}, s16[128,256]{1,0:T(8,128)(2,1)S(1)}, u32[]{:S(2)}, u32[]{:S(2)}) collective-permute-start(s16[128,256]{1,0:T(8,128)(2,1)S(1)} %get-tuple-element.67.refs_0_), channel_id=1, source_target_pairs={{0,2},{1,3},{2,0},{3,1},{4,6},{5,7},{6,4},{7,5},{8,10},{9,11},{10,... | collective-permute-start | bytes 196616 | tf_op jit(solution)/shard_map/ppermute | solution.py:250
  44.5 6.5 %collective-permute-start.17 = (s16[128,256]{1,0:T(8,128)(2,1)S(1)}, s16[128,256]{1,0:T(8,128)(2,1)S(1)}, u32[]{:S(2)}, u32[]{:S(2)}) collective-permute-start(s16[128,256]{1,0:T(8,128)(2,1)S(1)} %get-tuple-element.69.refs_0_), channel_id=1, source_target_pairs={{0,3},{1,2},{2,1},{3,0},{4,7},{5,6},{6,5},{7,4},{8,11},{9,10},{10,... | collective-permute-start | bytes 196616 | tf_op jit(solution)/shard_map/ppermute | solution.py:250
  47.6 5.2 %collective-permute-start.16 = (s16[128,256]{1,0:T(8,128)(2,1)S(1)}, s16[128,256]{1,0:T(8,128)(2,1)S(1)}, u32[]{:S(2)}, u32[]{:S(2)}) collective-permute-start(s16[128,256]{1,0:T(8,128)(2,1)S(1)} %get-tuple-element.69.refs_0_), channel_id=1, source_target_pairs={{0,1},{1,0},{2,3},{3,2},{4,5},{5,4},{6,7},{7,6},{8,9},{9,8},{10,11... | collective-permute-start | bytes 196616 | tf_op jit(solution)/shard_map/ppermute | solution.py:250
  47.6 5.2 %collective-permute-start.15 = (s16[128,256]{1,0:T(8,128)(2,1)S(1)}, s16[128,256]{1,0:T(8,128)(2,1)S(1)}, u32[]{:S(2)}, u32[]{:S(2)}) collective-permute-start(s16[128,256]{1,0:T(8,128)(2,1)S(1)} %get-tuple-element.69.refs_0_), channel_id=1, source_target_pairs={{0,2},{1,3},{2,0},{3,1},{4,6},{5,7},{6,4},{7,5},{8,10},{9,11},{10,... | collective-permute-start | bytes 196616 | tf_op jit(solution)/shard_map/ppermute | solution.py:250
  53.8 5.4 %collective-permute-start.20 = (f32[8,128]{1,0:T(8,128)S(1)}, f32[8,128]{1,0:T(8,128)S(1)}, u32[]{:S(2)}, u32[]{:S(2)}) collective-permute-start(f32[8,128]{1,0:T(8,128)S(1)} %get-tuple-element.73.refs_0_), channel_id=1, source_target_pairs={{0,3},{1,2},{2,1},{3,0},{4,7},{5,6},{6,5},{7,4},{8,11},{9,10},{10,... | collective-permute-start | bytes 12296 | tf_op jit(solution)/shard_map/ppermute | solution.py:250
  56.3 3.6 %collective-permute-start.19 = (f32[8,128]{1,0:T(8,128)S(1)}, f32[8,128]{1,0:T(8,128)S(1)}, u32[]{:S(2)}, u32[]{:S(2)}) collective-permute-start(f32[8,128]{1,0:T(8,128)S(1)} %get-tuple-element.73.refs_0_), channel_id=1, source_target_pairs={{0,1},{1,0},{2,3},{3,2},{4,5},{5,4},{6,7},{7,6},{8,9},{9,8},{10,11... | collective-permute-start | bytes 12296 | tf_op jit(solution)/shard_map/ppermute | solution.py:250
  56.3 4.5 %collective-permute-start.18 = (f32[8,128]{1,0:T(8,128)S(1)}, f32[8,128]{1,0:T(8,128)S(1)}, u32[]{:S(2)}, u32[]{:S(2)}) collective-permute-start(f32[8,128]{1,0:T(8,128)S(1)} %get-tuple-element.73.refs_0_), channel_id=1, source_target_pairs={{0,2},{1,3},{2,0},{3,1},{4,6},{5,7},{6,4},{7,5},{8,10},{9,11},{10,... | collective-permute-start | bytes 12296 | tf_op jit(solution)/shard_map/ppermute | solution.py:250
  (2 other events, 1.3 us)

commit v5 on v4

--- a/solution.py
+++ b/solution.py
@@ -108,7 +108,7 @@
                 out_ref[p, :, block] = bits * conf_ref[...]
 
 
-def gather_kernel(pieces, rows, first, last, *refs):
+def gather_kernel(pieces, rows, first, last, closing, *refs):
     info_ref, alpha_ref, conf_ref, prev_ref = refs[:4]
     at = 4
     arrays = refs[at : at + len(pieces)]
@@ -165,9 +165,81 @@
         image = image + jnp.dot(prev, high, preferred_element_type=F32)
         image = image + jnp.dot(prev, low, preferred_element_type=F32)
         pack((1.0 + conf_ref[...]) * rhs - image, msg_ref)
+    elif closing:
+        high = gram.astype(BF16)
+        low = (gram - high.astype(F32)).astype(BF16)
+        image = image + jnp.dot(prev, high, preferred_element_type=F32)
+        image = image + jnp.dot(prev, low, preferred_element_type=F32)
+        sums_ref[...] = (1.0 + conf_ref[...]) * rhs - image
     else:
         sums_ref[0] = rhs
         sums_ref[1] = image
+
+
+def add_gram(gram, pieces, arrays, rows, info_ref, obs):
+    me = info_ref[0]
+    for (_, pair, offset, length), ref in zip(pieces, arrays):
+        slot = lax.broadcasted_iota(jnp.int32, (length, gram.shape[0]), 0)
+        slot = slot + (shard_index(me, pair) * rows + offset)
+        for t in range(ref.shape[0]):
+            tile_rows = ref[t]
+            masked = jnp.where(slot < info_ref[1 + obs + t], tile_rows, jnp.zeros_like(tile_rows))
+            gram = gram + lax.dot_general(
+                masked, tile_rows, (((0,), (0,)), ((), ())), preferred_element_type=F32
+            )
+    return gram
+
+
+def keep_kernel(in_ref, out_ref):
+    for index in range(in_ref.shape[0]):
+        out_ref[index] = in_ref[index]
+
+
+def twin_kernel(pieces, rows, info_ref, twin_info_ref, alpha_ref, prev_ref, *refs):
+    *arrays, part_ref = refs
+    users, rank = prev_ref.shape
+    obs = alpha_ref.shape[0]
+    prev = prev_ref[...]
+    gram = add_gram(jnp.zeros((rank, rank), F32), pieces, arrays, rows, info_ref, obs)
+    rhs = jnp.zeros((users, rank), F32)
+    image = jnp.zeros((users, rank), F32)
+    conf = jnp.zeros((users, 1), F32)
+    for p in range(obs):
+        tile = twin_info_ref[1 + p]
+        conf = jnp.maximum(conf, jnp.max(alpha_ref[p], axis=1, keepdims=True))
+        for (spot, _, _, length), ref in zip(pieces, arrays):
+            items = ref[tile]
+            alpha = alpha_ref[p, :, spot : spot + length]
+            scores = jnp.dot(prev, items.T, preferred_element_type=F32)
+            weights = (alpha * scores).astype(BF16)
+            seen = jnp.where(alpha > 0.0, 1.0, 0.0).astype(BF16)
+            rhs = rhs + jnp.dot(seen, items, preferred_element_type=F32)
+            image = image + jnp.dot(weights, items, preferred_element_type=F32)
+    high = gram.astype(BF16)
+    low = (gram - high.astype(F32)).astype(BF16)
+    image = image + jnp.dot(prev, high, preferred_element_type=F32)
+    image = image + jnp.dot(prev, low, preferred_element_type=F32)
+    part_ref[...] = (1.0 + conf) * rhs - image
+
+
+def join_kernel(mine_ref, part_ref, msg_ref):
+    pack(mine_ref[...] + part_ref[...], msg_ref)
+
+
+def collect_kernel(pieces, rows, info_ref, gram_ref, *refs):
+    arrays = refs[: len(pieces)]
+    picked_ref, turned_ref, high_ref, low_ref = refs[len(pieces) :]
+    obs = picked_ref.shape[0]
+    for p in range(obs):
+        tile = info_ref[1 + p]
+        for (spot, _, _, length), ref in zip(pieces, arrays):
+            picked_ref[p, spot : spot + length, :] = ref[tile]
+        for block in blocks(picked_ref.shape[1]):
+            turned_ref[p, :, block] = picked_ref[p, block, :].T
+    gram = add_gram(gram_ref[...], pieces, arrays, rows, info_ref, obs)
+    high = gram.astype(BF16)
+    high_ref[...] = high
+    low_ref[...] = (gram - high.astype(F32)).astype(BF16)
 
 
 def in_order(refs, order):
@@ -254,7 +326,7 @@
     return lax.optimization_barrier((array, token))[0]
 
 
-def gather_stages(own, size, plan, work):
+def gather_stages(own, size, plan, work, prepare, finish):
     send = functools.partial(permuted, axis="row", size=size)
     held = {0: own}
     bit = 8 if size >= 8 else 1
@@ -289,13 +361,13 @@
     one = [first_way(a) for a in held.values()]
     two = [second_way(tied(a, early)) for a in held.values()]
     token = work([x for a in held.values() for x in (a, twin(a))])
-    one = [tied(a, token) for a in one]
+    ready = prepare(twin)
+    one = [tied(a, (token, ready)) for a in one]
     two = [tied(a, token) for a in two]
     far = [second_way(a) for a in one]
     token = work([x for a, b in zip(one, two) for x in (a, twin(a[:, :half]), twin(a[:, half:]), b, twin(b[:, :half]), twin(b[:, half:]))])
     far = [tied(a, token) for a in far]
-    work(far)
-    work([twin(a) for a in far])
+    finish(far, twin, ready)
 
 
 def local(mesh, item_factors, tile_counts, observed_tiles, mask_words, confidence, previous):
@@ -310,6 +382,7 @@
     shape = jax.ShapeDtypeStruct
 
     message = shape((users, rank), jnp.int16)
+    vec = shape((users, rank), F32)
     sums = shape((2, users, rank), F32)
     gram_shape = shape((rank, rank), F32)
     stages, picked, turned, alphas, carry, scalars = [], [], [], [], [], []
@@ -337,16 +410,16 @@
         scalars.append(kept_info)
         return alphas
 
-    def work(arrays):
+    def work(arrays, closing=False):
         index = len(picked)
         first, last = index == 0, index == len(stages) - 1
         pieces, alpha = stages[index], alphas[index]
         size = alpha.shape[2]
         split = shape((rank, rank), BF16)
         kept, kept_turned, *carried = call(
-            functools.partial(gather_kernel, pieces, rows, first, last),
+            functools.partial(gather_kernel, pieces, rows, first, last, closing),
             [shape((obs, size, rank), BF16), shape((obs, rank, size), BF16)]
-            + ([split, split, message] if last else [gram_shape, sums]),
+            + ([split, split, message] if last else [gram_shape, vec if closing else sums]),
             (*scalars, alpha, conf, previous, *arrays, *carry),
             1,
             2 * size * rank * (tiles * rank + 3 * obs * users),
@@ -357,7 +430,40 @@
         turned.append(kept_turned)
         return carried, alphas
 
-    gather_stages(item_factors, n_row, masks_of, work)
+    def prepare(twin):
+        (twin_info,) = call(keep_kernel, [], (twin(info),), 1, 0, "keep", [shape(info.shape, info.dtype)])
+        return twin_info, twin(alphas[3]), twin(previous)
+
+    def finish(far, twin, ready):
+        pieces, alpha = stages[2], alphas[3]
+        twin_info, twin_alpha, twin_prev = ready
+        size = alpha.shape[2]
+        flops = 2 * size * rank * (tiles * rank + 3 * obs * users)
+        (part,) = call(
+            functools.partial(twin_kernel, pieces, rows),
+            [vec],
+            (*scalars, twin_info, twin_alpha, twin_prev, *far),
+            2,
+            flops,
+            "twin",
+        )
+        part = twin(part)
+        gram, mine = work(far, True)[0]
+        (msg,) = call(join_kernel, [message], (mine, part), 0, 0, "join")
+        others = [twin(tied(a, msg)) for a in far]
+        kept, kept_turned, high, low = call(
+            functools.partial(collect_kernel, stages[3], rows),
+            [shape((obs, size, rank), BF16), shape((obs, rank, size), BF16)] + [shape((rank, rank), BF16)] * 2,
+            (*scalars, gram, *others),
+            1,
+            flops,
+            "collect",
+        )
+        picked.append(kept)
+        turned.append(kept_turned)
+        carry[:] = high, low, msg
+
+    gather_stages(item_factors, n_row, masks_of, work, prepare, finish)
     high, low, msg = carry
 
     order = [0, *range(2, n_col, 2), *range(1, n_col, 2)]
@@ -365,7 +471,6 @@
     def to_all(own):
         return [own] + [permuted(own, "col", n_col, lambda i: i ^ bits) for bits in order[1:]]
 
-    vec = shape((users, rank), F32)
     state = []
     for index in range(ITERS):
         last = index == ITERS - 1

time: 61.8 us -> 61.7 us (level)
  waiting for transfers between devices: 22.2 us -> 20.7 us
  Pallas kernels: 9.73 us -> 10.7 us
    ppermute x21 -> x25, waiting for transfers between devices: 22.2 us -> 20.7 us  [permuted(): return lax.ppermute(array, axis, [(i, target(i)) for i in range(size)])]
    pallas_call x8 -> x11, Pallas kernels: 8.92 us -> 9.89 us  [call(): pl.pallas_call(body, out_shape=[pltpu.VMEM(o.shape, o.dtype) for o in out...]
    ppermute x21 -> x25, starting transfers between devices: 27 us -> 27.4 us  [permuted(): return lax.ppermute(array, axis, [(i, target(i)) for i in range(size)])]
  transfers between devices with their start and end apart: 21 -> 25, of which waited for: 19 -> 20; matrix products, arithmetic and copies ran while one was open for 2% -> 2% of each run, Pallas kernels for 8% -> 9%
where the time goes in v5:
time: 61.7 us; the launch traced here: 61.5 us
  starting transfers between devices  27.4 us (44%)
  waiting for transfers between devices  20.7 us (34%)
  Pallas kernels  10.7 us (17%)
  local copies, waits for them, and re-layouts  1.52 us (2%)
  other arithmetic  1.04 us (2%)
    ppermute x25, starting transfers between devices, permuted(): return lax.ppermute(array, axis, [(i, target(i)) for i in range(size)])  27.4 us
    ppermute x25, waiting for transfers between devices, permuted(): return lax.ppermute(array, axis, [(i, target(i)) for i in range(size)])  20.7 us
    pallas_call x11, Pallas kernels, call(): pl.pallas_call(body, out_shape=[pltpu.VMEM(o.shape, o.dtype) for o in out...  9.89 us
    unnamed x10, local copies, waits for them, and re-layouts  1.34 us
  transfers between devices with their start and end apart: 25, of which 20 were waited for; matrix products, arithmetic and copies ran while one was open for 2% of the time, Pallas kernels for 9%

profile of v5, /device:TPU:0, one launch (start us, length us, event | category | flops | bytes accessed | tf_op | source)
XLA Modules:
  0.0 61.5 jit_solution(6725494743701940518)
XLA Ops:
  0.5 2.5 %collective-permute-start = (bf16[4,256,256]{2,1,0:T(8,128)(2,1)}, bf16[4,256,256]{2,1,0:T(8,128)(2,1)S(1)}, u32[]{:S(2)}, u32[]{:S(2)}) collective-permute-start(bf16[4,256,256]{2,1,0:T(8,128)(2,1)} %refs_4_.4), channel_id=1, source_target_pairs={{0,8},{4,20},{8,0},{12,28},{16,24},{20,4},{24,16},{28,12},{1,9},{5... | collective-permute-start | bytes 1572872 | tf_op jit(solution)/shard_map/ppermute | solution.py:322
  5.5 1.3 %masks.1 = (f32[2,128,512]{2,1,0:T(8,128)S(1)}, f32[2,128,1024]{2,1,0:T(8,128)S(1)}, f32[2,128,256]{2,1,0:T(8,128)S(1)}, f32[2,128,256]{2,1,0:T(8,128)S(1)}, s32[7]{0:T(128)S(4)}) custom-call(s32[7]{0:T(128)S(1)} %pad_add_fusion.info_ref, bf16[2,128,256]{2,1,0:T(8,128)(2,1)S(1)} %fusion.words_ref, f32[128,1]{1,0:T(8,128)S(1)} %copy.8.conf_ref.refs_2_), custom_call_target="tpu_custom_call" | custom-call | flops 268435456 | bytes 1048576 | tf_op jit(solution)/shard_map/masks/pallas_call | solution.py:22
  6.8 1.6 %collective-permute-start.8 = (bf16[4,256,256]{2,1,0:T(8,128)(2,1)S(1)}, bf16[4,256,256]{2,1,0:T(8,128)(2,1)S(1)}, u32[]{:S(2)}, u32[]{:S(2)}) collective-permute-start(bf16[4,256,256]{2,1,0:T(8,128)(2,1)S(1)} %copy-done.1), channel_id=1, source_target_pairs={{0,16},{4,12},{8,24},{12,4},{16,0},{20,28},{24,8},{28,20},{1,17},{... | collective-permute-start | bytes 1572872 | tf_op jit(solution)/shard_map/ppermute | solution.py:322
  8.9 1.0 %collective-permute-done.2.in_ref = s32[7]{0:T(128)S(1)} collective-permute-done((s32[7]{0:T(128)S(1)}, s32[7]{0:T(128)S(1)}, u32[]{:S(2)}, u32[]{:S(2)}) %collective-permute-start.2) | collective-permute-done | bytes 60 | tf_op jit(solution)/shard_map/ppermute | solution.py:322
  11.6 3.1 %collective-permute-start.5 = (bf16[4,256,256]{2,1,0:T(8,128)(2,1)S(1)}, bf16[4,256,256]{2,1,0:T(8,128)(2,1)S(1)}, u32[]{:S(2)}, u32[]{:S(2)}) collective-permute-start(bf16[4,256,256]{2,1,0:T(8,128)(2,1)S(1)} %collective-permute-done.refs_4_), channel_id=1, source_target_pairs={{0,16},{4,12},{8,24},{12,4},{16,0},{20,28},{24,8},{28,20},{1,17},{... | collective-permute-start | bytes 1572872 | tf_op jit(solution)/shard_map/ppermute | solution.py:322
  14.7 1.4 %collective-permute-done.8.refs_7_ = bf16[4,256,256]{2,1,0:T(8,128)(2,1)S(1)} collective-permute-done((bf16[4,256,256]{2,1,0:T(8,128)(2,1)S(1)}, bf16[4,256,256]{2,1,0:T(8,128)(2,1)S(1)}, u32[]{:S(2)}, u32[]{:S(2)}) %collective-permute-start.8) | collective-permute-done | bytes 524320 | tf_op jit(solution)/shard_map/ppermute | solution.py:322
  18.7 1.9 %stage.4 = (bf16[2,1024,256]{2,1,0:T(8,128)(2,1)S(1)}, bf16[2,256,1024]{2,1,0:T(8,128)(2,1)S(1)}, f32[256,256]{1,0:T(8,128)S(1)}, f32[2,128,256]{2,1,0:T(8,128)S(1)}) custom-call(s32[7]{0:T(128)S(4)} %get-tuple-element.41.refs_0_.info_ref, f32[2,128,1024]{2,1,0:T(8,128)S(1)} %get-tuple-element.46.refs_1_.refs_8_, f32[128,1]{1,0:T(8,128)S(1)} %copy.8.conf_ref.refs_2_, ...), custom_call_target="tpu_custom_call" | custom-call | flops 939524096 | bytes 1048576 | tf_op jit(solution)/shard_map/stage/pallas_call | solution.py:22
  20.6 1.2 %collective-permute-done.5.refs_4_.refs_0_ = bf16[4,256,256]{2,1,0:T(8,128)(2,1)S(1)} collective-permute-done((bf16[4,256,256]{2,1,0:T(8,128)(2,1)S(1)}, bf16[4,256,256]{2,1,0:T(8,128)(2,1)S(1)}, u32[]{:S(2)}, u32[]{:S(2)}) %collective-permute-start.5) | collective-permute-done | bytes 524320 | tf_op jit(solution)/shard_map/ppermute | solution.py:322
  24.2 3.6 %collective-permute-start.14 = (s16[128,256]{1,0:T(8,128)(2,1)S(1)}, s16[128,256]{1,0:T(8,128)(2,1)S(1)}, u32[]{:S(2)}, u32[]{:S(2)}) collective-permute-start(s16[128,256]{1,0:T(8,128)(2,1)S(1)} %join.1.refs_0_), channel_id=1, source_target_pairs={{0,3},{1,2},{2,1},{3,0},{4,7},{5,6},{6,5},{7,4},{8,11},{9,10},{10,... | collective-permute-start | bytes 196616 | tf_op jit(solution)/shard_map/ppermute | solution.py:322
  29.0 2.0 %collective-permute-done.14.refs_3_ = s16[128,256]{1,0:T(8,128)(2,1)S(1)} collective-permute-done((s16[128,256]{1,0:T(8,128)(2,1)S(1)}, s16[128,256]{1,0:T(8,128)(2,1)S(1)}, u32[]{:S(2)}, u32[]{:S(2)}) %collective-permute-start.14) | collective-permute-done | bytes 65568 | tf_op jit(solution)/shard_map/ppermute | solution.py:322
  31.0 2.1 %collective-permute-done.13.refs_2_ = s16[128,256]{1,0:T(8,128)(2,1)S(1)} collective-permute-done((s16[128,256]{1,0:T(8,128)(2,1)S(1)}, s16[128,256]{1,0:T(8,128)(2,1)S(1)}, u32[]{:S(2)}, u32[]{:S(2)}) %collective-permute-start.13) | collective-permute-done | bytes 65568 | tf_op jit(solution)/shard_map/ppermute | solution.py:322
  33.7 1.2 %round0.1 = (f32[128,256]{1,0:T(8,128)S(1)}, s16[128,256]{1,0:T(8,128)(2,1)S(1)}) custom-call(s16[128,256]{1,0:T(8,128)(2,1)S(1)} %join.1.refs_0_, s16[128,256]{1,0:T(8,128)(2,1)S(1)} %collective-permute-done.12.refs_1_, s16[128,256]{1,0:T(8,128)(2,1)S(1)} %collective-permute-done.13.refs_2_, s16[128,256]{1,0:T(8,128)(2,1)S(1)} %collective-permute-done.14.refs_3_, ...), custom_call_target="tpu_custom_call" | custom-call | flops 536870912 | bytes 1048576 | tf_op jit(solution)/shard_map/round0/pallas_call | solution.py:22
  34.8 2.3 %collective-permute-start.18 = (s16[128,256]{1,0:T(8,128)(2,1)S(1)}, s16[128,256]{1,0:T(8,128)(2,1)S(1)}, u32[]{:S(2)}, u32[]{:S(2)}) collective-permute-start(s16[128,256]{1,0:T(8,128)(2,1)S(1)} %get-tuple-element.67.refs_0_), channel_id=1, source_target_pairs={{0,3},{1,2},{2,1},{3,0},{4,7},{5,6},{6,5},{7,4},{8,11},{9,10},{10,... | collective-permute-start | bytes 196616 | tf_op jit(solution)/shard_map/ppermute | solution.py:322
  37.6 1.7 %collective-permute-start.16 = (s16[128,256]{1,0:T(8,128)(2,1)S(1)}, s16[128,256]{1,0:T(8,128)(2,1)S(1)}, u32[]{:S(2)}, u32[]{:S(2)}) collective-permute-start(s16[128,256]{1,0:T(8,128)(2,1)S(1)} %get-tuple-element.67.refs_0_), channel_id=1, source_target_pairs={{0,2},{1,3},{2,0},{3,1},{4,6},{5,7},{6,4},{7,5},{8,10},{9,11},{10,... | collective-permute-start | bytes 196616 | tf_op jit(solution)/shard_map/ppermute | solution.py:322
  39.3 1.8 %collective-permute-done.18.refs_3_ = s16[128,256]{1,0:T(8,128)(2,1)S(1)} collective-permute-done((s16[128,256]{1,0:T(8,128)(2,1)S(1)}, s16[128,256]{1,0:T(8,128)(2,1)S(1)}, u32[]{:S(2)}, u32[]{:S(2)}) %collective-permute-start.18) | collective-permute-done | bytes 65568 | tf_op jit(solution)/shard_map/ppermute | solution.py:322
  41.1 1.1 %collective-permute-done.17.refs_2_ = s16[128,256]{1,0:T(8,128)(2,1)S(1)} collective-permute-done((s16[128,256]{1,0:T(8,128)(2,1)S(1)}, s16[128,256]{1,0:T(8,128)(2,1)S(1)}, u32[]{:S(2)}, u32[]{:S(2)}) %collective-permute-start.17) | collective-permute-done | bytes 65568 | tf_op jit(solution)/shard_map/ppermute | solution.py:322
  43.0 1.3 %round1.1 = (f32[128,256]{1,0:T(8,128)S(1)}, f32[128,256]{1,0:T(8,128)S(1)}, f32[128,256]{1,0:T(8,128)S(1)}, s16[128,256]{1,0:T(8,128)(2,1)S(1)}) custom-call(s16[128,256]{1,0:T(8,128)(2,1)S(1)} %get-tuple-element.67.refs_0_, s16[128,256]{1,0:T(8,128)(2,1)S(1)} %collective-permute-done.16.refs_1_, s16[128,256]{1,0:T(8,128)(2,1)S(1)} %collective-permute-done.17.refs_2_, ...), custom_call_target="tpu_custom_call" | custom-call | flops 536870912 | bytes 1048576 | tf_op jit(solution)/shard_map/round1/pallas_call | solution.py:22
  44.3 3.1 %collective-permute-start.21 = (s16[128,256]{1,0:T(8,128)(2,1)S(1)}, s16[128,256]{1,0:T(8,128)(2,1)S(1)}, u32[]{:S(2)}, u32[]{:S(2)}) collective-permute-start(s16[128,256]{1,0:T(8,128)(2,1)S(1)} %get-tuple-element.69.refs_0_), channel_id=1, source_target_pairs={{0,3},{1,2},{2,1},{3,0},{4,7},{5,6},{6,5},{7,4},{8,11},{9,10},{10,... | collective-permute-start | bytes 196616 | tf_op jit(solution)/shard_map/ppermute | solution.py:322
  47.5 1.3 %collective-permute-start.19 = (s16[128,256]{1,0:T(8,128)(2,1)S(1)}, s16[128,256]{1,0:T(8,128)(2,1)S(1)}, u32[]{:S(2)}, u32[]{:S(2)}) collective-permute-start(s16[128,256]{1,0:T(8,128)(2,1)S(1)} %get-tuple-element.69.refs_0_), channel_id=1, source_target_pairs={{0,2},{1,3},{2,0},{3,1},{4,6},{5,7},{6,4},{7,5},{8,10},{9,11},{10,... | collective-permute-start | bytes 196616 | tf_op jit(solution)/shard_map/ppermute | solution.py:322
  48.8 2.0 %collective-permute-done.21.refs_3_ = s16[128,256]{1,0:T(8,128)(2,1)S(1)} collective-permute-done((s16[128,256]{1,0:T(8,128)(2,1)S(1)}, s16[128,256]{1,0:T(8,128)(2,1)S(1)}, u32[]{:S(2)}, u32[]{:S(2)}) %collective-permute-start.21) | collective-permute-done | bytes 65568 | tf_op jit(solution)/shard_map/ppermute | solution.py:322
  50.8 1.1 %collective-permute-done.20.refs_2_ = s16[128,256]{1,0:T(8,128)(2,1)S(1)} collective-permute-done((s16[128,256]{1,0:T(8,128)(2,1)S(1)}, s16[128,256]{1,0:T(8,128)(2,1)S(1)}, u32[]{:S(2)}, u32[]{:S(2)}) %collective-permute-start.20) | collective-permute-done | bytes 65568 | tf_op jit(solution)/shard_map/ppermute | solution.py:322
  53.6 2.6 %collective-permute-start.24 = (f32[8,128]{1,0:T(8,128)S(1)}, f32[8,128]{1,0:T(8,128)S(1)}, u32[]{:S(2)}, u32[]{:S(2)}) collective-permute-start(f32[8,128]{1,0:T(8,128)S(1)} %get-tuple-element.73.refs_0_), channel_id=1, source_target_pairs={{0,3},{1,2},{2,1},{3,0},{4,7},{5,6},{6,5},{7,4},{8,11},{9,10},{10,... | collective-permute-start | bytes 12296 | tf_op jit(solution)/shard_map/ppermute | solution.py:322
  56.2 1.8 %collective-permute-start.22 = (f32[8,128]{1,0:T(8,128)S(1)}, f32[8,128]{1,0:T(8,128)S(1)}, u32[]{:S(2)}, u32[]{:S(2)}) collective-permute-start(f32[8,128]{1,0:T(8,128)S(1)} %get-tuple-element.73.refs_0_), channel_id=1, source_target_pairs={{0,2},{1,3},{2,0},{3,1},{4,6},{5,7},{6,4},{7,5},{8,10},{9,11},{10,... | collective-permute-start | bytes 12296 | tf_op jit(solution)/shard_map/ppermute | solution.py:322
  58.0 1.0 %collective-permute-done.24.refs_3_ = f32[8,128]{1,0:T(8,128)S(1)} collective-permute-done((f32[8,128]{1,0:T(8,128)S(1)}, f32[8,128]{1,0:T(8,128)S(1)}, u32[]{:S(2)}, u32[]{:S(2)}) %collective-permute-start.24) | collective-permute-done | bytes 4128 | tf_op jit(solution)/shard_map/ppermute | solution.py:322
  (53 shorter events, 17.3 us)
Async XLA Ops:
  0.0 10.6 %collective-permute-start.1 = (bf16[4,256,256]{2,1,0:T(8,128)(2,1)}, bf16[4,256,256]{2,1,0:T(8,128)(2,1)S(1)}, u32[]{:S(2)}, u32[]{:S(2)}) collective-permute-start(bf16[4,256,256]{2,1,0:T(8,128)(2,1)} %refs_4_.4), channel_id=1, source_target_pairs={{0,4},{4,0},{8,12},{12,8},{16,20},{20,16},{24,28},{28,24},{1,5},{5... | collective-permute-start | bytes 1572872 | tf_op jit(solution)/shard_map/ppermute | solution.py:322
  0.5 11.1 %collective-permute-start = (bf16[4,256,256]{2,1,0:T(8,128)(2,1)}, bf16[4,256,256]{2,1,0:T(8,128)(2,1)S(1)}, u32[]{:S(2)}, u32[]{:S(2)}) collective-permute-start(bf16[4,256,256]{2,1,0:T(8,128)(2,1)} %refs_4_.4), channel_id=1, source_target_pairs={{0,8},{4,20},{8,0},{12,28},{16,24},{20,4},{24,16},{28,12},{1,9},{5... | collective-permute-start | bytes 1572872 | tf_op jit(solution)/shard_map/ppermute | solution.py:322
  6.8 9.2 %collective-permute-start.8 = (bf16[4,256,256]{2,1,0:T(8,128)(2,1)S(1)}, bf16[4,256,256]{2,1,0:T(8,128)(2,1)S(1)}, u32[]{:S(2)}, u32[]{:S(2)}) collective-permute-start(bf16[4,256,256]{2,1,0:T(8,128)(2,1)S(1)} %copy-done.1), channel_id=1, source_target_pairs={{0,16},{4,12},{8,24},{12,4},{16,0},{20,28},{24,8},{28,20},{1,17},{... | collective-permute-start | bytes 1572872 | tf_op jit(solution)/shard_map/ppermute | solution.py:322
  8.4 3.1 %collective-permute-start.3 = (f32[2,128,256]{2,1,0:T(8,128)S(1)}, f32[2,128,256]{2,1,0:T(8,128)S(1)}, u32[]{:S(2)}, u32[]{:S(2)}) collective-permute-start(f32[2,128,256]{2,1,0:T(8,128)S(1)} %get-tuple-element.47.refs_10_), channel_id=1, source_target_pairs={{0,4},{4,0},{8,12},{12,8},{16,20},{20,16},{24,28},{28,24},{1,5},{5... | collective-permute-start | bytes 786440 | tf_op jit(solution)/shard_map/ppermute | solution.py:322
  8.4 1.5 %collective-permute-start.2 = (s32[7]{0:T(128)S(1)}, s32[7]{0:T(128)S(1)}, u32[]{:S(2)}, u32[]{:S(2)}) collective-permute-start(s32[7]{0:T(128)S(1)} %pad_add_fusion.info_ref), channel_id=1, source_target_pairs={{0,4},{4,0},{8,12},{12,8},{16,20},{20,16},{24,28},{28,24},{1,5},{5... | collective-permute-start | bytes 92 | tf_op jit(solution)/shard_map/ppermute | solution.py:322
  9.9 1.6 %collective-permute-start.4 = (bf16[128,256]{1,0:T(8,128)(2,1)S(1)}, bf16[128,256]{1,0:T(8,128)(2,1)S(1)}, u32[]{:S(2)}, u32[]{:S(2)}) collective-permute-start(bf16[128,256]{1,0:T(8,128)(2,1)S(1)} %copy-done), channel_id=1, source_target_pairs={{0,4},{4,0},{8,12},{12,8},{16,20},{20,16},{24,28},{28,24},{1,5},{5... | collective-permute-start | bytes 196616 | tf_op jit(solution)/shard_map/ppermute | solution.py:322
  11.6 10.2 %collective-permute-start.5 = (bf16[4,256,256]{2,1,0:T(8,128)(2,1)S(1)}, bf16[4,256,256]{2,1,0:T(8,128)(2,1)S(1)}, u32[]{:S(2)}, u32[]{:S(2)}) collective-permute-start(bf16[4,256,256]{2,1,0:T(8,128)(2,1)S(1)} %collective-permute-done.refs_4_), channel_id=1, source_target_pairs={{0,16},{4,12},{8,24},{12,4},{16,0},{20,28},{24,8},{28,20},{1,17},{... | collective-permute-start | bytes 1572872 | tf_op jit(solution)/shard_map/ppermute | solution.py:322
  16.1 1.5 %collective-permute-start.7 = (bf16[4,128,256]{2,1,0:T(8,128)(2,1)S(1)}, bf16[4,128,256]{2,1,0:T(8,128)(2,1)S(1)}, u32[]{:S(2)}, u32[]{:S(2)}) collective-permute-start(bf16[4,128,256]{2,1,0:T(8,128)(2,1)S(1)} %get-tuple-element.79), channel_id=1, source_target_pairs={{0,4},{4,0},{8,12},{12,8},{16,20},{20,16},{24,28},{28,24},{1,5},{5... | collective-permute-start | bytes 786440 | tf_op jit(solution)/shard_map/ppermute | solution.py:322
  16.1 1.9 %collective-permute-start.6 = (bf16[4,128,256]{2,1,0:T(8,128)(2,1)S(1)}, bf16[4,128,256]{2,1,0:T(8,128)(2,1)S(1)}, u32[]{:S(2)}, u32[]{:S(2)}) collective-permute-start(bf16[4,128,256]{2,1,0:T(8,128)(2,1)S(1)} %get-tuple-element.80), channel_id=1, source_target_pairs={{0,4},{4,0},{8,12},{12,8},{16,20},{20,16},{24,28},{28,24},{1,5},{5... | collective-permute-start | bytes 786440 | tf_op jit(solution)/shard_map/ppermute | solution.py:322
  16.6 1.7 %collective-permute-start.10 = (bf16[4,128,256]{2,1,0:T(8,128)(2,1)S(1)}, bf16[4,128,256]{2,1,0:T(8,128)(2,1)S(1)}, u32[]{:S(2)}, u32[]{:S(2)}) collective-permute-start(bf16[4,128,256]{2,1,0:T(8,128)(2,1)S(1)} %get-tuple-element.77), channel_id=1, source_target_pairs={{0,4},{4,0},{8,12},{12,8},{16,20},{20,16},{24,28},{28,24},{1,5},{5... | collective-permute-start | bytes 786440 | tf_op jit(solution)/shard_map/ppermute | solution.py:322
  16.7 2.0 %collective-permute-start.9 = (bf16[4,128,256]{2,1,0:T(8,128)(2,1)S(1)}, bf16[4,128,256]{2,1,0:T(8,128)(2,1)S(1)}, u32[]{:S(2)}, u32[]{:S(2)}) collective-permute-start(bf16[4,128,256]{2,1,0:T(8,128)(2,1)S(1)} %get-tuple-element.78), channel_id=1, source_target_pairs={{0,4},{4,0},{8,12},{12,8},{16,20},{20,16},{24,28},{28,24},{1,5},{5... | collective-permute-start | bytes 786440 | tf_op jit(solution)/shard_map/ppermute | solution.py:322
  24.0 4.6 %collective-permute-start.15 = (bf16[4,256,256]{2,1,0:T(8,128)(2,1)S(1)}, bf16[4,256,256]{2,1,0:T(8,128)(2,1)S(1)}, u32[]{:S(2)}, u32[]{:S(2)}) collective-permute-start(bf16[4,256,256]{2,1,0:T(8,128)(2,1)S(1)} %collective-permute-done.5.refs_4_.refs_0_), channel_id=1, source_target_pairs={{0,4},{4,0},{8,12},{12,8},{16,20},{20,16},{24,28},{28,24},{1,5},{5... | collective-permute-start | bytes 1572872 | tf_op jit(solution)/shard_map/ppermute | solution.py:322
  24.2 6.7 %collective-permute-start.14 = (s16[128,256]{1,0:T(8,128)(2,1)S(1)}, s16[128,256]{1,0:T(8,128)(2,1)S(1)}, u32[]{:S(2)}, u32[]{:S(2)}) collective-permute-start(s16[128,256]{1,0:T(8,128)(2,1)S(1)} %join.1.refs_0_), channel_id=1, source_target_pairs={{0,3},{1,2},{2,1},{3,0},{4,7},{5,6},{6,5},{7,4},{8,11},{9,10},{10,... | collective-permute-start | bytes 196616 | tf_op jit(solution)/shard_map/ppermute | solution.py:322
  27.8 5.3 %collective-permute-start.13 = (s16[128,256]{1,0:T(8,128)(2,1)S(1)}, s16[128,256]{1,0:T(8,128)(2,1)S(1)}, u32[]{:S(2)}, u32[]{:S(2)}) collective-permute-start(s16[128,256]{1,0:T(8,128)(2,1)S(1)} %join.1.refs_0_), channel_id=1, source_target_pairs={{0,1},{1,0},{2,3},{3,2},{4,5},{5,4},{6,7},{7,6},{8,9},{9,8},{10,11... | collective-permute-start | bytes 196616 | tf_op jit(solution)/shard_map/ppermute | solution.py:322
  27.8 5.9 %collective-permute-start.12 = (s16[128,256]{1,0:T(8,128)(2,1)S(1)}, s16[128,256]{1,0:T(8,128)(2,1)S(1)}, u32[]{:S(2)}, u32[]{:S(2)}) collective-permute-start(s16[128,256]{1,0:T(8,128)(2,1)S(1)} %join.1.refs_0_), channel_id=1, source_target_pairs={{0,2},{1,3},{2,0},{3,1},{4,6},{5,7},{6,4},{7,5},{8,10},{9,11},{10,... | collective-permute-start | bytes 196616 | tf_op jit(solution)/shard_map/ppermute | solution.py:322
  34.8 6.3 %collective-permute-start.18 = (s16[128,256]{1,0:T(8,128)(2,1)S(1)}, s16[128,256]{1,0:T(8,128)(2,1)S(1)}, u32[]{:S(2)}, u32[]{:S(2)}) collective-permute-start(s16[128,256]{1,0:T(8,128)(2,1)S(1)} %get-tuple-element.67.refs_0_), channel_id=1, source_target_pairs={{0,3},{1,2},{2,1},{3,0},{4,7},{5,6},{6,5},{7,4},{8,11},{9,10},{10,... | collective-permute-start | bytes 196616 | tf_op jit(solution)/shard_map/ppermute | solution.py:322
  37.1 5.0 %collective-permute-start.17 = (s16[128,256]{1,0:T(8,128)(2,1)S(1)}, s16[128,256]{1,0:T(8,128)(2,1)S(1)}, u32[]{:S(2)}, u32[]{:S(2)}) collective-permute-start(s16[128,256]{1,0:T(8,128)(2,1)S(1)} %get-tuple-element.67.refs_0_), channel_id=1, source_target_pairs={{0,1},{1,0},{2,3},{3,2},{4,5},{5,4},{6,7},{7,6},{8,9},{9,8},{10,11... | collective-permute-start | bytes 196616 | tf_op jit(solution)/shard_map/ppermute | solution.py:322
  37.6 5.4 %collective-permute-start.16 = (s16[128,256]{1,0:T(8,128)(2,1)S(1)}, s16[128,256]{1,0:T(8,128)(2,1)S(1)}, u32[]{:S(2)}, u32[]{:S(2)}) collective-permute-start(s16[128,256]{1,0:T(8,128)(2,1)S(1)} %get-tuple-element.67.refs_0_), channel_id=1, source_target_pairs={{0,2},{1,3},{2,0},{3,1},{4,6},{5,7},{6,4},{7,5},{8,10},{9,11},{10,... | collective-permute-start | bytes 196616 | tf_op jit(solution)/shard_map/ppermute | solution.py:322
  44.3 6.5 %collective-permute-start.21 = (s16[128,256]{1,0:T(8,128)(2,1)S(1)}, s16[128,256]{1,0:T(8,128)(2,1)S(1)}, u32[]{:S(2)}, u32[]{:S(2)}) collective-permute-start(s16[128,256]{1,0:T(8,128)(2,1)S(1)} %get-tuple-element.69.refs_0_), channel_id=1, source_target_pairs={{0,3},{1,2},{2,1},{3,0},{4,7},{5,6},{6,5},{7,4},{8,11},{9,10},{10,... | collective-permute-start | bytes 196616 | tf_op jit(solution)/shard_map/ppermute | solution.py:322
  47.5 4.5 %collective-permute-start.20 = (s16[128,256]{1,0:T(8,128)(2,1)S(1)}, s16[128,256]{1,0:T(8,128)(2,1)S(1)}, u32[]{:S(2)}, u32[]{:S(2)}) collective-permute-start(s16[128,256]{1,0:T(8,128)(2,1)S(1)} %get-tuple-element.69.refs_0_), channel_id=1, source_target_pairs={{0,1},{1,0},{2,3},{3,2},{4,5},{5,4},{6,7},{7,6},{8,9},{9,8},{10,11... | collective-permute-start | bytes 196616 | tf_op jit(solution)/shard_map/ppermute | solution.py:322
  47.5 5.2 %collective-permute-start.19 = (s16[128,256]{1,0:T(8,128)(2,1)S(1)}, s16[128,256]{1,0:T(8,128)(2,1)S(1)}, u32[]{:S(2)}, u32[]{:S(2)}) collective-permute-start(s16[128,256]{1,0:T(8,128)(2,1)S(1)} %get-tuple-element.69.refs_0_), channel_id=1, source_target_pairs={{0,2},{1,3},{2,0},{3,1},{4,6},{5,7},{6,4},{7,5},{8,10},{9,11},{10,... | collective-permute-start | bytes 196616 | tf_op jit(solution)/shard_map/ppermute | solution.py:322
  53.6 5.4 %collective-permute-start.24 = (f32[8,128]{1,0:T(8,128)S(1)}, f32[8,128]{1,0:T(8,128)S(1)}, u32[]{:S(2)}, u32[]{:S(2)}) collective-permute-start(f32[8,128]{1,0:T(8,128)S(1)} %get-tuple-element.73.refs_0_), channel_id=1, source_target_pairs={{0,3},{1,2},{2,1},{3,0},{4,7},{5,6},{6,5},{7,4},{8,11},{9,10},{10,... | collective-permute-start | bytes 12296 | tf_op jit(solution)/shard_map/ppermute | solution.py:322
  56.2 3.6 %collective-permute-start.23 = (f32[8,128]{1,0:T(8,128)S(1)}, f32[8,128]{1,0:T(8,128)S(1)}, u32[]{:S(2)}, u32[]{:S(2)}) collective-permute-start(f32[8,128]{1,0:T(8,128)S(1)} %get-tuple-element.73.refs_0_), channel_id=1, source_target_pairs={{0,1},{1,0},{2,3},{3,2},{4,5},{5,4},{6,7},{7,6},{8,9},{9,8},{10,11... | collective-permute-start | bytes 12296 | tf_op jit(solution)/shard_map/ppermute | solution.py:322
  56.2 4.5 %collective-permute-start.22 = (f32[8,128]{1,0:T(8,128)S(1)}, f32[8,128]{1,0:T(8,128)S(1)}, u32[]{:S(2)}, u32[]{:S(2)}) collective-permute-start(f32[8,128]{1,0:T(8,128)S(1)} %get-tuple-element.73.refs_0_), channel_id=1, source_target_pairs={{0,2},{1,3},{2,0},{3,1},{4,6},{5,7},{6,4},{7,5},{8,10},{9,11},{10,... | collective-permute-start | bytes 12296 | tf_op jit(solution)/shard_map/ppermute | solution.py:322
  (6 other events, 9.3 us)

commit v6 on v5

--- a/solution.py
+++ b/solution.py
@@ -468,8 +468,17 @@
 
     order = [0, *range(2, n_col, 2), *range(1, n_col, 2)]
 
+    def partner(place, bits):
+        row, col = place // n_col, place % n_col
+        if row & 1 and n_col > 2:
+            bits = (bits & ~3) | (0, 2, 1, 3)[bits & 3]
+        return row * n_col + (col ^ bits)
+
+    def sent(own, bits):
+        return lax.ppermute(own, ("row", "col"), [(i, partner(i, bits)) for i in range(n_row * n_col)])
+
     def to_all(own):
-        return [own] + [permuted(own, "col", n_col, lambda i: i ^ bits) for bits in order[1:]]
+        return [own] + [sent(own, bits) for bits in order[1:]]
 
     state = []
     for index in range(ITERS):

time: 61.7 us -> 61.5 us (level)
    ppermute x25 -> x13, starting transfers between devices: 27.4 us -> 9.62 us  [permuted(): return lax.ppermute(array, axis, [(i, target(i)) for i in range(size)])]
    ppermute x0 -> x12, starting transfers between devices: none -> 17.7 us  [sent(): lax.ppermute(own, ('row', 'col'), [(i, partner(i, bits)) for i in range(n...]
    ppermute x25 -> x13, waiting for transfers between devices: 20.7 us -> 5.83 us  [permuted(): return lax.ppermute(array, axis, [(i, target(i)) for i in range(size)])]
    ppermute x0 -> x12, waiting for transfers between devices: none -> 14.7 us  [sent(): lax.ppermute(own, ('row', 'col'), [(i, partner(i, bits)) for i in range(n...]
  transfers between devices with their start and end apart: 25 -> 25, of which waited for: 20 -> 17; matrix products, arithmetic and copies ran while one was open for 2% -> 2% of each run, Pallas kernels for 9% -> 9%
where the time goes in v6:
time: 61.5 us; the launch traced here: 61.3 us
  starting transfers between devices  27.4 us (45%)
  waiting for transfers between devices  20.5 us (33%)
  Pallas kernels  10.7 us (17%)
  local copies, waits for them, and re-layouts  1.52 us (2%)
  other arithmetic  1.04 us (2%)
    ppermute x12, starting transfers between devices, sent(): lax.ppermute(own, ('row', 'col'), [(i, partner(i, bits)) for i in range(n...  17.7 us
    ppermute x12, waiting for transfers between devices, sent(): lax.ppermute(own, ('row', 'col'), [(i, partner(i, bits)) for i in range(n...  14.7 us
    pallas_call x11, Pallas kernels, call(): pl.pallas_call(body, out_shape=[pltpu.VMEM(o.shape, o.dtype) for o in out...  9.9 us
    ppermute x13, starting transfers between devices, permuted(): return lax.ppermute(array, axis, [(i, target(i)) for i in range(size)])  9.62 us
    ppermute x13, waiting for transfers between devices, permuted(): return lax.ppermute(array, axis, [(i, target(i)) for i in range(size)])  5.83 us
    unnamed x10, local copies, waits for them, and re-layouts  1.34 us
  transfers between devices with their start and end apart: 25, of which 17 were waited for; matrix products, arithmetic and copies ran while one was open for 2% of the time, Pallas kernels for 9%

profile of v6, /device:TPU:0, one launch (start us, length us, event | category | flops | bytes accessed | tf_op | source)
XLA Modules:
  0.0 61.3 jit_solution(17365078037592534777)
XLA Ops:
  0.5 2.5 %collective-permute-start = (bf16[4,256,256]{2,1,0:T(8,128)(2,1)}, bf16[4,256,256]{2,1,0:T(8,128)(2,1)S(1)}, u32[]{:S(2)}, u32[]{:S(2)}) collective-permute-start(bf16[4,256,256]{2,1,0:T(8,128)(2,1)} %refs_4_.4), channel_id=1, source_target_pairs={{0,8},{4,20},{8,0},{12,28},{16,24},{20,4},{24,16},{28,12},{1,9},{5... | collective-permute-start | bytes 1572872 | tf_op jit(solution)/shard_map/ppermute | solution.py:322
  5.5 1.3 %masks.1 = (f32[2,128,512]{2,1,0:T(8,128)S(1)}, f32[2,128,1024]{2,1,0:T(8,128)S(1)}, f32[2,128,256]{2,1,0:T(8,128)S(1)}, f32[2,128,256]{2,1,0:T(8,128)S(1)}, s32[7]{0:T(128)S(4)}) custom-call(s32[7]{0:T(128)S(1)} %pad_add_fusion.info_ref, bf16[2,128,256]{2,1,0:T(8,128)(2,1)S(1)} %fusion.words_ref, f32[128,1]{1,0:T(8,128)S(1)} %copy.8.conf_ref.refs_2_), custom_call_target="tpu_custom_call" | custom-call | flops 268435456 | bytes 1048576 | tf_op jit(solution)/shard_map/masks/pallas_call | solution.py:22
  6.8 1.6 %collective-permute-start.8 = (bf16[4,256,256]{2,1,0:T(8,128)(2,1)S(1)}, bf16[4,256,256]{2,1,0:T(8,128)(2,1)S(1)}, u32[]{:S(2)}, u32[]{:S(2)}) collective-permute-start(bf16[4,256,256]{2,1,0:T(8,128)(2,1)S(1)} %copy-done.1), channel_id=1, source_target_pairs={{0,16},{4,12},{8,24},{12,4},{16,0},{20,28},{24,8},{28,20},{1,17},{... | collective-permute-start | bytes 1572872 | tf_op jit(solution)/shard_map/ppermute | solution.py:322
  8.9 1.0 %collective-permute-done.2.in_ref = s32[7]{0:T(128)S(1)} collective-permute-done((s32[7]{0:T(128)S(1)}, s32[7]{0:T(128)S(1)}, u32[]{:S(2)}, u32[]{:S(2)}) %collective-permute-start.2) | collective-permute-done | bytes 60 | tf_op jit(solution)/shard_map/ppermute | solution.py:322
  11.6 3.1 %collective-permute-start.5 = (bf16[4,256,256]{2,1,0:T(8,128)(2,1)S(1)}, bf16[4,256,256]{2,1,0:T(8,128)(2,1)S(1)}, u32[]{:S(2)}, u32[]{:S(2)}) collective-permute-start(bf16[4,256,256]{2,1,0:T(8,128)(2,1)S(1)} %collective-permute-done.refs_4_), channel_id=1, source_target_pairs={{0,16},{4,12},{8,24},{12,4},{16,0},{20,28},{24,8},{28,20},{1,17},{... | collective-permute-start | bytes 1572872 | tf_op jit(solution)/shard_map/ppermute | solution.py:322
  14.7 1.4 %collective-permute-done.8.refs_7_ = bf16[4,256,256]{2,1,0:T(8,128)(2,1)S(1)} collective-permute-done((bf16[4,256,256]{2,1,0:T(8,128)(2,1)S(1)}, bf16[4,256,256]{2,1,0:T(8,128)(2,1)S(1)}, u32[]{:S(2)}, u32[]{:S(2)}) %collective-permute-start.8) | collective-permute-done | bytes 524320 | tf_op jit(solution)/shard_map/ppermute | solution.py:322
  18.7 1.9 %stage.4 = (bf16[2,1024,256]{2,1,0:T(8,128)(2,1)S(1)}, bf16[2,256,1024]{2,1,0:T(8,128)(2,1)S(1)}, f32[256,256]{1,0:T(8,128)S(1)}, f32[2,128,256]{2,1,0:T(8,128)S(1)}) custom-call(s32[7]{0:T(128)S(4)} %get-tuple-element.41.refs_0_.info_ref, f32[2,128,1024]{2,1,0:T(8,128)S(1)} %get-tuple-element.46.refs_1_.refs_8_, f32[128,1]{1,0:T(8,128)S(1)} %copy.8.conf_ref.refs_2_, ...), custom_call_target="tpu_custom_call" | custom-call | flops 939524096 | bytes 1048576 | tf_op jit(solution)/shard_map/stage/pallas_call | solution.py:22
  20.6 1.2 %collective-permute-done.5.refs_4_.refs_0_ = bf16[4,256,256]{2,1,0:T(8,128)(2,1)S(1)} collective-permute-done((bf16[4,256,256]{2,1,0:T(8,128)(2,1)S(1)}, bf16[4,256,256]{2,1,0:T(8,128)(2,1)S(1)}, u32[]{:S(2)}, u32[]{:S(2)}) %collective-permute-start.5) | collective-permute-done | bytes 524320 | tf_op jit(solution)/shard_map/ppermute | solution.py:322
  24.2 3.6 %collective-permute-start.14 = (s16[128,256]{1,0:T(8,128)(2,1)S(1)}, s16[128,256]{1,0:T(8,128)(2,1)S(1)}, u32[]{:S(2)}, u32[]{:S(2)}) collective-permute-start(s16[128,256]{1,0:T(8,128)(2,1)S(1)} %join.1.refs_0_), channel_id=1, source_target_pairs={{0,3},{1,2},{2,1},{3,0},{4,7},{5,6},{6,5},{7,4},{8,11},{9,10},{10,... | collective-permute-start | bytes 196616 | tf_op jit(solution)/shard_map/ppermute | solution.py:478
  29.0 1.7 %collective-permute-done.14.refs_3_ = s16[128,256]{1,0:T(8,128)(2,1)S(1)} collective-permute-done((s16[128,256]{1,0:T(8,128)(2,1)S(1)}, s16[128,256]{1,0:T(8,128)(2,1)S(1)}, u32[]{:S(2)}, u32[]{:S(2)}) %collective-permute-start.14) | collective-permute-done | bytes 65568 | tf_op jit(solution)/shard_map/ppermute | solution.py:478
  30.7 2.8 %collective-permute-done.13.refs_2_ = s16[128,256]{1,0:T(8,128)(2,1)S(1)} collective-permute-done((s16[128,256]{1,0:T(8,128)(2,1)S(1)}, s16[128,256]{1,0:T(8,128)(2,1)S(1)}, u32[]{:S(2)}, u32[]{:S(2)}) %collective-permute-start.13) | collective-permute-done | bytes 65568 | tf_op jit(solution)/shard_map/ppermute | solution.py:478
  33.5 1.2 %round0.1 = (f32[128,256]{1,0:T(8,128)S(1)}, s16[128,256]{1,0:T(8,128)(2,1)S(1)}) custom-call(s16[128,256]{1,0:T(8,128)(2,1)S(1)} %join.1.refs_0_, s16[128,256]{1,0:T(8,128)(2,1)S(1)} %collective-permute-done.12.refs_1_, s16[128,256]{1,0:T(8,128)(2,1)S(1)} %collective-permute-done.13.refs_2_, s16[128,256]{1,0:T(8,128)(2,1)S(1)} %collective-permute-done.14.refs_3_, ...), custom_call_target="tpu_custom_call" | custom-call | flops 536870912 | bytes 1048576 | tf_op jit(solution)/shard_map/round0/pallas_call | solution.py:22
  34.6 2.1 %collective-permute-start.18 = (s16[128,256]{1,0:T(8,128)(2,1)S(1)}, s16[128,256]{1,0:T(8,128)(2,1)S(1)}, u32[]{:S(2)}, u32[]{:S(2)}) collective-permute-start(s16[128,256]{1,0:T(8,128)(2,1)S(1)} %get-tuple-element.67.refs_0_), channel_id=1, source_target_pairs={{0,3},{1,2},{2,1},{3,0},{4,7},{5,6},{6,5},{7,4},{8,11},{9,10},{10,... | collective-permute-start | bytes 196616 | tf_op jit(solution)/shard_map/ppermute | solution.py:478
  37.6 1.5 %collective-permute-start.16 = (s16[128,256]{1,0:T(8,128)(2,1)S(1)}, s16[128,256]{1,0:T(8,128)(2,1)S(1)}, u32[]{:S(2)}, u32[]{:S(2)}) collective-permute-start(s16[128,256]{1,0:T(8,128)(2,1)S(1)} %get-tuple-element.67.refs_0_), channel_id=1, source_target_pairs={{0,2},{1,3},{2,0},{3,1},{4,5},{5,4},{6,7},{7,6},{8,10},{9,11},{10,... | collective-permute-start | bytes 196616 | tf_op jit(solution)/shard_map/ppermute | solution.py:478
  39.1 1.8 %collective-permute-done.18.refs_3_ = s16[128,256]{1,0:T(8,128)(2,1)S(1)} collective-permute-done((s16[128,256]{1,0:T(8,128)(2,1)S(1)}, s16[128,256]{1,0:T(8,128)(2,1)S(1)}, u32[]{:S(2)}, u32[]{:S(2)}) %collective-permute-start.18) | collective-permute-done | bytes 65568 | tf_op jit(solution)/shard_map/ppermute | solution.py:478
  40.9 2.0 %collective-permute-done.17.refs_2_ = s16[128,256]{1,0:T(8,128)(2,1)S(1)} collective-permute-done((s16[128,256]{1,0:T(8,128)(2,1)S(1)}, s16[128,256]{1,0:T(8,128)(2,1)S(1)}, u32[]{:S(2)}, u32[]{:S(2)}) %collective-permute-start.17) | collective-permute-done | bytes 65568 | tf_op jit(solution)/shard_map/ppermute | solution.py:478
  43.0 1.3 %round1.1 = (f32[128,256]{1,0:T(8,128)S(1)}, f32[128,256]{1,0:T(8,128)S(1)}, f32[128,256]{1,0:T(8,128)S(1)}, s16[128,256]{1,0:T(8,128)(2,1)S(1)}) custom-call(s16[128,256]{1,0:T(8,128)(2,1)S(1)} %get-tuple-element.67.refs_0_, s16[128,256]{1,0:T(8,128)(2,1)S(1)} %collective-permute-done.16.refs_1_, s16[128,256]{1,0:T(8,128)(2,1)S(1)} %collective-permute-done.17.refs_2_, ...), custom_call_target="tpu_custom_call" | custom-call | flops 536870912 | bytes 1048576 | tf_op jit(solution)/shard_map/round1/pallas_call | solution.py:22
  44.3 2.1 %collective-permute-start.21 = (s16[128,256]{1,0:T(8,128)(2,1)S(1)}, s16[128,256]{1,0:T(8,128)(2,1)S(1)}, u32[]{:S(2)}, u32[]{:S(2)}) collective-permute-start(s16[128,256]{1,0:T(8,128)(2,1)S(1)} %get-tuple-element.69.refs_0_), channel_id=1, source_target_pairs={{0,3},{1,2},{2,1},{3,0},{4,7},{5,6},{6,5},{7,4},{8,11},{9,10},{10,... | collective-permute-start | bytes 196616 | tf_op jit(solution)/shard_map/ppermute | solution.py:478
  46.7 2.0 %collective-permute-start.19 = (s16[128,256]{1,0:T(8,128)(2,1)S(1)}, s16[128,256]{1,0:T(8,128)(2,1)S(1)}, u32[]{:S(2)}, u32[]{:S(2)}) collective-permute-start(s16[128,256]{1,0:T(8,128)(2,1)S(1)} %get-tuple-element.69.refs_0_), channel_id=1, source_target_pairs={{0,2},{1,3},{2,0},{3,1},{4,5},{5,4},{6,7},{7,6},{8,10},{9,11},{10,... | collective-permute-start | bytes 196616 | tf_op jit(solution)/shard_map/ppermute | solution.py:478
  48.7 2.1 %collective-permute-done.21.refs_3_ = s16[128,256]{1,0:T(8,128)(2,1)S(1)} collective-permute-done((s16[128,256]{1,0:T(8,128)(2,1)S(1)}, s16[128,256]{1,0:T(8,128)(2,1)S(1)}, u32[]{:S(2)}, u32[]{:S(2)}) %collective-permute-start.21) | collective-permute-done | bytes 65568 | tf_op jit(solution)/shard_map/ppermute | solution.py:478
  50.8 1.4 %collective-permute-done.20.refs_2_ = s16[128,256]{1,0:T(8,128)(2,1)S(1)} collective-permute-done((s16[128,256]{1,0:T(8,128)(2,1)S(1)}, s16[128,256]{1,0:T(8,128)(2,1)S(1)}, u32[]{:S(2)}, u32[]{:S(2)}) %collective-permute-start.20) | collective-permute-done | bytes 65568 | tf_op jit(solution)/shard_map/ppermute | solution.py:478
  53.2 2.8 %collective-permute-start.24 = (f32[8,128]{1,0:T(8,128)S(1)}, f32[8,128]{1,0:T(8,128)S(1)}, u32[]{:S(2)}, u32[]{:S(2)}) collective-permute-start(f32[8,128]{1,0:T(8,128)S(1)} %get-tuple-element.73.refs_0_), channel_id=1, source_target_pairs={{0,3},{1,2},{2,1},{3,0},{4,7},{5,6},{6,5},{7,4},{8,11},{9,10},{10,... | collective-permute-start | bytes 12296 | tf_op jit(solution)/shard_map/ppermute | solution.py:478
  56.0 1.6 %collective-permute-start.22 = (f32[8,128]{1,0:T(8,128)S(1)}, f32[8,128]{1,0:T(8,128)S(1)}, u32[]{:S(2)}, u32[]{:S(2)}) collective-permute-start(f32[8,128]{1,0:T(8,128)S(1)} %get-tuple-element.73.refs_0_), channel_id=1, source_target_pairs={{0,2},{1,3},{2,0},{3,1},{4,5},{5,4},{6,7},{7,6},{8,10},{9,11},{10,... | collective-permute-start | bytes 12296 | tf_op jit(solution)/shard_map/ppermute | solution.py:478
  57.6 1.0 %collective-permute-done.24.refs_3_ = f32[8,128]{1,0:T(8,128)S(1)} collective-permute-done((f32[8,128]{1,0:T(8,128)S(1)}, f32[8,128]{1,0:T(8,128)S(1)}, u32[]{:S(2)}, u32[]{:S(2)}) %collective-permute-start.24) | collective-permute-done | bytes 4128 | tf_op jit(solution)/shard_map/ppermute | solution.py:478
  (53 shorter events, 16.2 us)
Async XLA Ops:
  0.0 10.6 %collective-permute-start.1 = (bf16[4,256,256]{2,1,0:T(8,128)(2,1)}, bf16[4,256,256]{2,1,0:T(8,128)(2,1)S(1)}, u32[]{:S(2)}, u32[]{:S(2)}) collective-permute-start(bf16[4,256,256]{2,1,0:T(8,128)(2,1)} %refs_4_.4), channel_id=1, source_target_pairs={{0,4},{4,0},{8,12},{12,8},{16,20},{20,16},{24,28},{28,24},{1,5},{5... | collective-permute-start | bytes 1572872 | tf_op jit(solution)/shard_map/ppermute | solution.py:322
  0.5 11.1 %collective-permute-start = (bf16[4,256,256]{2,1,0:T(8,128)(2,1)}, bf16[4,256,256]{2,1,0:T(8,128)(2,1)S(1)}, u32[]{:S(2)}, u32[]{:S(2)}) collective-permute-start(bf16[4,256,256]{2,1,0:T(8,128)(2,1)} %refs_4_.4), channel_id=1, source_target_pairs={{0,8},{4,20},{8,0},{12,28},{16,24},{20,4},{24,16},{28,12},{1,9},{5... | collective-permute-start | bytes 1572872 | tf_op jit(solution)/shard_map/ppermute | solution.py:322
  6.8 9.2 %collective-permute-start.8 = (bf16[4,256,256]{2,1,0:T(8,128)(2,1)S(1)}, bf16[4,256,256]{2,1,0:T(8,128)(2,1)S(1)}, u32[]{:S(2)}, u32[]{:S(2)}) collective-permute-start(bf16[4,256,256]{2,1,0:T(8,128)(2,1)S(1)} %copy-done.1), channel_id=1, source_target_pairs={{0,16},{4,12},{8,24},{12,4},{16,0},{20,28},{24,8},{28,20},{1,17},{... | collective-permute-start | bytes 1572872 | tf_op jit(solution)/shard_map/ppermute | solution.py:322
  8.4 3.1 %collective-permute-start.3 = (f32[2,128,256]{2,1,0:T(8,128)S(1)}, f32[2,128,256]{2,1,0:T(8,128)S(1)}, u32[]{:S(2)}, u32[]{:S(2)}) collective-permute-start(f32[2,128,256]{2,1,0:T(8,128)S(1)} %get-tuple-element.47.refs_10_), channel_id=1, source_target_pairs={{0,4},{4,0},{8,12},{12,8},{16,20},{20,16},{24,28},{28,24},{1,5},{5... | collective-permute-start | bytes 786440 | tf_op jit(solution)/shard_map/ppermute | solution.py:322
  8.4 1.5 %collective-permute-start.2 = (s32[7]{0:T(128)S(1)}, s32[7]{0:T(128)S(1)}, u32[]{:S(2)}, u32[]{:S(2)}) collective-permute-start(s32[7]{0:T(128)S(1)} %pad_add_fusion.info_ref), channel_id=1, source_target_pairs={{0,4},{4,0},{8,12},{12,8},{16,20},{20,16},{24,28},{28,24},{1,5},{5... | collective-permute-start | bytes 92 | tf_op jit(solution)/shard_map/ppermute | solution.py:322
  9.9 1.6 %collective-permute-start.4 = (bf16[128,256]{1,0:T(8,128)(2,1)S(1)}, bf16[128,256]{1,0:T(8,128)(2,1)S(1)}, u32[]{:S(2)}, u32[]{:S(2)}) collective-permute-start(bf16[128,256]{1,0:T(8,128)(2,1)S(1)} %copy-done), channel_id=1, source_target_pairs={{0,4},{4,0},{8,12},{12,8},{16,20},{20,16},{24,28},{28,24},{1,5},{5... | collective-permute-start | bytes 196616 | tf_op jit(solution)/shard_map/ppermute | solution.py:322
  11.6 10.2 %collective-permute-start.5 = (bf16[4,256,256]{2,1,0:T(8,128)(2,1)S(1)}, bf16[4,256,256]{2,1,0:T(8,128)(2,1)S(1)}, u32[]{:S(2)}, u32[]{:S(2)}) collective-permute-start(bf16[4,256,256]{2,1,0:T(8,128)(2,1)S(1)} %collective-permute-done.refs_4_), channel_id=1, source_target_pairs={{0,16},{4,12},{8,24},{12,4},{16,0},{20,28},{24,8},{28,20},{1,17},{... | collective-permute-start | bytes 1572872 | tf_op jit(solution)/shard_map/ppermute | solution.py:322
  16.1 1.5 %collective-permute-start.7 = (bf16[4,128,256]{2,1,0:T(8,128)(2,1)S(1)}, bf16[4,128,256]{2,1,0:T(8,128)(2,1)S(1)}, u32[]{:S(2)}, u32[]{:S(2)}) collective-permute-start(bf16[4,128,256]{2,1,0:T(8,128)(2,1)S(1)} %get-tuple-element.79), channel_id=1, source_target_pairs={{0,4},{4,0},{8,12},{12,8},{16,20},{20,16},{24,28},{28,24},{1,5},{5... | collective-permute-start | bytes 786440 | tf_op jit(solution)/shard_map/ppermute | solution.py:322
  16.1 1.9 %collective-permute-start.6 = (bf16[4,128,256]{2,1,0:T(8,128)(2,1)S(1)}, bf16[4,128,256]{2,1,0:T(8,128)(2,1)S(1)}, u32[]{:S(2)}, u32[]{:S(2)}) collective-permute-start(bf16[4,128,256]{2,1,0:T(8,128)(2,1)S(1)} %get-tuple-element.80), channel_id=1, source_target_pairs={{0,4},{4,0},{8,12},{12,8},{16,20},{20,16},{24,28},{28,24},{1,5},{5... | collective-permute-start | bytes 786440 | tf_op jit(solution)/shard_map/ppermute | solution.py:322
  16.6 1.7 %collective-permute-start.10 = (bf16[4,128,256]{2,1,0:T(8,128)(2,1)S(1)}, bf16[4,128,256]{2,1,0:T(8,128)(2,1)S(1)}, u32[]{:S(2)}, u32[]{:S(2)}) collective-permute-start(bf16[4,128,256]{2,1,0:T(8,128)(2,1)S(1)} %get-tuple-element.77), channel_id=1, source_target_pairs={{0,4},{4,0},{8,12},{12,8},{16,20},{20,16},{24,28},{28,24},{1,5},{5... | collective-permute-start | bytes 786440 | tf_op jit(solution)/shard_map/ppermute | solution.py:322
  16.7 2.0 %collective-permute-start.9 = (bf16[4,128,256]{2,1,0:T(8,128)(2,1)S(1)}, bf16[4,128,256]{2,1,0:T(8,128)(2,1)S(1)}, u32[]{:S(2)}, u32[]{:S(2)}) collective-permute-start(bf16[4,128,256]{2,1,0:T(8,128)(2,1)S(1)} %get-tuple-element.78), channel_id=1, source_target_pairs={{0,4},{4,0},{8,12},{12,8},{16,20},{20,16},{24,28},{28,24},{1,5},{5... | collective-permute-start | bytes 786440 | tf_op jit(solution)/shard_map/ppermute | solution.py:322
  24.0 4.6 %collective-permute-start.15 = (bf16[4,256,256]{2,1,0:T(8,128)(2,1)S(1)}, bf16[4,256,256]{2,1,0:T(8,128)(2,1)S(1)}, u32[]{:S(2)}, u32[]{:S(2)}) collective-permute-start(bf16[4,256,256]{2,1,0:T(8,128)(2,1)S(1)} %collective-permute-done.5.refs_4_.refs_0_), channel_id=1, source_target_pairs={{0,4},{4,0},{8,12},{12,8},{16,20},{20,16},{24,28},{28,24},{1,5},{5... | collective-permute-start | bytes 1572872 | tf_op jit(solution)/shard_map/ppermute | solution.py:322
  24.2 6.5 %collective-permute-start.14 = (s16[128,256]{1,0:T(8,128)(2,1)S(1)}, s16[128,256]{1,0:T(8,128)(2,1)S(1)}, u32[]{:S(2)}, u32[]{:S(2)}) collective-permute-start(s16[128,256]{1,0:T(8,128)(2,1)S(1)} %join.1.refs_0_), channel_id=1, source_target_pairs={{0,3},{1,2},{2,1},{3,0},{4,7},{5,6},{6,5},{7,4},{8,11},{9,10},{10,... | collective-permute-start | bytes 196616 | tf_op jit(solution)/shard_map/ppermute | solution.py:478
  27.8 5.7 %collective-permute-start.13 = (s16[128,256]{1,0:T(8,128)(2,1)S(1)}, s16[128,256]{1,0:T(8,128)(2,1)S(1)}, u32[]{:S(2)}, u32[]{:S(2)}) collective-permute-start(s16[128,256]{1,0:T(8,128)(2,1)S(1)} %join.1.refs_0_), channel_id=1, source_target_pairs={{0,1},{1,0},{2,3},{3,2},{4,6},{5,7},{6,4},{7,5},{8,9},{9,8},{10,11... | collective-permute-start | bytes 196616 | tf_op jit(solution)/shard_map/ppermute | solution.py:478
  27.8 5.7 %collective-permute-start.12 = (s16[128,256]{1,0:T(8,128)(2,1)S(1)}, s16[128,256]{1,0:T(8,128)(2,1)S(1)}, u32[]{:S(2)}, u32[]{:S(2)}) collective-permute-start(s16[128,256]{1,0:T(8,128)(2,1)S(1)} %join.1.refs_0_), channel_id=1, source_target_pairs={{0,2},{1,3},{2,0},{3,1},{4,5},{5,4},{6,7},{7,6},{8,10},{9,11},{10,... | collective-permute-start | bytes 196616 | tf_op jit(solution)/shard_map/ppermute | solution.py:478
  34.6 6.3 %collective-permute-start.18 = (s16[128,256]{1,0:T(8,128)(2,1)S(1)}, s16[128,256]{1,0:T(8,128)(2,1)S(1)}, u32[]{:S(2)}, u32[]{:S(2)}) collective-permute-start(s16[128,256]{1,0:T(8,128)(2,1)S(1)} %get-tuple-element.67.refs_0_), channel_id=1, source_target_pairs={{0,3},{1,2},{2,1},{3,0},{4,7},{5,6},{6,5},{7,4},{8,11},{9,10},{10,... | collective-permute-start | bytes 196616 | tf_op jit(solution)/shard_map/ppermute | solution.py:478
  36.8 6.2 %collective-permute-start.17 = (s16[128,256]{1,0:T(8,128)(2,1)S(1)}, s16[128,256]{1,0:T(8,128)(2,1)S(1)}, u32[]{:S(2)}, u32[]{:S(2)}) collective-permute-start(s16[128,256]{1,0:T(8,128)(2,1)S(1)} %get-tuple-element.67.refs_0_), channel_id=1, source_target_pairs={{0,1},{1,0},{2,3},{3,2},{4,6},{5,7},{6,4},{7,5},{8,9},{9,8},{10,11... | collective-permute-start | bytes 196616 | tf_op jit(solution)/shard_map/ppermute | solution.py:478
  37.6 5.3 %collective-permute-start.16 = (s16[128,256]{1,0:T(8,128)(2,1)S(1)}, s16[128,256]{1,0:T(8,128)(2,1)S(1)}, u32[]{:S(2)}, u32[]{:S(2)}) collective-permute-start(s16[128,256]{1,0:T(8,128)(2,1)S(1)} %get-tuple-element.67.refs_0_), channel_id=1, source_target_pairs={{0,2},{1,3},{2,0},{3,1},{4,5},{5,4},{6,7},{7,6},{8,10},{9,11},{10,... | collective-permute-start | bytes 196616 | tf_op jit(solution)/shard_map/ppermute | solution.py:478
  44.3 6.5 %collective-permute-start.21 = (s16[128,256]{1,0:T(8,128)(2,1)S(1)}, s16[128,256]{1,0:T(8,128)(2,1)S(1)}, u32[]{:S(2)}, u32[]{:S(2)}) collective-permute-start(s16[128,256]{1,0:T(8,128)(2,1)S(1)} %get-tuple-element.69.refs_0_), channel_id=1, source_target_pairs={{0,3},{1,2},{2,1},{3,0},{4,7},{5,6},{6,5},{7,4},{8,11},{9,10},{10,... | collective-permute-start | bytes 196616 | tf_op jit(solution)/shard_map/ppermute | solution.py:478
  46.4 5.8 %collective-permute-start.20 = (s16[128,256]{1,0:T(8,128)(2,1)S(1)}, s16[128,256]{1,0:T(8,128)(2,1)S(1)}, u32[]{:S(2)}, u32[]{:S(2)}) collective-permute-start(s16[128,256]{1,0:T(8,128)(2,1)S(1)} %get-tuple-element.69.refs_0_), channel_id=1, source_target_pairs={{0,1},{1,0},{2,3},{3,2},{4,6},{5,7},{6,4},{7,5},{8,9},{9,8},{10,11... | collective-permute-start | bytes 196616 | tf_op jit(solution)/shard_map/ppermute | solution.py:478
  46.7 5.5 %collective-permute-start.19 = (s16[128,256]{1,0:T(8,128)(2,1)S(1)}, s16[128,256]{1,0:T(8,128)(2,1)S(1)}, u32[]{:S(2)}, u32[]{:S(2)}) collective-permute-start(s16[128,256]{1,0:T(8,128)(2,1)S(1)} %get-tuple-element.69.refs_0_), channel_id=1, source_target_pairs={{0,2},{1,3},{2,0},{3,1},{4,5},{5,4},{6,7},{7,6},{8,10},{9,11},{10,... | collective-permute-start | bytes 196616 | tf_op jit(solution)/shard_map/ppermute | solution.py:478
  53.2 5.4 %collective-permute-start.24 = (f32[8,128]{1,0:T(8,128)S(1)}, f32[8,128]{1,0:T(8,128)S(1)}, u32[]{:S(2)}, u32[]{:S(2)}) collective-permute-start(f32[8,128]{1,0:T(8,128)S(1)} %get-tuple-element.73.refs_0_), channel_id=1, source_target_pairs={{0,3},{1,2},{2,1},{3,0},{4,7},{5,6},{6,5},{7,4},{8,11},{9,10},{10,... | collective-permute-start | bytes 12296 | tf_op jit(solution)/shard_map/ppermute | solution.py:478
  56.0 3.6 %collective-permute-start.23 = (f32[8,128]{1,0:T(8,128)S(1)}, f32[8,128]{1,0:T(8,128)S(1)}, u32[]{:S(2)}, u32[]{:S(2)}) collective-permute-start(f32[8,128]{1,0:T(8,128)S(1)} %get-tuple-element.73.refs_0_), channel_id=1, source_target_pairs={{0,1},{1,0},{2,3},{3,2},{4,6},{5,7},{6,4},{7,5},{8,9},{9,8},{10,11... | collective-permute-start | bytes 12296 | tf_op jit(solution)/shard_map/ppermute | solution.py:478
  56.0 4.5 %collective-permute-start.22 = (f32[8,128]{1,0:T(8,128)S(1)}, f32[8,128]{1,0:T(8,128)S(1)}, u32[]{:S(2)}, u32[]{:S(2)}) collective-permute-start(f32[8,128]{1,0:T(8,128)S(1)} %get-tuple-element.73.refs_0_), channel_id=1, source_target_pairs={{0,2},{1,3},{2,0},{3,1},{4,5},{5,4},{6,7},{7,6},{8,10},{9,11},{10,... | collective-permute-start | bytes 12296 | tf_op jit(solution)/shard_map/ppermute | solution.py:478
  (6 other events, 9.3 us)

commit v7 on v6

--- a/solution.py
+++ b/solution.py
@@ -219,11 +219,11 @@
     low = (gram - high.astype(F32)).astype(BF16)
     image = image + jnp.dot(prev, high, preferred_element_type=F32)
     image = image + jnp.dot(prev, low, preferred_element_type=F32)
-    part_ref[...] = (1.0 + conf) * rhs - image
+    pack((1.0 + conf) * rhs - image, part_ref)
 
 
 def join_kernel(mine_ref, part_ref, msg_ref):
-    pack(mine_ref[...] + part_ref[...], msg_ref)
+    pack(mine_ref[...] + unpack(part_ref), msg_ref)
 
 
 def collect_kernel(pieces, rows, info_ref, gram_ref, *refs):
@@ -441,7 +441,7 @@
         flops = 2 * size * rank * (tiles * rank + 3 * obs * users)
         (part,) = call(
             functools.partial(twin_kernel, pieces, rows),
-            [vec],
+            [message],
             (*scalars, twin_info, twin_alpha, twin_prev, *far),
             2,
             flops,

time: 61.5 us -> 61.6 us (level)
  no operation moved by 1% of the time
where the time goes in v7:
time: 61.6 us; the launch traced here: 61.4 us
  starting transfers between devices  27.4 us (44%)
  waiting for transfers between devices  20.5 us (33%)
  Pallas kernels  10.9 us (18%)
  local copies, waits for them, and re-layouts  1.52 us (2%)
  other arithmetic  1.04 us (2%)
    ppermute x12, starting transfers between devices, sent(): lax.ppermute(own, ('row', 'col'), [(i, partner(i, bits)) for i in range(n...  17.7 us
    ppermute x12, waiting for transfers between devices, sent(): lax.ppermute(own, ('row', 'col'), [(i, partner(i, bits)) for i in range(n...  14.7 us
    pallas_call x11, Pallas kernels, call(): pl.pallas_call(body, out_shape=[pltpu.VMEM(o.shape, o.dtype) for o in out...  10.1 us
    ppermute x13, starting transfers between devices, permuted(): return lax.ppermute(array, axis, [(i, target(i)) for i in range(size)])  9.63 us
    ppermute x13, waiting for transfers between devices, permuted(): return lax.ppermute(array, axis, [(i, target(i)) for i in range(size)])  5.73 us
    unnamed x10, local copies, waits for them, and re-layouts  1.34 us
  transfers between devices with their start and end apart: 25, of which 17 were waited for; matrix products, arithmetic and copies ran while one was open for 2% of the time, Pallas kernels for 9%

profile of v7, /device:TPU:0, one launch (start us, length us, event | category | flops | bytes accessed | tf_op | source)
XLA Modules:
  0.0 61.4 jit_solution(2198237643075883229)
XLA Ops:
  0.5 2.5 %collective-permute-start = (bf16[4,256,256]{2,1,0:T(8,128)(2,1)}, bf16[4,256,256]{2,1,0:T(8,128)(2,1)S(1)}, u32[]{:S(2)}, u32[]{:S(2)}) collective-permute-start(bf16[4,256,256]{2,1,0:T(8,128)(2,1)} %refs_4_.4), channel_id=1, source_target_pairs={{0,8},{4,20},{8,0},{12,28},{16,24},{20,4},{24,16},{28,12},{1,9},{5... | collective-permute-start | bytes 1572872 | tf_op jit(solution)/shard_map/ppermute | solution.py:322
  5.5 1.3 %masks.1 = (f32[2,128,512]{2,1,0:T(8,128)S(1)}, f32[2,128,1024]{2,1,0:T(8,128)S(1)}, f32[2,128,256]{2,1,0:T(8,128)S(1)}, f32[2,128,256]{2,1,0:T(8,128)S(1)}, s32[7]{0:T(128)S(4)}) custom-call(s32[7]{0:T(128)S(1)} %pad_add_fusion.info_ref, bf16[2,128,256]{2,1,0:T(8,128)(2,1)S(1)} %fusion.words_ref, f32[128,1]{1,0:T(8,128)S(1)} %copy.8.conf_ref.refs_2_), custom_call_target="tpu_custom_call" | custom-call | flops 268435456 | bytes 1048576 | tf_op jit(solution)/shard_map/masks/pallas_call | solution.py:22
  6.8 1.6 %collective-permute-start.8 = (bf16[4,256,256]{2,1,0:T(8,128)(2,1)S(1)}, bf16[4,256,256]{2,1,0:T(8,128)(2,1)S(1)}, u32[]{:S(2)}, u32[]{:S(2)}) collective-permute-start(bf16[4,256,256]{2,1,0:T(8,128)(2,1)S(1)} %copy-done.1), channel_id=1, source_target_pairs={{0,16},{4,12},{8,24},{12,4},{16,0},{20,28},{24,8},{28,20},{1,17},{... | collective-permute-start | bytes 1572872 | tf_op jit(solution)/shard_map/ppermute | solution.py:322
  8.9 1.0 %collective-permute-done.2.in_ref = s32[7]{0:T(128)S(1)} collective-permute-done((s32[7]{0:T(128)S(1)}, s32[7]{0:T(128)S(1)}, u32[]{:S(2)}, u32[]{:S(2)}) %collective-permute-start.2) | collective-permute-done | bytes 60 | tf_op jit(solution)/shard_map/ppermute | solution.py:322
  11.6 3.1 %collective-permute-start.5 = (bf16[4,256,256]{2,1,0:T(8,128)(2,1)S(1)}, bf16[4,256,256]{2,1,0:T(8,128)(2,1)S(1)}, u32[]{:S(2)}, u32[]{:S(2)}) collective-permute-start(bf16[4,256,256]{2,1,0:T(8,128)(2,1)S(1)} %collective-permute-done.refs_4_), channel_id=1, source_target_pairs={{0,16},{4,12},{8,24},{12,4},{16,0},{20,28},{24,8},{28,20},{1,17},{... | collective-permute-start | bytes 1572872 | tf_op jit(solution)/shard_map/ppermute | solution.py:322
  14.7 1.4 %collective-permute-done.8.refs_7_ = bf16[4,256,256]{2,1,0:T(8,128)(2,1)S(1)} collective-permute-done((bf16[4,256,256]{2,1,0:T(8,128)(2,1)S(1)}, bf16[4,256,256]{2,1,0:T(8,128)(2,1)S(1)}, u32[]{:S(2)}, u32[]{:S(2)}) %collective-permute-start.8) | collective-permute-done | bytes 524320 | tf_op jit(solution)/shard_map/ppermute | solution.py:322
  18.7 1.9 %stage.4 = (bf16[2,1024,256]{2,1,0:T(8,128)(2,1)S(1)}, bf16[2,256,1024]{2,1,0:T(8,128)(2,1)S(1)}, f32[256,256]{1,0:T(8,128)S(1)}, f32[2,128,256]{2,1,0:T(8,128)S(1)}) custom-call(s32[7]{0:T(128)S(4)} %get-tuple-element.41.refs_0_.info_ref, f32[2,128,1024]{2,1,0:T(8,128)S(1)} %get-tuple-element.46.refs_1_.refs_8_, f32[128,1]{1,0:T(8,128)S(1)} %copy.8.conf_ref.refs_2_, ...), custom_call_target="tpu_custom_call" | custom-call | flops 939524096 | bytes 1048576 | tf_op jit(solution)/shard_map/stage/pallas_call | solution.py:22
  20.6 1.2 %collective-permute-done.5.refs_4_.refs_0_ = bf16[4,256,256]{2,1,0:T(8,128)(2,1)S(1)} collective-permute-done((bf16[4,256,256]{2,1,0:T(8,128)(2,1)S(1)}, bf16[4,256,256]{2,1,0:T(8,128)(2,1)S(1)}, u32[]{:S(2)}, u32[]{:S(2)}) %collective-permute-start.5) | collective-permute-done | bytes 524320 | tf_op jit(solution)/shard_map/ppermute | solution.py:322
  24.4 3.5 %collective-permute-start.14 = (s16[128,256]{1,0:T(8,128)(2,1)S(1)}, s16[128,256]{1,0:T(8,128)(2,1)S(1)}, u32[]{:S(2)}, u32[]{:S(2)}) collective-permute-start(s16[128,256]{1,0:T(8,128)(2,1)S(1)} %join.1.refs_0_), channel_id=1, source_target_pairs={{0,3},{1,2},{2,1},{3,0},{4,7},{5,6},{6,5},{7,4},{8,11},{9,10},{10,... | collective-permute-start | bytes 196616 | tf_op jit(solution)/shard_map/ppermute | solution.py:478
  29.1 1.7 %collective-permute-done.14.refs_3_ = s16[128,256]{1,0:T(8,128)(2,1)S(1)} collective-permute-done((s16[128,256]{1,0:T(8,128)(2,1)S(1)}, s16[128,256]{1,0:T(8,128)(2,1)S(1)}, u32[]{:S(2)}, u32[]{:S(2)}) %collective-permute-start.14) | collective-permute-done | bytes 65568 | tf_op jit(solution)/shard_map/ppermute | solution.py:478
  30.8 2.8 %collective-permute-done.13.refs_2_ = s16[128,256]{1,0:T(8,128)(2,1)S(1)} collective-permute-done((s16[128,256]{1,0:T(8,128)(2,1)S(1)}, s16[128,256]{1,0:T(8,128)(2,1)S(1)}, u32[]{:S(2)}, u32[]{:S(2)}) %collective-permute-start.13) | collective-permute-done | bytes 65568 | tf_op jit(solution)/shard_map/ppermute | solution.py:478
  33.6 1.2 %round0.1 = (f32[128,256]{1,0:T(8,128)S(1)}, s16[128,256]{1,0:T(8,128)(2,1)S(1)}) custom-call(s16[128,256]{1,0:T(8,128)(2,1)S(1)} %join.1.refs_0_, s16[128,256]{1,0:T(8,128)(2,1)S(1)} %collective-permute-done.12.refs_1_, s16[128,256]{1,0:T(8,128)(2,1)S(1)} %collective-permute-done.13.refs_2_, s16[128,256]{1,0:T(8,128)(2,1)S(1)} %collective-permute-done.14.refs_3_, ...), custom_call_target="tpu_custom_call" | custom-call | flops 536870912 | bytes 1048576 | tf_op jit(solution)/shard_map/round0/pallas_call | solution.py:22
  34.7 2.1 %collective-permute-start.18 = (s16[128,256]{1,0:T(8,128)(2,1)S(1)}, s16[128,256]{1,0:T(8,128)(2,1)S(1)}, u32[]{:S(2)}, u32[]{:S(2)}) collective-permute-start(s16[128,256]{1,0:T(8,128)(2,1)S(1)} %get-tuple-element.67.refs_0_), channel_id=1, source_target_pairs={{0,3},{1,2},{2,1},{3,0},{4,7},{5,6},{6,5},{7,4},{8,11},{9,10},{10,... | collective-permute-start | bytes 196616 | tf_op jit(solution)/shard_map/ppermute | solution.py:478
  37.7 1.5 %collective-permute-start.16 = (s16[128,256]{1,0:T(8,128)(2,1)S(1)}, s16[128,256]{1,0:T(8,128)(2,1)S(1)}, u32[]{:S(2)}, u32[]{:S(2)}) collective-permute-start(s16[128,256]{1,0:T(8,128)(2,1)S(1)} %get-tuple-element.67.refs_0_), channel_id=1, source_target_pairs={{0,2},{1,3},{2,0},{3,1},{4,5},{5,4},{6,7},{7,6},{8,10},{9,11},{10,... | collective-permute-start | bytes 196616 | tf_op jit(solution)/shard_map/ppermute | solution.py:478
  39.2 1.8 %collective-permute-done.18.refs_3_ = s16[128,256]{1,0:T(8,128)(2,1)S(1)} collective-permute-done((s16[128,256]{1,0:T(8,128)(2,1)S(1)}, s16[128,256]{1,0:T(8,128)(2,1)S(1)}, u32[]{:S(2)}, u32[]{:S(2)}) %collective-permute-start.18) | collective-permute-done | bytes 65568 | tf_op jit(solution)/shard_map/ppermute | solution.py:478
  41.0 2.0 %collective-permute-done.17.refs_2_ = s16[128,256]{1,0:T(8,128)(2,1)S(1)} collective-permute-done((s16[128,256]{1,0:T(8,128)(2,1)S(1)}, s16[128,256]{1,0:T(8,128)(2,1)S(1)}, u32[]{:S(2)}, u32[]{:S(2)}) %collective-permute-start.17) | collective-permute-done | bytes 65568 | tf_op jit(solution)/shard_map/ppermute | solution.py:478
  43.1 1.3 %round1.1 = (f32[128,256]{1,0:T(8,128)S(1)}, f32[128,256]{1,0:T(8,128)S(1)}, f32[128,256]{1,0:T(8,128)S(1)}, s16[128,256]{1,0:T(8,128)(2,1)S(1)}) custom-call(s16[128,256]{1,0:T(8,128)(2,1)S(1)} %get-tuple-element.67.refs_0_, s16[128,256]{1,0:T(8,128)(2,1)S(1)} %collective-permute-done.16.refs_1_, s16[128,256]{1,0:T(8,128)(2,1)S(1)} %collective-permute-done.17.refs_2_, ...), custom_call_target="tpu_custom_call" | custom-call | flops 536870912 | bytes 1048576 | tf_op jit(solution)/shard_map/round1/pallas_call | solution.py:22
  44.4 2.1 %collective-permute-start.21 = (s16[128,256]{1,0:T(8,128)(2,1)S(1)}, s16[128,256]{1,0:T(8,128)(2,1)S(1)}, u32[]{:S(2)}, u32[]{:S(2)}) collective-permute-start(s16[128,256]{1,0:T(8,128)(2,1)S(1)} %get-tuple-element.69.refs_0_), channel_id=1, source_target_pairs={{0,3},{1,2},{2,1},{3,0},{4,7},{5,6},{6,5},{7,4},{8,11},{9,10},{10,... | collective-permute-start | bytes 196616 | tf_op jit(solution)/shard_map/ppermute | solution.py:478
  46.8 2.0 %collective-permute-start.19 = (s16[128,256]{1,0:T(8,128)(2,1)S(1)}, s16[128,256]{1,0:T(8,128)(2,1)S(1)}, u32[]{:S(2)}, u32[]{:S(2)}) collective-permute-start(s16[128,256]{1,0:T(8,128)(2,1)S(1)} %get-tuple-element.69.refs_0_), channel_id=1, source_target_pairs={{0,2},{1,3},{2,0},{3,1},{4,5},{5,4},{6,7},{7,6},{8,10},{9,11},{10,... | collective-permute-start | bytes 196616 | tf_op jit(solution)/shard_map/ppermute | solution.py:478
  48.8 2.1 %collective-permute-done.21.refs_3_ = s16[128,256]{1,0:T(8,128)(2,1)S(1)} collective-permute-done((s16[128,256]{1,0:T(8,128)(2,1)S(1)}, s16[128,256]{1,0:T(8,128)(2,1)S(1)}, u32[]{:S(2)}, u32[]{:S(2)}) %collective-permute-start.21) | collective-permute-done | bytes 65568 | tf_op jit(solution)/shard_map/ppermute | solution.py:478
  50.9 1.4 %collective-permute-done.20.refs_2_ = s16[128,256]{1,0:T(8,128)(2,1)S(1)} collective-permute-done((s16[128,256]{1,0:T(8,128)(2,1)S(1)}, s16[128,256]{1,0:T(8,128)(2,1)S(1)}, u32[]{:S(2)}, u32[]{:S(2)}) %collective-permute-start.20) | collective-permute-done | bytes 65568 | tf_op jit(solution)/shard_map/ppermute | solution.py:478
  53.3 2.8 %collective-permute-start.24 = (f32[8,128]{1,0:T(8,128)S(1)}, f32[8,128]{1,0:T(8,128)S(1)}, u32[]{:S(2)}, u32[]{:S(2)}) collective-permute-start(f32[8,128]{1,0:T(8,128)S(1)} %get-tuple-element.73.refs_0_), channel_id=1, source_target_pairs={{0,3},{1,2},{2,1},{3,0},{4,7},{5,6},{6,5},{7,4},{8,11},{9,10},{10,... | collective-permute-start | bytes 12296 | tf_op jit(solution)/shard_map/ppermute | solution.py:478
  56.1 1.6 %collective-permute-start.22 = (f32[8,128]{1,0:T(8,128)S(1)}, f32[8,128]{1,0:T(8,128)S(1)}, u32[]{:S(2)}, u32[]{:S(2)}) collective-permute-start(f32[8,128]{1,0:T(8,128)S(1)} %get-tuple-element.73.refs_0_), channel_id=1, source_target_pairs={{0,2},{1,3},{2,0},{3,1},{4,5},{5,4},{6,7},{7,6},{8,10},{9,11},{10,... | collective-permute-start | bytes 12296 | tf_op jit(solution)/shard_map/ppermute | solution.py:478
  57.7 1.0 %collective-permute-done.24.refs_3_ = f32[8,128]{1,0:T(8,128)S(1)} collective-permute-done((f32[8,128]{1,0:T(8,128)S(1)}, f32[8,128]{1,0:T(8,128)S(1)}, u32[]{:S(2)}, u32[]{:S(2)}) %collective-permute-start.24) | collective-permute-done | bytes 4128 | tf_op jit(solution)/shard_map/ppermute | solution.py:478
  (53 shorter events, 16.4 us)
Async XLA Ops:
  0.0 10.6 %collective-permute-start.1 = (bf16[4,256,256]{2,1,0:T(8,128)(2,1)}, bf16[4,256,256]{2,1,0:T(8,128)(2,1)S(1)}, u32[]{:S(2)}, u32[]{:S(2)}) collective-permute-start(bf16[4,256,256]{2,1,0:T(8,128)(2,1)} %refs_4_.4), channel_id=1, source_target_pairs={{0,4},{4,0},{8,12},{12,8},{16,20},{20,16},{24,28},{28,24},{1,5},{5... | collective-permute-start | bytes 1572872 | tf_op jit(solution)/shard_map/ppermute | solution.py:322
  0.5 11.1 %collective-permute-start = (bf16[4,256,256]{2,1,0:T(8,128)(2,1)}, bf16[4,256,256]{2,1,0:T(8,128)(2,1)S(1)}, u32[]{:S(2)}, u32[]{:S(2)}) collective-permute-start(bf16[4,256,256]{2,1,0:T(8,128)(2,1)} %refs_4_.4), channel_id=1, source_target_pairs={{0,8},{4,20},{8,0},{12,28},{16,24},{20,4},{24,16},{28,12},{1,9},{5... | collective-permute-start | bytes 1572872 | tf_op jit(solution)/shard_map/ppermute | solution.py:322
  6.8 9.2 %collective-permute-start.8 = (bf16[4,256,256]{2,1,0:T(8,128)(2,1)S(1)}, bf16[4,256,256]{2,1,0:T(8,128)(2,1)S(1)}, u32[]{:S(2)}, u32[]{:S(2)}) collective-permute-start(bf16[4,256,256]{2,1,0:T(8,128)(2,1)S(1)} %copy-done.1), channel_id=1, source_target_pairs={{0,16},{4,12},{8,24},{12,4},{16,0},{20,28},{24,8},{28,20},{1,17},{... | collective-permute-start | bytes 1572872 | tf_op jit(solution)/shard_map/ppermute | solution.py:322
  8.4 3.1 %collective-permute-start.3 = (f32[2,128,256]{2,1,0:T(8,128)S(1)}, f32[2,128,256]{2,1,0:T(8,128)S(1)}, u32[]{:S(2)}, u32[]{:S(2)}) collective-permute-start(f32[2,128,256]{2,1,0:T(8,128)S(1)} %get-tuple-element.47.refs_10_), channel_id=1, source_target_pairs={{0,4},{4,0},{8,12},{12,8},{16,20},{20,16},{24,28},{28,24},{1,5},{5... | collective-permute-start | bytes 786440 | tf_op jit(solution)/shard_map/ppermute | solution.py:322
  8.4 1.5 %collective-permute-start.2 = (s32[7]{0:T(128)S(1)}, s32[7]{0:T(128)S(1)}, u32[]{:S(2)}, u32[]{:S(2)}) collective-permute-start(s32[7]{0:T(128)S(1)} %pad_add_fusion.info_ref), channel_id=1, source_target_pairs={{0,4},{4,0},{8,12},{12,8},{16,20},{20,16},{24,28},{28,24},{1,5},{5... | collective-permute-start | bytes 92 | tf_op jit(solution)/shard_map/ppermute | solution.py:322
  9.9 1.6 %collective-permute-start.4 = (bf16[128,256]{1,0:T(8,128)(2,1)S(1)}, bf16[128,256]{1,0:T(8,128)(2,1)S(1)}, u32[]{:S(2)}, u32[]{:S(2)}) collective-permute-start(bf16[128,256]{1,0:T(8,128)(2,1)S(1)} %copy-done), channel_id=1, source_target_pairs={{0,4},{4,0},{8,12},{12,8},{16,20},{20,16},{24,28},{28,24},{1,5},{5... | collective-permute-start | bytes 196616 | tf_op jit(solution)/shard_map/ppermute | solution.py:322
  11.6 10.2 %collective-permute-start.5 = (bf16[4,256,256]{2,1,0:T(8,128)(2,1)S(1)}, bf16[4,256,256]{2,1,0:T(8,128)(2,1)S(1)}, u32[]{:S(2)}, u32[]{:S(2)}) collective-permute-start(bf16[4,256,256]{2,1,0:T(8,128)(2,1)S(1)} %collective-permute-done.refs_4_), channel_id=1, source_target_pairs={{0,16},{4,12},{8,24},{12,4},{16,0},{20,28},{24,8},{28,20},{1,17},{... | collective-permute-start | bytes 1572872 | tf_op jit(solution)/shard_map/ppermute | solution.py:322
  16.1 1.5 %collective-permute-start.7 = (bf16[4,128,256]{2,1,0:T(8,128)(2,1)S(1)}, bf16[4,128,256]{2,1,0:T(8,128)(2,1)S(1)}, u32[]{:S(2)}, u32[]{:S(2)}) collective-permute-start(bf16[4,128,256]{2,1,0:T(8,128)(2,1)S(1)} %get-tuple-element.79), channel_id=1, source_target_pairs={{0,4},{4,0},{8,12},{12,8},{16,20},{20,16},{24,28},{28,24},{1,5},{5... | collective-permute-start | bytes 786440 | tf_op jit(solution)/shard_map/ppermute | solution.py:322
  16.1 1.9 %collective-permute-start.6 = (bf16[4,128,256]{2,1,0:T(8,128)(2,1)S(1)}, bf16[4,128,256]{2,1,0:T(8,128)(2,1)S(1)}, u32[]{:S(2)}, u32[]{:S(2)}) collective-permute-start(bf16[4,128,256]{2,1,0:T(8,128)(2,1)S(1)} %get-tuple-element.80), channel_id=1, source_target_pairs={{0,4},{4,0},{8,12},{12,8},{16,20},{20,16},{24,28},{28,24},{1,5},{5... | collective-permute-start | bytes 786440 | tf_op jit(solution)/shard_map/ppermute | solution.py:322
  16.6 1.7 %collective-permute-start.10 = (bf16[4,128,256]{2,1,0:T(8,128)(2,1)S(1)}, bf16[4,128,256]{2,1,0:T(8,128)(2,1)S(1)}, u32[]{:S(2)}, u32[]{:S(2)}) collective-permute-start(bf16[4,128,256]{2,1,0:T(8,128)(2,1)S(1)} %get-tuple-element.77), channel_id=1, source_target_pairs={{0,4},{4,0},{8,12},{12,8},{16,20},{20,16},{24,28},{28,24},{1,5},{5... | collective-permute-start | bytes 786440 | tf_op jit(solution)/shard_map/ppermute | solution.py:322
  16.7 2.0 %collective-permute-start.9 = (bf16[4,128,256]{2,1,0:T(8,128)(2,1)S(1)}, bf16[4,128,256]{2,1,0:T(8,128)(2,1)S(1)}, u32[]{:S(2)}, u32[]{:S(2)}) collective-permute-start(bf16[4,128,256]{2,1,0:T(8,128)(2,1)S(1)} %get-tuple-element.78), channel_id=1, source_target_pairs={{0,4},{4,0},{8,12},{12,8},{16,20},{20,16},{24,28},{28,24},{1,5},{5... | collective-permute-start | bytes 786440 | tf_op jit(solution)/shard_map/ppermute | solution.py:322
  24.1 4.6 %collective-permute-start.15 = (bf16[4,256,256]{2,1,0:T(8,128)(2,1)S(1)}, bf16[4,256,256]{2,1,0:T(8,128)(2,1)S(1)}, u32[]{:S(2)}, u32[]{:S(2)}) collective-permute-start(bf16[4,256,256]{2,1,0:T(8,128)(2,1)S(1)} %collective-permute-done.5.refs_4_.refs_0_), channel_id=1, source_target_pairs={{0,4},{4,0},{8,12},{12,8},{16,20},{20,16},{24,28},{28,24},{1,5},{5... | collective-permute-start | bytes 1572872 | tf_op jit(solution)/shard_map/ppermute | solution.py:322
  24.4 6.5 %collective-permute-start.14 = (s16[128,256]{1,0:T(8,128)(2,1)S(1)}, s16[128,256]{1,0:T(8,128)(2,1)S(1)}, u32[]{:S(2)}, u32[]{:S(2)}) collective-permute-start(s16[128,256]{1,0:T(8,128)(2,1)S(1)} %join.1.refs_0_), channel_id=1, source_target_pairs={{0,3},{1,2},{2,1},{3,0},{4,7},{5,6},{6,5},{7,4},{8,11},{9,10},{10,... | collective-permute-start | bytes 196616 | tf_op jit(solution)/shard_map/ppermute | solution.py:478
  27.9 5.7 %collective-permute-start.13 = (s16[128,256]{1,0:T(8,128)(2,1)S(1)}, s16[128,256]{1,0:T(8,128)(2,1)S(1)}, u32[]{:S(2)}, u32[]{:S(2)}) collective-permute-start(s16[128,256]{1,0:T(8,128)(2,1)S(1)} %join.1.refs_0_), channel_id=1, source_target_pairs={{0,1},{1,0},{2,3},{3,2},{4,6},{5,7},{6,4},{7,5},{8,9},{9,8},{10,11... | collective-permute-start | bytes 196616 | tf_op jit(solution)/shard_map/ppermute | solution.py:478
  27.9 5.7 %collective-permute-start.12 = (s16[128,256]{1,0:T(8,128)(2,1)S(1)}, s16[128,256]{1,0:T(8,128)(2,1)S(1)}, u32[]{:S(2)}, u32[]{:S(2)}) collective-permute-start(s16[128,256]{1,0:T(8,128)(2,1)S(1)} %join.1.refs_0_), channel_id=1, source_target_pairs={{0,2},{1,3},{2,0},{3,1},{4,5},{5,4},{6,7},{7,6},{8,10},{9,11},{10,... | collective-permute-start | bytes 196616 | tf_op jit(solution)/shard_map/ppermute | solution.py:478
  34.7 6.3 %collective-permute-start.18 = (s16[128,256]{1,0:T(8,128)(2,1)S(1)}, s16[128,256]{1,0:T(8,128)(2,1)S(1)}, u32[]{:S(2)}, u32[]{:S(2)}) collective-permute-start(s16[128,256]{1,0:T(8,128)(2,1)S(1)} %get-tuple-element.67.refs_0_), channel_id=1, source_target_pairs={{0,3},{1,2},{2,1},{3,0},{4,7},{5,6},{6,5},{7,4},{8,11},{9,10},{10,... | collective-permute-start | bytes 196616 | tf_op jit(solution)/shard_map/ppermute | solution.py:478
  36.9 6.2 %collective-permute-start.17 = (s16[128,256]{1,0:T(8,128)(2,1)S(1)}, s16[128,256]{1,0:T(8,128)(2,1)S(1)}, u32[]{:S(2)}, u32[]{:S(2)}) collective-permute-start(s16[128,256]{1,0:T(8,128)(2,1)S(1)} %get-tuple-element.67.refs_0_), channel_id=1, source_target_pairs={{0,1},{1,0},{2,3},{3,2},{4,6},{5,7},{6,4},{7,5},{8,9},{9,8},{10,11... | collective-permute-start | bytes 196616 | tf_op jit(solution)/shard_map/ppermute | solution.py:478
  37.7 5.3 %collective-permute-start.16 = (s16[128,256]{1,0:T(8,128)(2,1)S(1)}, s16[128,256]{1,0:T(8,128)(2,1)S(1)}, u32[]{:S(2)}, u32[]{:S(2)}) collective-permute-start(s16[128,256]{1,0:T(8,128)(2,1)S(1)} %get-tuple-element.67.refs_0_), channel_id=1, source_target_pairs={{0,2},{1,3},{2,0},{3,1},{4,5},{5,4},{6,7},{7,6},{8,10},{9,11},{10,... | collective-permute-start | bytes 196616 | tf_op jit(solution)/shard_map/ppermute | solution.py:478
  44.4 6.5 %collective-permute-start.21 = (s16[128,256]{1,0:T(8,128)(2,1)S(1)}, s16[128,256]{1,0:T(8,128)(2,1)S(1)}, u32[]{:S(2)}, u32[]{:S(2)}) collective-permute-start(s16[128,256]{1,0:T(8,128)(2,1)S(1)} %get-tuple-element.69.refs_0_), channel_id=1, source_target_pairs={{0,3},{1,2},{2,1},{3,0},{4,7},{5,6},{6,5},{7,4},{8,11},{9,10},{10,... | collective-permute-start | bytes 196616 | tf_op jit(solution)/shard_map/ppermute | solution.py:478
  46.5 5.8 %collective-permute-start.20 = (s16[128,256]{1,0:T(8,128)(2,1)S(1)}, s16[128,256]{1,0:T(8,128)(2,1)S(1)}, u32[]{:S(2)}, u32[]{:S(2)}) collective-permute-start(s16[128,256]{1,0:T(8,128)(2,1)S(1)} %get-tuple-element.69.refs_0_), channel_id=1, source_target_pairs={{0,1},{1,0},{2,3},{3,2},{4,6},{5,7},{6,4},{7,5},{8,9},{9,8},{10,11... | collective-permute-start | bytes 196616 | tf_op jit(solution)/shard_map/ppermute | solution.py:478
  46.8 5.5 %collective-permute-start.19 = (s16[128,256]{1,0:T(8,128)(2,1)S(1)}, s16[128,256]{1,0:T(8,128)(2,1)S(1)}, u32[]{:S(2)}, u32[]{:S(2)}) collective-permute-start(s16[128,256]{1,0:T(8,128)(2,1)S(1)} %get-tuple-element.69.refs_0_), channel_id=1, source_target_pairs={{0,2},{1,3},{2,0},{3,1},{4,5},{5,4},{6,7},{7,6},{8,10},{9,11},{10,... | collective-permute-start | bytes 196616 | tf_op jit(solution)/shard_map/ppermute | solution.py:478
  53.3 5.4 %collective-permute-start.24 = (f32[8,128]{1,0:T(8,128)S(1)}, f32[8,128]{1,0:T(8,128)S(1)}, u32[]{:S(2)}, u32[]{:S(2)}) collective-permute-start(f32[8,128]{1,0:T(8,128)S(1)} %get-tuple-element.73.refs_0_), channel_id=1, source_target_pairs={{0,3},{1,2},{2,1},{3,0},{4,7},{5,6},{6,5},{7,4},{8,11},{9,10},{10,... | collective-permute-start | bytes 12296 | tf_op jit(solution)/shard_map/ppermute | solution.py:478
  56.1 3.6 %collective-permute-start.23 = (f32[8,128]{1,0:T(8,128)S(1)}, f32[8,128]{1,0:T(8,128)S(1)}, u32[]{:S(2)}, u32[]{:S(2)}) collective-permute-start(f32[8,128]{1,0:T(8,128)S(1)} %get-tuple-element.73.refs_0_), channel_id=1, source_target_pairs={{0,1},{1,0},{2,3},{3,2},{4,6},{5,7},{6,4},{7,5},{8,9},{9,8},{10,11... | collective-permute-start | bytes 12296 | tf_op jit(solution)/shard_map/ppermute | solution.py:478
  56.1 4.5 %collective-permute-start.22 = (f32[8,128]{1,0:T(8,128)S(1)}, f32[8,128]{1,0:T(8,128)S(1)}, u32[]{:S(2)}, u32[]{:S(2)}) collective-permute-start(f32[8,128]{1,0:T(8,128)S(1)} %get-tuple-element.73.refs_0_), channel_id=1, source_target_pairs={{0,2},{1,3},{2,0},{3,1},{4,5},{5,4},{6,7},{7,6},{8,10},{9,11},{10,... | collective-permute-start | bytes 12296 | tf_op jit(solution)/shard_map/ppermute | solution.py:478
  (6 other events, 9.2 us)

commit v8 on v6

--- a/solution.py
+++ b/solution.py
@@ -477,7 +477,7 @@
     def sent(own, bits):
         return lax.ppermute(own, ("row", "col"), [(i, partner(i, bits)) for i in range(n_row * n_col)])
 
-    def to_all(own):
+    def to_all(own, order=order):
         return [own] + [sent(own, bits) for bits in order[1:]]
 
     state = []
@@ -496,7 +496,8 @@
             4 * obs * users * slots * rank,
             f"round{index}",
         )
-    msgs = to_all(msg)
+    order = list(range(n_col))
+    msgs = to_all(msg, order)
     (out,) = pl.pallas_call(
         functools.partial(final_kernel, order),
         out_shape=[vec],

time: 61.5 us -> 61.5 us (level)
  transfers between devices with their start and end apart: 25 -> 25, of which waited for: 17 -> 16; matrix products, arithmetic and copies ran while one was open for 2% -> 2% of each run, Pallas kernels for 9% -> 9%
where the time goes in v8:
time: 61.5 us; the launch traced here: 61.3 us
  starting transfers between devices  27.4 us (45%)
  waiting for transfers between devices  20.5 us (33%)
  Pallas kernels  10.7 us (17%)
  local copies, waits for them, and re-layouts  1.52 us (2%)
  other arithmetic  1.04 us (2%)
    ppermute x12, starting transfers between devices, sent(): lax.ppermute(own, ('row', 'col'), [(i, partner(i, bits)) for i in range(n...  17.7 us
    ppermute x12, waiting for transfers between devices, sent(): lax.ppermute(own, ('row', 'col'), [(i, partner(i, bits)) for i in range(n...  14.7 us
    pallas_call x11, Pallas kernels, call(): pl.pallas_call(body, out_shape=[pltpu.VMEM(o.shape, o.dtype) for o in out...  9.9 us
    ppermute x13, starting transfers between devices, permuted(): return lax.ppermute(array, axis, [(i, target(i)) for i in range(size)])  9.62 us
    ppermute x13, waiting for transfers between devices, permuted(): return lax.ppermute(array, axis, [(i, target(i)) for i in range(size)])  5.83 us
    unnamed x10, local copies, waits for them, and re-layouts  1.34 us
  transfers between devices with their start and end apart: 25, of which 16 were waited for; matrix products, arithmetic and copies ran while one was open for 2% of the time, Pallas kernels for 9%

profile of v8, /device:TPU:0, one launch (start us, length us, event | category | flops | bytes accessed | tf_op | source)
XLA Modules:
  0.0 61.3 jit_solution(12397129699099240866)
XLA Ops:
  0.5 2.5 %collective-permute-start = (bf16[4,256,256]{2,1,0:T(8,128)(2,1)}, bf16[4,256,256]{2,1,0:T(8,128)(2,1)S(1)}, u32[]{:S(2)}, u32[]{:S(2)}) collective-permute-start(bf16[4,256,256]{2,1,0:T(8,128)(2,1)} %refs_4_.4), channel_id=1, source_target_pairs={{0,8},{4,20},{8,0},{12,28},{16,24},{20,4},{24,16},{28,12},{1,9},{5... | collective-permute-start | bytes 1572872 | tf_op jit(solution)/shard_map/ppermute | solution.py:322
  5.5 1.3 %masks.1 = (f32[2,128,512]{2,1,0:T(8,128)S(1)}, f32[2,128,1024]{2,1,0:T(8,128)S(1)}, f32[2,128,256]{2,1,0:T(8,128)S(1)}, f32[2,128,256]{2,1,0:T(8,128)S(1)}, s32[7]{0:T(128)S(4)}) custom-call(s32[7]{0:T(128)S(1)} %pad_add_fusion.info_ref, bf16[2,128,256]{2,1,0:T(8,128)(2,1)S(1)} %fusion.words_ref, f32[128,1]{1,0:T(8,128)S(1)} %copy.8.conf_ref.refs_2_), custom_call_target="tpu_custom_call" | custom-call | flops 268435456 | bytes 1048576 | tf_op jit(solution)/shard_map/masks/pallas_call | solution.py:22
  6.8 1.6 %collective-permute-start.8 = (bf16[4,256,256]{2,1,0:T(8,128)(2,1)S(1)}, bf16[4,256,256]{2,1,0:T(8,128)(2,1)S(1)}, u32[]{:S(2)}, u32[]{:S(2)}) collective-permute-start(bf16[4,256,256]{2,1,0:T(8,128)(2,1)S(1)} %copy-done.1), channel_id=1, source_target_pairs={{0,16},{4,12},{8,24},{12,4},{16,0},{20,28},{24,8},{28,20},{1,17},{... | collective-permute-start | bytes 1572872 | tf_op jit(solution)/shard_map/ppermute | solution.py:322
  8.9 1.0 %collective-permute-done.2.in_ref = s32[7]{0:T(128)S(1)} collective-permute-done((s32[7]{0:T(128)S(1)}, s32[7]{0:T(128)S(1)}, u32[]{:S(2)}, u32[]{:S(2)}) %collective-permute-start.2) | collective-permute-done | bytes 60 | tf_op jit(solution)/shard_map/ppermute | solution.py:322
  11.6 3.1 %collective-permute-start.5 = (bf16[4,256,256]{2,1,0:T(8,128)(2,1)S(1)}, bf16[4,256,256]{2,1,0:T(8,128)(2,1)S(1)}, u32[]{:S(2)}, u32[]{:S(2)}) collective-permute-start(bf16[4,256,256]{2,1,0:T(8,128)(2,1)S(1)} %collective-permute-done.refs_4_), channel_id=1, source_target_pairs={{0,16},{4,12},{8,24},{12,4},{16,0},{20,28},{24,8},{28,20},{1,17},{... | collective-permute-start | bytes 1572872 | tf_op jit(solution)/shard_map/ppermute | solution.py:322
  14.7 1.4 %collective-permute-done.8.refs_7_ = bf16[4,256,256]{2,1,0:T(8,128)(2,1)S(1)} collective-permute-done((bf16[4,256,256]{2,1,0:T(8,128)(2,1)S(1)}, bf16[4,256,256]{2,1,0:T(8,128)(2,1)S(1)}, u32[]{:S(2)}, u32[]{:S(2)}) %collective-permute-start.8) | collective-permute-done | bytes 524320 | tf_op jit(solution)/shard_map/ppermute | solution.py:322
  18.7 1.9 %stage.4 = (bf16[2,1024,256]{2,1,0:T(8,128)(2,1)S(1)}, bf16[2,256,1024]{2,1,0:T(8,128)(2,1)S(1)}, f32[256,256]{1,0:T(8,128)S(1)}, f32[2,128,256]{2,1,0:T(8,128)S(1)}) custom-call(s32[7]{0:T(128)S(4)} %get-tuple-element.41.refs_0_.info_ref, f32[2,128,1024]{2,1,0:T(8,128)S(1)} %get-tuple-element.46.refs_1_.refs_8_, f32[128,1]{1,0:T(8,128)S(1)} %copy.8.conf_ref.refs_2_, ...), custom_call_target="tpu_custom_call" | custom-call | flops 939524096 | bytes 1048576 | tf_op jit(solution)/shard_map/stage/pallas_call | solution.py:22
  20.6 1.2 %collective-permute-done.5.refs_4_.refs_0_ = bf16[4,256,256]{2,1,0:T(8,128)(2,1)S(1)} collective-permute-done((bf16[4,256,256]{2,1,0:T(8,128)(2,1)S(1)}, bf16[4,256,256]{2,1,0:T(8,128)(2,1)S(1)}, u32[]{:S(2)}, u32[]{:S(2)}) %collective-permute-start.5) | collective-permute-done | bytes 524320 | tf_op jit(solution)/shard_map/ppermute | solution.py:322
  24.2 3.6 %collective-permute-start.14 = (s16[128,256]{1,0:T(8,128)(2,1)S(1)}, s16[128,256]{1,0:T(8,128)(2,1)S(1)}, u32[]{:S(2)}, u32[]{:S(2)}) collective-permute-start(s16[128,256]{1,0:T(8,128)(2,1)S(1)} %join.1.refs_0_), channel_id=1, source_target_pairs={{0,3},{1,2},{2,1},{3,0},{4,7},{5,6},{6,5},{7,4},{8,11},{9,10},{10,... | collective-permute-start | bytes 196616 | tf_op jit(solution)/shard_map/ppermute | solution.py:478
  29.0 1.7 %collective-permute-done.14.refs_3_ = s16[128,256]{1,0:T(8,128)(2,1)S(1)} collective-permute-done((s16[128,256]{1,0:T(8,128)(2,1)S(1)}, s16[128,256]{1,0:T(8,128)(2,1)S(1)}, u32[]{:S(2)}, u32[]{:S(2)}) %collective-permute-start.14) | collective-permute-done | bytes 65568 | tf_op jit(solution)/shard_map/ppermute | solution.py:478
  30.7 2.8 %collective-permute-done.13.refs_2_ = s16[128,256]{1,0:T(8,128)(2,1)S(1)} collective-permute-done((s16[128,256]{1,0:T(8,128)(2,1)S(1)}, s16[128,256]{1,0:T(8,128)(2,1)S(1)}, u32[]{:S(2)}, u32[]{:S(2)}) %collective-permute-start.13) | collective-permute-done | bytes 65568 | tf_op jit(solution)/shard_map/ppermute | solution.py:478
  33.5 1.2 %round0.1 = (f32[128,256]{1,0:T(8,128)S(1)}, s16[128,256]{1,0:T(8,128)(2,1)S(1)}) custom-call(s16[128,256]{1,0:T(8,128)(2,1)S(1)} %join.1.refs_0_, s16[128,256]{1,0:T(8,128)(2,1)S(1)} %collective-permute-done.12.refs_1_, s16[128,256]{1,0:T(8,128)(2,1)S(1)} %collective-permute-done.13.refs_2_, s16[128,256]{1,0:T(8,128)(2,1)S(1)} %collective-permute-done.14.refs_3_, ...), custom_call_target="tpu_custom_call" | custom-call | flops 536870912 | bytes 1048576 | tf_op jit(solution)/shard_map/round0/pallas_call | solution.py:22
  34.6 2.1 %collective-permute-start.18 = (s16[128,256]{1,0:T(8,128)(2,1)S(1)}, s16[128,256]{1,0:T(8,128)(2,1)S(1)}, u32[]{:S(2)}, u32[]{:S(2)}) collective-permute-start(s16[128,256]{1,0:T(8,128)(2,1)S(1)} %get-tuple-element.67.refs_0_), channel_id=1, source_target_pairs={{0,3},{1,2},{2,1},{3,0},{4,7},{5,6},{6,5},{7,4},{8,11},{9,10},{10,... | collective-permute-start | bytes 196616 | tf_op jit(solution)/shard_map/ppermute | solution.py:478
  37.6 1.5 %collective-permute-start.16 = (s16[128,256]{1,0:T(8,128)(2,1)S(1)}, s16[128,256]{1,0:T(8,128)(2,1)S(1)}, u32[]{:S(2)}, u32[]{:S(2)}) collective-permute-start(s16[128,256]{1,0:T(8,128)(2,1)S(1)} %get-tuple-element.67.refs_0_), channel_id=1, source_target_pairs={{0,2},{1,3},{2,0},{3,1},{4,5},{5,4},{6,7},{7,6},{8,10},{9,11},{10,... | collective-permute-start | bytes 196616 | tf_op jit(solution)/shard_map/ppermute | solution.py:478
  39.1 1.8 %collective-permute-done.18.refs_3_ = s16[128,256]{1,0:T(8,128)(2,1)S(1)} collective-permute-done((s16[128,256]{1,0:T(8,128)(2,1)S(1)}, s16[128,256]{1,0:T(8,128)(2,1)S(1)}, u32[]{:S(2)}, u32[]{:S(2)}) %collective-permute-start.18) | collective-permute-done | bytes 65568 | tf_op jit(solution)/shard_map/ppermute | solution.py:478
  40.9 2.0 %collective-permute-done.17.refs_2_ = s16[128,256]{1,0:T(8,128)(2,1)S(1)} collective-permute-done((s16[128,256]{1,0:T(8,128)(2,1)S(1)}, s16[128,256]{1,0:T(8,128)(2,1)S(1)}, u32[]{:S(2)}, u32[]{:S(2)}) %collective-permute-start.17) | collective-permute-done | bytes 65568 | tf_op jit(solution)/shard_map/ppermute | solution.py:478
  43.0 1.3 %round1.1 = (f32[128,256]{1,0:T(8,128)S(1)}, f32[128,256]{1,0:T(8,128)S(1)}, f32[128,256]{1,0:T(8,128)S(1)}, s16[128,256]{1,0:T(8,128)(2,1)S(1)}) custom-call(s16[128,256]{1,0:T(8,128)(2,1)S(1)} %get-tuple-element.67.refs_0_, s16[128,256]{1,0:T(8,128)(2,1)S(1)} %collective-permute-done.16.refs_1_, s16[128,256]{1,0:T(8,128)(2,1)S(1)} %collective-permute-done.17.refs_2_, ...), custom_call_target="tpu_custom_call" | custom-call | flops 536870912 | bytes 1048576 | tf_op jit(solution)/shard_map/round1/pallas_call | solution.py:22
  44.3 2.1 %collective-permute-start.21 = (s16[128,256]{1,0:T(8,128)(2,1)S(1)}, s16[128,256]{1,0:T(8,128)(2,1)S(1)}, u32[]{:S(2)}, u32[]{:S(2)}) collective-permute-start(s16[128,256]{1,0:T(8,128)(2,1)S(1)} %get-tuple-element.69.refs_0_), channel_id=1, source_target_pairs={{0,3},{1,2},{2,1},{3,0},{4,7},{5,6},{6,5},{7,4},{8,11},{9,10},{10,... | collective-permute-start | bytes 196616 | tf_op jit(solution)/shard_map/ppermute | solution.py:478
  46.7 2.0 %collective-permute-start.19 = (s16[128,256]{1,0:T(8,128)(2,1)S(1)}, s16[128,256]{1,0:T(8,128)(2,1)S(1)}, u32[]{:S(2)}, u32[]{:S(2)}) collective-permute-start(s16[128,256]{1,0:T(8,128)(2,1)S(1)} %get-tuple-element.69.refs_0_), channel_id=1, source_target_pairs={{0,2},{1,3},{2,0},{3,1},{4,5},{5,4},{6,7},{7,6},{8,10},{9,11},{10,... | collective-permute-start | bytes 196616 | tf_op jit(solution)/shard_map/ppermute | solution.py:478
  48.7 2.1 %collective-permute-done.21.refs_3_ = s16[128,256]{1,0:T(8,128)(2,1)S(1)} collective-permute-done((s16[128,256]{1,0:T(8,128)(2,1)S(1)}, s16[128,256]{1,0:T(8,128)(2,1)S(1)}, u32[]{:S(2)}, u32[]{:S(2)}) %collective-permute-start.21) | collective-permute-done | bytes 65568 | tf_op jit(solution)/shard_map/ppermute | solution.py:478
  50.8 1.4 %collective-permute-done.20.refs_2_ = s16[128,256]{1,0:T(8,128)(2,1)S(1)} collective-permute-done((s16[128,256]{1,0:T(8,128)(2,1)S(1)}, s16[128,256]{1,0:T(8,128)(2,1)S(1)}, u32[]{:S(2)}, u32[]{:S(2)}) %collective-permute-start.20) | collective-permute-done | bytes 65568 | tf_op jit(solution)/shard_map/ppermute | solution.py:478
  53.2 2.8 %collective-permute-start.24 = (f32[8,128]{1,0:T(8,128)S(1)}, f32[8,128]{1,0:T(8,128)S(1)}, u32[]{:S(2)}, u32[]{:S(2)}) collective-permute-start(f32[8,128]{1,0:T(8,128)S(1)} %get-tuple-element.73.refs_0_), channel_id=1, source_target_pairs={{0,3},{1,2},{2,1},{3,0},{4,7},{5,6},{6,5},{7,4},{8,11},{9,10},{10,... | collective-permute-start | bytes 12296 | tf_op jit(solution)/shard_map/ppermute | solution.py:478
  56.0 1.6 %collective-permute-start.22 = (f32[8,128]{1,0:T(8,128)S(1)}, f32[8,128]{1,0:T(8,128)S(1)}, u32[]{:S(2)}, u32[]{:S(2)}) collective-permute-start(f32[8,128]{1,0:T(8,128)S(1)} %get-tuple-element.73.refs_0_), channel_id=1, source_target_pairs={{0,1},{1,0},{2,3},{3,2},{4,6},{5,7},{6,4},{7,5},{8,9},{9,8},{10,11... | collective-permute-start | bytes 12296 | tf_op jit(solution)/shard_map/ppermute | solution.py:478
  58.6 1.9 %collective-permute-done.23.refs_2_ = f32[8,128]{1,0:T(8,128)S(1)} collective-permute-done((f32[8,128]{1,0:T(8,128)S(1)}, f32[8,128]{1,0:T(8,128)S(1)}, u32[]{:S(2)}, u32[]{:S(2)}) %collective-permute-start.23) | collective-permute-done | bytes 4128 | tf_op jit(solution)/shard_map/ppermute | solution.py:478
  (53 shorter events, 15.3 us)
Async XLA Ops:
  0.0 10.6 %collective-permute-start.1 = (bf16[4,256,256]{2,1,0:T(8,128)(2,1)}, bf16[4,256,256]{2,1,0:T(8,128)(2,1)S(1)}, u32[]{:S(2)}, u32[]{:S(2)}) collective-permute-start(bf16[4,256,256]{2,1,0:T(8,128)(2,1)} %refs_4_.4), channel_id=1, source_target_pairs={{0,4},{4,0},{8,12},{12,8},{16,20},{20,16},{24,28},{28,24},{1,5},{5... | collective-permute-start | bytes 1572872 | tf_op jit(solution)/shard_map/ppermute | solution.py:322
  0.5 11.1 %collective-permute-start = (bf16[4,256,256]{2,1,0:T(8,128)(2,1)}, bf16[4,256,256]{2,1,0:T(8,128)(2,1)S(1)}, u32[]{:S(2)}, u32[]{:S(2)}) collective-permute-start(bf16[4,256,256]{2,1,0:T(8,128)(2,1)} %refs_4_.4), channel_id=1, source_target_pairs={{0,8},{4,20},{8,0},{12,28},{16,24},{20,4},{24,16},{28,12},{1,9},{5... | collective-permute-start | bytes 1572872 | tf_op jit(solution)/shard_map/ppermute | solution.py:322
  6.8 9.2 %collective-permute-start.8 = (bf16[4,256,256]{2,1,0:T(8,128)(2,1)S(1)}, bf16[4,256,256]{2,1,0:T(8,128)(2,1)S(1)}, u32[]{:S(2)}, u32[]{:S(2)}) collective-permute-start(bf16[4,256,256]{2,1,0:T(8,128)(2,1)S(1)} %copy-done.1), channel_id=1, source_target_pairs={{0,16},{4,12},{8,24},{12,4},{16,0},{20,28},{24,8},{28,20},{1,17},{... | collective-permute-start | bytes 1572872 | tf_op jit(solution)/shard_map/ppermute | solution.py:322
  8.4 3.1 %collective-permute-start.3 = (f32[2,128,256]{2,1,0:T(8,128)S(1)}, f32[2,128,256]{2,1,0:T(8,128)S(1)}, u32[]{:S(2)}, u32[]{:S(2)}) collective-permute-start(f32[2,128,256]{2,1,0:T(8,128)S(1)} %get-tuple-element.47.refs_10_), channel_id=1, source_target_pairs={{0,4},{4,0},{8,12},{12,8},{16,20},{20,16},{24,28},{28,24},{1,5},{5... | collective-permute-start | bytes 786440 | tf_op jit(solution)/shard_map/ppermute | solution.py:322
  8.4 1.5 %collective-permute-start.2 = (s32[7]{0:T(128)S(1)}, s32[7]{0:T(128)S(1)}, u32[]{:S(2)}, u32[]{:S(2)}) collective-permute-start(s32[7]{0:T(128)S(1)} %pad_add_fusion.info_ref), channel_id=1, source_target_pairs={{0,4},{4,0},{8,12},{12,8},{16,20},{20,16},{24,28},{28,24},{1,5},{5... | collective-permute-start | bytes 92 | tf_op jit(solution)/shard_map/ppermute | solution.py:322
  9.9 1.6 %collective-permute-start.4 = (bf16[128,256]{1,0:T(8,128)(2,1)S(1)}, bf16[128,256]{1,0:T(8,128)(2,1)S(1)}, u32[]{:S(2)}, u32[]{:S(2)}) collective-permute-start(bf16[128,256]{1,0:T(8,128)(2,1)S(1)} %copy-done), channel_id=1, source_target_pairs={{0,4},{4,0},{8,12},{12,8},{16,20},{20,16},{24,28},{28,24},{1,5},{5... | collective-permute-start | bytes 196616 | tf_op jit(solution)/shard_map/ppermute | solution.py:322
  11.6 10.2 %collective-permute-start.5 = (bf16[4,256,256]{2,1,0:T(8,128)(2,1)S(1)}, bf16[4,256,256]{2,1,0:T(8,128)(2,1)S(1)}, u32[]{:S(2)}, u32[]{:S(2)}) collective-permute-start(bf16[4,256,256]{2,1,0:T(8,128)(2,1)S(1)} %collective-permute-done.refs_4_), channel_id=1, source_target_pairs={{0,16},{4,12},{8,24},{12,4},{16,0},{20,28},{24,8},{28,20},{1,17},{... | collective-permute-start | bytes 1572872 | tf_op jit(solution)/shard_map/ppermute | solution.py:322
  16.1 1.5 %collective-permute-start.7 = (bf16[4,128,256]{2,1,0:T(8,128)(2,1)S(1)}, bf16[4,128,256]{2,1,0:T(8,128)(2,1)S(1)}, u32[]{:S(2)}, u32[]{:S(2)}) collective-permute-start(bf16[4,128,256]{2,1,0:T(8,128)(2,1)S(1)} %get-tuple-element.79), channel_id=1, source_target_pairs={{0,4},{4,0},{8,12},{12,8},{16,20},{20,16},{24,28},{28,24},{1,5},{5... | collective-permute-start | bytes 786440 | tf_op jit(solution)/shard_map/ppermute | solution.py:322
  16.1 1.9 %collective-permute-start.6 = (bf16[4,128,256]{2,1,0:T(8,128)(2,1)S(1)}, bf16[4,128,256]{2,1,0:T(8,128)(2,1)S(1)}, u32[]{:S(2)}, u32[]{:S(2)}) collective-permute-start(bf16[4,128,256]{2,1,0:T(8,128)(2,1)S(1)} %get-tuple-element.80), channel_id=1, source_target_pairs={{0,4},{4,0},{8,12},{12,8},{16,20},{20,16},{24,28},{28,24},{1,5},{5... | collective-permute-start | bytes 786440 | tf_op jit(solution)/shard_map/ppermute | solution.py:322
  16.6 1.7 %collective-permute-start.10 = (bf16[4,128,256]{2,1,0:T(8,128)(2,1)S(1)}, bf16[4,128,256]{2,1,0:T(8,128)(2,1)S(1)}, u32[]{:S(2)}, u32[]{:S(2)}) collective-permute-start(bf16[4,128,256]{2,1,0:T(8,128)(2,1)S(1)} %get-tuple-element.77), channel_id=1, source_target_pairs={{0,4},{4,0},{8,12},{12,8},{16,20},{20,16},{24,28},{28,24},{1,5},{5... | collective-permute-start | bytes 786440 | tf_op jit(solution)/shard_map/ppermute | solution.py:322
  16.7 2.0 %collective-permute-start.9 = (bf16[4,128,256]{2,1,0:T(8,128)(2,1)S(1)}, bf16[4,128,256]{2,1,0:T(8,128)(2,1)S(1)}, u32[]{:S(2)}, u32[]{:S(2)}) collective-permute-start(bf16[4,128,256]{2,1,0:T(8,128)(2,1)S(1)} %get-tuple-element.78), channel_id=1, source_target_pairs={{0,4},{4,0},{8,12},{12,8},{16,20},{20,16},{24,28},{28,24},{1,5},{5... | collective-permute-start | bytes 786440 | tf_op jit(solution)/shard_map/ppermute | solution.py:322
  24.0 4.6 %collective-permute-start.15 = (bf16[4,256,256]{2,1,0:T(8,128)(2,1)S(1)}, bf16[4,256,256]{2,1,0:T(8,128)(2,1)S(1)}, u32[]{:S(2)}, u32[]{:S(2)}) collective-permute-start(bf16[4,256,256]{2,1,0:T(8,128)(2,1)S(1)} %collective-permute-done.5.refs_4_.refs_0_), channel_id=1, source_target_pairs={{0,4},{4,0},{8,12},{12,8},{16,20},{20,16},{24,28},{28,24},{1,5},{5... | collective-permute-start | bytes 1572872 | tf_op jit(solution)/shard_map/ppermute | solution.py:322
  24.2 6.5 %collective-permute-start.14 = (s16[128,256]{1,0:T(8,128)(2,1)S(1)}, s16[128,256]{1,0:T(8,128)(2,1)S(1)}, u32[]{:S(2)}, u32[]{:S(2)}) collective-permute-start(s16[128,256]{1,0:T(8,128)(2,1)S(1)} %join.1.refs_0_), channel_id=1, source_target_pairs={{0,3},{1,2},{2,1},{3,0},{4,7},{5,6},{6,5},{7,4},{8,11},{9,10},{10,... | collective-permute-start | bytes 196616 | tf_op jit(solution)/shard_map/ppermute | solution.py:478
  27.8 5.7 %collective-permute-start.13 = (s16[128,256]{1,0:T(8,128)(2,1)S(1)}, s16[128,256]{1,0:T(8,128)(2,1)S(1)}, u32[]{:S(2)}, u32[]{:S(2)}) collective-permute-start(s16[128,256]{1,0:T(8,128)(2,1)S(1)} %join.1.refs_0_), channel_id=1, source_target_pairs={{0,1},{1,0},{2,3},{3,2},{4,6},{5,7},{6,4},{7,5},{8,9},{9,8},{10,11... | collective-permute-start | bytes 196616 | tf_op jit(solution)/shard_map/ppermute | solution.py:478
  27.8 5.7 %collective-permute-start.12 = (s16[128,256]{1,0:T(8,128)(2,1)S(1)}, s16[128,256]{1,0:T(8,128)(2,1)S(1)}, u32[]{:S(2)}, u32[]{:S(2)}) collective-permute-start(s16[128,256]{1,0:T(8,128)(2,1)S(1)} %join.1.refs_0_), channel_id=1, source_target_pairs={{0,2},{1,3},{2,0},{3,1},{4,5},{5,4},{6,7},{7,6},{8,10},{9,11},{10,... | collective-permute-start | bytes 196616 | tf_op jit(solution)/shard_map/ppermute | solution.py:478
  34.6 6.3 %collective-permute-start.18 = (s16[128,256]{1,0:T(8,128)(2,1)S(1)}, s16[128,256]{1,0:T(8,128)(2,1)S(1)}, u32[]{:S(2)}, u32[]{:S(2)}) collective-permute-start(s16[128,256]{1,0:T(8,128)(2,1)S(1)} %get-tuple-element.67.refs_0_), channel_id=1, source_target_pairs={{0,3},{1,2},{2,1},{3,0},{4,7},{5,6},{6,5},{7,4},{8,11},{9,10},{10,... | collective-permute-start | bytes 196616 | tf_op jit(solution)/shard_map/ppermute | solution.py:478
  36.8 6.2 %collective-permute-start.17 = (s16[128,256]{1,0:T(8,128)(2,1)S(1)}, s16[128,256]{1,0:T(8,128)(2,1)S(1)}, u32[]{:S(2)}, u32[]{:S(2)}) collective-permute-start(s16[128,256]{1,0:T(8,128)(2,1)S(1)} %get-tuple-element.67.refs_0_), channel_id=1, source_target_pairs={{0,1},{1,0},{2,3},{3,2},{4,6},{5,7},{6,4},{7,5},{8,9},{9,8},{10,11... | collective-permute-start | bytes 196616 | tf_op jit(solution)/shard_map/ppermute | solution.py:478
  37.6 5.3 %collective-permute-start.16 = (s16[128,256]{1,0:T(8,128)(2,1)S(1)}, s16[128,256]{1,0:T(8,128)(2,1)S(1)}, u32[]{:S(2)}, u32[]{:S(2)}) collective-permute-start(s16[128,256]{1,0:T(8,128)(2,1)S(1)} %get-tuple-element.67.refs_0_), channel_id=1, source_target_pairs={{0,2},{1,3},{2,0},{3,1},{4,5},{5,4},{6,7},{7,6},{8,10},{9,11},{10,... | collective-permute-start | bytes 196616 | tf_op jit(solution)/shard_map/ppermute | solution.py:478
  44.3 6.5 %collective-permute-start.21 = (s16[128,256]{1,0:T(8,128)(2,1)S(1)}, s16[128,256]{1,0:T(8,128)(2,1)S(1)}, u32[]{:S(2)}, u32[]{:S(2)}) collective-permute-start(s16[128,256]{1,0:T(8,128)(2,1)S(1)} %get-tuple-element.69.refs_0_), channel_id=1, source_target_pairs={{0,3},{1,2},{2,1},{3,0},{4,7},{5,6},{6,5},{7,4},{8,11},{9,10},{10,... | collective-permute-start | bytes 196616 | tf_op jit(solution)/shard_map/ppermute | solution.py:478
  46.4 5.8 %collective-permute-start.20 = (s16[128,256]{1,0:T(8,128)(2,1)S(1)}, s16[128,256]{1,0:T(8,128)(2,1)S(1)}, u32[]{:S(2)}, u32[]{:S(2)}) collective-permute-start(s16[128,256]{1,0:T(8,128)(2,1)S(1)} %get-tuple-element.69.refs_0_), channel_id=1, source_target_pairs={{0,1},{1,0},{2,3},{3,2},{4,6},{5,7},{6,4},{7,5},{8,9},{9,8},{10,11... | collective-permute-start | bytes 196616 | tf_op jit(solution)/shard_map/ppermute | solution.py:478
  46.7 5.5 %collective-permute-start.19 = (s16[128,256]{1,0:T(8,128)(2,1)S(1)}, s16[128,256]{1,0:T(8,128)(2,1)S(1)}, u32[]{:S(2)}, u32[]{:S(2)}) collective-permute-start(s16[128,256]{1,0:T(8,128)(2,1)S(1)} %get-tuple-element.69.refs_0_), channel_id=1, source_target_pairs={{0,2},{1,3},{2,0},{3,1},{4,5},{5,4},{6,7},{7,6},{8,10},{9,11},{10,... | collective-permute-start | bytes 196616 | tf_op jit(solution)/shard_map/ppermute | solution.py:478
  53.2 5.4 %collective-permute-start.24 = (f32[8,128]{1,0:T(8,128)S(1)}, f32[8,128]{1,0:T(8,128)S(1)}, u32[]{:S(2)}, u32[]{:S(2)}) collective-permute-start(f32[8,128]{1,0:T(8,128)S(1)} %get-tuple-element.73.refs_0_), channel_id=1, source_target_pairs={{0,3},{1,2},{2,1},{3,0},{4,7},{5,6},{6,5},{7,4},{8,11},{9,10},{10,... | collective-permute-start | bytes 12296 | tf_op jit(solution)/shard_map/ppermute | solution.py:478
  56.0 4.5 %collective-permute-start.23 = (f32[8,128]{1,0:T(8,128)S(1)}, f32[8,128]{1,0:T(8,128)S(1)}, u32[]{:S(2)}, u32[]{:S(2)}) collective-permute-start(f32[8,128]{1,0:T(8,128)S(1)} %get-tuple-element.73.refs_0_), channel_id=1, source_target_pairs={{0,2},{1,3},{2,0},{3,1},{4,5},{5,4},{6,7},{7,6},{8,10},{9,11},{10,... | collective-permute-start | bytes 12296 | tf_op jit(solution)/shard_map/ppermute | solution.py:478
  56.0 4.5 %collective-permute-start.22 = (f32[8,128]{1,0:T(8,128)S(1)}, f32[8,128]{1,0:T(8,128)S(1)}, u32[]{:S(2)}, u32[]{:S(2)}) collective-permute-start(f32[8,128]{1,0:T(8,128)S(1)} %get-tuple-element.73.refs_0_), channel_id=1, source_target_pairs={{0,1},{1,0},{2,3},{3,2},{4,6},{5,7},{6,4},{7,5},{8,9},{9,8},{10,11... | collective-permute-start | bytes 12296 | tf_op jit(solution)/shard_map/ppermute | solution.py:478
  (6 other events, 9.3 us)
